TPU v7x, 256 devices: a whole 4x4x8 slice. The times are simulated.
256 devices in a mesh: fsdp: 8 (over x, core), ep: 32 (over z, y).
Axes of the slice: x: 4, y: 4, z: 8, core: 2. Of those that a mesh axis runs over, the one named last changes fastest.
Arguments:
- out_grad: bfloat16 [4096, 7168], P('ep', 'fsdp'), may hold values from -1.5 to 1.5
- router_input: bfloat16 [4096, 7168], P('ep', 'fsdp'), may hold values from -6 to 6
- router_weight: float32 [7168, 32], P('fsdp'), may hold values from -0.0625 to 0.0625
- routes: int32 [4096, 8], P('ep'), may hold values from 0 to 31, all different within a row; in each aligned block of 128 rows (0 to 127, 128 to 255, ...) at most 36 rows name the same one
- balance_grad: float32 [4096, 32], P('ep'), may hold values from -6 to 6
- saved_hidden: bfloat16 [32, 32, 36, 2048], P('ep', None, None, 'fsdp'), may hold values from -6 to 6
- expert_down: bfloat16 [32, 2048, 7168], P('ep', None, 'fsdp'), may hold values from -0.125 to 0.125
- attention_grads: bfloat16 [32, 4, 288, 7168], P('ep', None, None, 'fsdp'), may hold values from -6 to 6
Outputs:
- grad_hidden: bfloat16 [32, 32, 36, 2048], P('ep', None, None, 'fsdp')
- grad_down: bfloat16 [32, 2048, 7168], P('ep', None, 'fsdp')
- router_grad: float32 [7168, 32], P('fsdp')
- token_grad: bfloat16 [4096, 7168], P('ep', 'fsdp')
- muon_update: bfloat16 [4, 288, 7168], P(None, None, 'fsdp')
Inputs may be any that keep to these rules, and one draw needn't show every extreme that they name: `routes`: each expert is named by at most 36 of the rows of one device's block of 128 tokens, and by exactly 36 in some block; a row names 8 different experts.
All inputs are finite; a program needn't handle non-finite values.
Results may differ from a plain program's by a relative error of at most 0.029.
Values may be sent and summed in bfloat16 or wider, within the bound.
No kernel may reach another device: no remote copies, remote signals or barrier semaphores. Data moves between devices by JAX's collectives and lax.ppermute only.
A program may use at most 128 MiB of HBM per device.

v0:
```python
import jax
import jax.numpy as jnp
from jax import lax
from jax.experimental import pallas as pl
from jax.experimental.pallas import tpu as pltpu
from jax.sharding import Mesh, PartitionSpec as P

D = 7168
LATENT = 288
ROUTE_SCALE = 2.827
NORM_EPS = 1e-07
COEF_A = 3.4445
COEF_B = -4.775
COEF_C = 2.0315
CAP = 36
SLOTS = 40
EXPERTS = 32
TOK = 128

FS = ("x", "c")
EP = ("z", "y")
f32 = jnp.float32
bf16 = jnp.bfloat16
VMEM_LIMIT = 48 * 1024 * 1024


def pack_kernel(routes_ref, tokens_ref, input_ref, weight_ref, out_ref, pos_ref, logit_ref):
    expert_ids = lax.broadcasted_iota(jnp.int32, (EXPERTS, TOK), 0)
    chosen = jnp.zeros((EXPERTS, TOK), f32)
    for k in range(routes_ref.shape[0]):
        chosen = chosen + jnp.where(routes_ref[k : k + 1, :] == expert_ids, 1.0, 0.0)
    before = lax.broadcasted_iota(jnp.int32, (TOK, TOK), 0)
    after = lax.broadcasted_iota(jnp.int32, (TOK, TOK), 1)
    upper = jnp.where(before <= after, 1.0, 0.0).astype(bf16)
    counted = jnp.dot(chosen.astype(bf16), upper, preferred_element_type=f32)
    position = jnp.where(chosen > 0.0, counted - 1.0, -1.0)
    pos_ref[...] = position
    slot_ids = lax.broadcasted_iota(jnp.int32, (SLOTS, TOK), 0).astype(f32)
    tokens = tokens_ref[...]
    group = 8
    for start in range(0, EXPERTS, group):
        picks = [
            jnp.where(slot_ids == position[e : e + 1, :], 1.0, 0.0)
            for e in range(start, start + group)
        ]
        pick = jnp.concatenate(picks, axis=0).astype(bf16)
        rows = jnp.dot(pick, tokens, preferred_element_type=f32)
        for i in range(group):
            out_ref[start + i] = rows[i * SLOTS : (i + 1) * SLOTS].astype(bf16)
    rest = weight_ref[...]
    logits = jnp.zeros((EXPERTS, TOK), f32)
    for _ in range(3):
        term = rest.astype(bf16)
        rest = rest - term.astype(f32)
        logits = logits + lax.dot_general(
            term, input_ref[...], (((1,), (1,)), ((), ())), preferred_element_type=f32
        )
    logit_ref[...] = logits


def pack(routes_t, tokens, router_input, weight_t):
    width = tokens.shape[1]
    return pl.pallas_call(
        pack_kernel,
        out_shape=(
            jax.ShapeDtypeStruct((EXPERTS, SLOTS, width), bf16),
            jax.ShapeDtypeStruct((EXPERTS, TOK), f32),
            jax.ShapeDtypeStruct((EXPERTS, TOK), f32),
        ),
        compiler_params=pltpu.CompilerParams(vmem_limit_bytes=VMEM_LIMIT),
        cost_estimate=pl.CostEstimate(flops=300_000_000, bytes_accessed=2_800_000, transcendentals=0),
    )(routes_t, tokens, router_input, weight_t)


def upstream_kernel(first_ref, rows_ref, down_ref, *refs):
    refs[-1][0] = lax.dot_general(
        rows_ref[...], down_ref[...], (((1,), (1,)), ((), ())), preferred_element_type=f32
    ).astype(bf16)


def upstream_partial(rows, down, place, core, after):
    count, width = rows.shape
    share = down.shape[0] // 8
    grid_spec = pltpu.PrefetchScalarGridSpec(
        num_scalar_prefetch=1,
        grid=(4,),
        in_specs=[
            pl.BlockSpec((count, width), lambda g, p: (0, 0)),
            pl.BlockSpec((share, width), lambda g, p: (2 * lax.rem(p[0] + g, 4) + p[1], 0)),
            pl.BlockSpec(memory_space=pl.ANY),
        ],
        out_specs=pl.BlockSpec((1, count, share), lambda g, p: (g, 0, 0)),
    )
    return pl.pallas_call(
        upstream_kernel,
        grid_spec=grid_spec,
        out_shape=jax.ShapeDtypeStruct((4, count, share), bf16),
        compiler_params=pltpu.CompilerParams(vmem_limit_bytes=VMEM_LIMIT),
        cost_estimate=pl.CostEstimate(
            flops=count * width * down.shape[0], bytes_accessed=6_300_000, transcendentals=0
        ),
    )(jnp.stack([place, core]), rows, down, after)


def back_kernel(hidden_ref, down_ref, out_ref):
    parts = hidden_ref.shape[0]
    whole = jnp.concatenate([hidden_ref[g] for g in range(parts)], axis=1)
    out_ref[...] = jnp.dot(whole, down_ref[...], preferred_element_type=f32)


def hidden_times_down(hidden, down):
    parts, count, share = hidden.shape
    width = down.shape[1]
    steps = 4
    block = count // steps
    return pl.pallas_call(
        back_kernel,
        grid=(steps,),
        in_specs=[
            pl.BlockSpec((parts, block, share), lambda g: (0, g, 0)),
            pl.BlockSpec((parts * share, width), lambda g: (0, 0)),
        ],
        out_specs=pl.BlockSpec((block, width), lambda g: (g, 0)),
        out_shape=jax.ShapeDtypeStruct((count, width), f32),
        compiler_params=pltpu.CompilerParams(vmem_limit_bytes=VMEM_LIMIT),
        cost_estimate=pl.CostEstimate(
            flops=2 * count * width * down.shape[0], bytes_accessed=12_500_000, transcendentals=0
        ),
    )(hidden, down)


def grad_down_kernel(hidden_ref, rows_ref, gate_ref, out_ref, scaled_ref):
    @pl.when(pl.program_id(0) == 0)
    def _():
        scaled_ref[...] = (gate_ref[...] * rows_ref[...].astype(f32)).astype(bf16)

    out_ref[0] = lax.dot_general(
        hidden_ref[0], scaled_ref[...], (((0,), (0,)), ((), ())), preferred_element_type=f32
    ).astype(bf16)


def grad_down_of(hidden, rows, gate):
    parts, count, share = hidden.shape
    width = rows.shape[1]
    return pl.pallas_call(
        grad_down_kernel,
        grid=(parts,),
        in_specs=[
            pl.BlockSpec((1, count, share), lambda g: (g, 0, 0)),
            pl.BlockSpec((count, width), lambda g: (0, 0)),
            pl.BlockSpec((count, 1), lambda g: (0, 0)),
        ],
        out_specs=pl.BlockSpec((1, share, width), lambda g: (0, g, 0)),
        out_shape=jax.ShapeDtypeStruct((1, parts * share, width), bf16),
        scratch_shapes=[pltpu.VMEM((count, width), bf16)],
        compiler_params=pltpu.CompilerParams(vmem_limit_bytes=VMEM_LIMIT),
        cost_estimate=pl.CostEstimate(
            flops=2 * count * width * parts * share, bytes_accessed=12_500_000, transcendentals=0
        ),
    )(hidden, rows, gate)


def exchange(value, axes):
    return lax.all_to_all(value, axes, split_axis=0, concat_axis=0, tiled=True)


def spread(value, axes, copies):
    return exchange(jnp.broadcast_to(value[None], (copies,) + value.shape), axes)


def swap(pieces, axes, size):
    got = [pieces[0]]
    for k in range(1, size):
        got.append(lax.ppermute(pieces[k], axes, [(i, (i + k) % size) for i in range(size)]))
    return got


def total_of(pieces):
    total = pieces[0].astype(f32)
    for piece in pieces[1:]:
        total = total + piece.astype(f32)
    return total


BLOCK = 40
PADDED = 8 * BLOCK
SHARE = LATENT // 8


def cut_kernel(z_ref, *refs):
    total, outs = refs[0][...], refs[2:]
    row = lax.broadcasted_iota(jnp.int32, (PADDED, LATENT), 0)
    column = lax.broadcasted_iota(jnp.int32, (PADDED, LATENT), 1)
    shift = row // BLOCK
    within = row - shift * BLOCK
    block = shift + z_ref[0]
    block = jnp.where(block >= 8, block - 8, block)
    source = jnp.where(within < SHARE, block * SHARE + within, -1)
    pick = jnp.where(source == column, 1.0, 0.0).astype(bf16)
    rows = jnp.dot(pick, total, preferred_element_type=f32)
    for k in range(8):
        outs[k][...] = rows[k * BLOCK : (k + 1) * BLOCK].astype(bf16)


def gram_kernel(z_ref, *refs):
    parts, whole_ref, gram_ref = refs[:8], refs[9], refs[10]
    rows = jnp.concatenate([part[...].astype(f32) for part in parts], axis=0).astype(bf16)
    row = lax.broadcasted_iota(jnp.int32, (LATENT, PADDED), 0)
    column = lax.broadcasted_iota(jnp.int32, (LATENT, PADDED), 1)
    shift = column // BLOCK
    within = column - shift * BLOCK
    block = z_ref[0] - shift
    block = jnp.where(block < 0, block + 8, block)
    target = jnp.where(within < SHARE, block * SHARE + within, -1)
    pick = jnp.where(target == row, 1.0, 0.0).astype(bf16)
    whole = jnp.dot(pick, rows, preferred_element_type=f32).astype(bf16)
    whole_ref[...] = whole
    gram_ref[...] = lax.dot_general(
        whole, whole, (((1,), (1,)), ((), ())), preferred_element_type=f32
    )


def newton_kernel(grams_ref, whole_ref, after_ref, out_ref):
    gram = total_of([grams_ref[g] for g in range(grams_ref.shape[0])])
    row = lax.broadcasted_iota(jnp.int32, (LATENT, LATENT), 0)
    column = lax.broadcasted_iota(jnp.int32, (LATENT, LATENT), 1)
    eye = jnp.where(row == column, 1.0, 0.0)
    squares = jnp.sum(jnp.sum(gram * eye, axis=1, keepdims=True), axis=0, keepdims=True)
    inverse = 1.0 / (jnp.sqrt(squares) + NORM_EPS)
    dot = lambda a, b: jnp.dot(
        a, b, precision=lax.Precision.HIGHEST, preferred_element_type=f32
    )
    first = gram * inverse * inverse
    poly_first = COEF_A * eye + COEF_B * first + COEF_C * dot(first, first)
    second = dot(poly_first, dot(first, poly_first))
    poly_second = COEF_A * eye + COEF_B * second + COEF_C * dot(second, second)
    factor = 0.2 * float(D) ** 0.5
    both = dot(poly_second, poly_first) * (factor * inverse)
    high = both.astype(bf16)
    low = (both - high.astype(f32)).astype(bf16)
    whole = whole_ref[...]
    out_ref[...] = (
        jnp.dot(high, whole, preferred_element_type=f32)
        + jnp.dot(low, whole, preferred_element_type=f32)
    ).astype(bf16)


SMEM = pl.BlockSpec(memory_space=pltpu.SMEM)
WHOLE = pl.BlockSpec(memory_space=pltpu.VMEM)


PIECE = jax.ShapeDtypeStruct((BLOCK, D // 8), bf16)
AFTER = pl.BlockSpec(memory_space=pl.ANY)
PARAMS = pltpu.CompilerParams(vmem_limit_bytes=VMEM_LIMIT)


def muon_blocks(attention, after):
    part = lax.psum_scatter(attention, "y", scatter_dimension=0, tiled=True)[0]
    blocks = pl.pallas_call(
        cut_kernel,
        in_specs=[SMEM, WHOLE, AFTER],
        out_specs=[WHOLE] * 8,
        out_shape=[PIECE] * 8,
        compiler_params=PARAMS,
        cost_estimate=pl.CostEstimate(flops=170_000_000, bytes_accessed=1_200_000, transcendentals=0),
    )(lax.axis_index("z")[None], part, after)
    return total_of(swap(blocks, "z", 8)).astype(bf16)


def muon_gram(row_block, after):
    gathered = swap([row_block] * 8, "z", 8)
    return pl.pallas_call(
        gram_kernel,
        in_specs=[SMEM] + [WHOLE] * 8 + [AFTER],
        out_specs=[WHOLE] * 2,
        out_shape=[
            jax.ShapeDtypeStruct((LATENT, D // 8), bf16),
            jax.ShapeDtypeStruct((LATENT, LATENT), f32),
        ],
        compiler_params=PARAMS,
        cost_estimate=pl.CostEstimate(flops=300_000_000, bytes_accessed=1_600_000, transcendentals=0),
    )(lax.axis_index("z")[None], *gathered, after)


def muon_update_of(whole, grams, after):
    return pl.pallas_call(
        newton_kernel,
        in_specs=[WHOLE, WHOLE, AFTER],
        out_specs=WHOLE,
        out_shape=jax.ShapeDtypeStruct((LATENT, D // 8), bf16),
        compiler_params=PARAMS,
        cost_estimate=pl.CostEstimate(
            flops=3_000_000_000, bytes_accessed=3_600_000, transcendentals=0
        ),
    )(grams, whole, after)


def muon_spread(update):
    y_at = lax.axis_index("y")
    out = jnp.zeros((4,) + update.shape, bf16)
    for k, got in enumerate(swap([update] * 4, "y", 4)):
        out = lax.dynamic_update_index_in_dim(out, got, lax.rem(y_at + 4 - k, 4), 0)
    return out


def join_kernel(first_ref, second_ref, after_ref, out_ref):
    out_ref[:, 0, :] = first_ref[...]
    out_ref[:, 1, :] = second_ref[...]


def join(first, second, after):
    return pl.pallas_call(
        join_kernel,
        in_specs=[WHOLE, WHOLE, AFTER],
        out_specs=WHOLE,
        out_shape=jax.ShapeDtypeStruct((first.shape[0], 2, first.shape[1]), f32),
        compiler_params=PARAMS,
    )(first, second, after)


def hand_kernel(value_ref, *refs):
    refs[-1][...] = value_ref[...]


def hand(value, *after):
    return pl.pallas_call(
        hand_kernel,
        in_specs=[WHOLE] + [AFTER] * len(after),
        out_specs=WHOLE,
        out_shape=jax.ShapeDtypeStruct(value.shape, value.dtype),
        compiler_params=PARAMS,
    )(value, *after)


def add_kernel(values_ref, after_ref, out_ref):
    total = values_ref[0]
    for i in range(1, values_ref.shape[0]):
        total = total + values_ref[i]
    out_ref[...] = total


def add_up(values, after):
    return pl.pallas_call(
        add_kernel,
        in_specs=[WHOLE, AFTER],
        out_specs=WHOLE,
        out_shape=jax.ShapeDtypeStruct(values.shape[1:], values.dtype),
        compiler_params=PARAMS,
    )(values, after)


def on_device(
    out_grad,
    router_input,
    router_weight,
    routes,
    balance_grad,
    saved_hidden,
    expert_down,
    attention_grads,
):
    width = out_grad.shape[1]
    down = expert_down[0]
    share = saved_hidden.shape[3]
    count = CAP * EXPERTS
    weight_t = router_weight.T
    input_f = router_input.astype(f32)
    packed, position, partial_logits = pack(routes.T, out_grad, router_input, weight_t)
    rows_got = exchange(packed, EP)
    hidden_share = jnp.swapaxes(saved_hidden[0], 0, 1).reshape(count, share)
    hidden = lax.all_gather(hand(hidden_share, position), FS, axis=0, tiled=False)
    logits = total_of(swap([partial_logits] * 8, FS, 8))

    scores = jax.nn.sigmoid(logits)
    chosen = position >= 0.0
    selected = chosen.astype(f32)
    score_total = jnp.sum(selected * scores, axis=0, keepdims=True)
    gates = (selected * ROUTE_SCALE * scores / score_total).astype(bf16).astype(f32)
    slot_ids = jnp.arange(SLOTS, dtype=jnp.int32).astype(f32)
    matches = position[:, None, :] == slot_ids[None, :, None]
    slot_gates = jnp.sum(jnp.where(matches, gates[:, None, :], 0.0), axis=2)
    back = hidden_times_down(hidden, down)
    row_block = muon_blocks(attention_grads[0], slot_gates)
    ready = (row_block[0, 0] < f32(jnp.inf)) & (back[0, 0] < f32(jnp.inf))
    keep = jnp.where(ready, 1.0, 0.0).astype(bf16)
    rows = jnp.swapaxes(rows_got[:, :CAP] * keep, 0, 1).reshape(count, width)
    whole, gram = muon_gram(row_block, back)
    grams = lax.all_gather(gram, FS, axis=0, tiled=False)
    gate_part = jnp.sum(back * rows.astype(f32), axis=1)
    gate_part_t = jnp.pad(gate_part.reshape(CAP, EXPERTS).T, ((0, 0), (0, SLOTS - CAP)))
    joined = join(slot_gates, gate_part_t, position)
    both_got = exchange(joined, EP)
    gate_column = both_got[:, 0, :CAP].T.reshape(count, 1)
    returned = both_got[:, 1]
    back_part = jnp.sum(jnp.where(matches, returned[:, :, None], 0.0), axis=1)
    grad_down = grad_down_of(hidden, rows, gate_column)
    x_at, core_at = lax.axis_index("x"), lax.axis_index("c")
    for_other = upstream_partial(rows, down, x_at, 1 - core_at, joined)
    from_other = lax.ppermute(for_other, "c", [(0, 1), (1, 0)])
    for_own = upstream_partial(rows, down, x_at, core_at, for_other)
    both_cores = (from_other.astype(f32) + for_own.astype(f32)).astype(bf16)
    upstream = total_of(swap([both_cores[k] for k in range(4)], "x", 4))
    back_parts = spread(hand(back_part, gram, for_own), FS, 8)
    gate_back = add_up(back_parts, grad_down)

    grad_hidden = (gate_column * upstream).astype(bf16)
    grad_hidden = jnp.swapaxes(grad_hidden.reshape(CAP, EXPERTS, share), 0, 1)[None]

    weighted = jnp.sum(selected * gate_back * scores, axis=0, keepdims=True) / score_total
    score_grad = balance_grad.T + selected * (ROUTE_SCALE / score_total) * (gate_back - weighted)
    logit_grad = score_grad * scores * (1.0 - scores)
    router_part = jnp.dot(logit_grad, input_f, precision=lax.Precision.HIGHEST)
    router_got = exchange(router_part.reshape(EXPERTS, 1, width), EP)
    update = muon_update_of(whole, grams, router_part)
    muon_update = muon_spread(update)
    router_row = add_up(router_got, update)
    router_grad = spread(router_row, EP, EXPERTS).reshape(EXPERTS, width).T
    token_grad = lax.dot_general(
        logit_grad, weight_t, (((0,), (0,)), ((), ())), precision=lax.Precision.HIGHEST
    ).astype(bf16)
    return (grad_hidden, grad_down, router_grad, token_grad, muon_update)


def solution(mesh):
    split = Mesh(mesh.devices.reshape(4, 2, 8, 4), ("x", "c", "z", "y"))
    in_specs = (
        P(EP, FS),
        P(EP, FS),
        P(FS, None),
        P(EP, None),
        P(EP, None),
        P(EP, None, None, FS),
        P(EP, None, FS),
        P(EP, None, None, FS),
    )
    out_specs = (
        P(EP, None, None, FS),
        P(EP, None, FS),
        P(FS, None),
        P(EP, FS),
        P(None, None, FS),
    )
    return jax.shard_map(
        on_device, mesh=split, in_specs=in_specs, out_specs=out_specs, check_vma=False
    )
```

profile of v0, /device:TPU:2, one launch (start us, length us, event | category | flops | bytes accessed | tf_op | source)
XLA Modules:
  0.0 244.5 jit_solution(13105923898152825060)
XLA Ops:
  8.8 0.9 copy-done.7
  9.7 0.9 copy-done.9
  10.6 0.9 copy-done.13
  11.6 0.7 copy-done.14
  12.3 2.3 shard_map.119
  14.6 0.9 shard_map.120
  15.4 11.6 %all-to-all-start = ((bf16[32,40,896]{2,1,0:T(8,128)(2,1)}), bf16[32,40,896]{2,1,0:T(8,128)(2,1)}, u32[]{:S(2)}, u32[]{:S(2)}) async-start(bf16[32,40,896]{2,1,0:T(8,128)(2,1)} %get-tuple-element.20), calls=%async_computation | async-start | bytes 4587520 | tf_op jit(solution)/shard_map/all_to_all | solution.py:164
  27.1 1.6 collective-permute-start.1
  28.7 1.0 collective-permute-start.2
  29.7 2.4 collective-permute-start.3
  32.8 2.2 collective-permute-start.5
  35.5 1.5 collective-permute-done.5
  37.4 25.1 %reduce-scatter.2.cloned.1.call-done = bf16[1,288,896]{2,1,0:T(8,128)(2,1)} async-done(((bf16[4,288,896]{2,1,0:T(8,128)(2,1)}), bf16[1,288,896]{2,1,0:T(8,128)(2,1)}) %reduce-scatter.2.cloned.1.call-update) | async-done | bytes 516112 | tf_op jit(solution)/shard_map/reduce_scatter | solution.py:258
  62.5 1.0 copy-done.12
  64.1 9.4 %collective-permute-start.10 = (bf16[40,896]{1,0:T(8,128)(2,1)S(1)}, bf16[40,896]{1,0:T(8,128)(2,1)S(1)}, u32[]{:S(2)}, u32[]{:S(2)}) collective-permute-start(bf16[40,896]{1,0:T(8,128)(2,1)S(1)} %get-tuple-element.25), channel_id=1, source_target_pairs={{0,16},{4,20},{8,24},{12,28},{16,0},{20,4},{24,8},{28,12},{1,17},{... | collective-permute-start | bytes 215048 | tf_op jit(solution)/shard_map/ppermute | solution.py:174
  73.5 1.9 collective-permute-start.12
  75.4 2.2 collective-permute-start.13
  77.6 8.2 %collective-permute-done.10 = bf16[40,896]{1,0:T(8,128)(2,1)S(1)} collective-permute-done((bf16[40,896]{1,0:T(8,128)(2,1)S(1)}, bf16[40,896]{1,0:T(8,128)(2,1)S(1)}, u32[]{:S(2)}, u32[]{:S(2)}) %collective-permute-start.10) | collective-permute-done | bytes 71712 | tf_op jit(solution)/shard_map/ppermute | solution.py:174
  86.1 1.4 collective-permute-done.11
  87.5 4.2 %collective-permute-start.9 = (bf16[40,896]{1,0:T(8,128)(2,1)S(1)}, bf16[40,896]{1,0:T(8,128)(2,1)S(1)}, u32[]{:S(2)}, u32[]{:S(2)}) collective-permute-start(bf16[40,896]{1,0:T(8,128)(2,1)S(1)} %get-tuple-element.24), channel_id=1, source_target_pairs={{0,12},{4,16},{8,20},{12,24},{16,28},{20,0},{24,4},{28,8},{1,13},{... | collective-permute-start | bytes 215048 | tf_op jit(solution)/shard_map/ppermute | solution.py:174
  91.8 1.9 collective-permute-done.8
  93.7 1.1 collective-permute-done.9
  94.9 5.8 %collective-permute-start.18 = (bf16[40,896]{1,0:T(8,128)(2,1)S(1)}, bf16[40,896]{1,0:T(8,128)(2,1)S(1)}, u32[]{:S(2)}, u32[]{:S(2)}) collective-permute-start(bf16[40,896]{1,0:T(8,128)(2,1)S(1)} %add_convert_fusion.1.refs_0_), channel_id=1, source_target_pairs={{0,4},{4,8},{8,12},{12,16},{16,20},{20,24},{24,28},{28,0},{1,5},{5... | collective-permute-start | bytes 215048 | tf_op jit(solution)/shard_map/ppermute | solution.py:174
  100.7 2.2 collective-permute-start.20
  102.9 4.0 %collective-permute-start.21 = (bf16[40,896]{1,0:T(8,128)(2,1)S(1)}, bf16[40,896]{1,0:T(8,128)(2,1)S(1)}, u32[]{:S(2)}, u32[]{:S(2)}) collective-permute-start(bf16[40,896]{1,0:T(8,128)(2,1)S(1)} %add_convert_fusion.1.refs_0_), channel_id=1, source_target_pairs={{0,16},{4,20},{8,24},{12,28},{16,0},{20,4},{24,8},{28,12},{1,17},{... | collective-permute-start | bytes 215048 | tf_op jit(solution)/shard_map/ppermute | solution.py:174
  106.9 0.8 collective-permute-start.22
  108.9 2.0 copy-done.4
  110.9 8.2 %shard_map.121.refs_8_ = f32[1152,896]{1,0:T(8,128)} custom-call(bf16[8,1152,256]{2,1,0:T(8,128)(2,1)} %bitcast.82, bf16[2048,896]{1,0:T(8,128)(2,1)S(1)} %bitcast.70), custom_call_target="tpu_custom_call" | custom-call | flops 4227858432 | bytes 12500000 | tf_op jit(solution)/shard_map/pallas_call | solution.py:116
  119.1 1.2 slice.38
  121.0 2.3 collective-permute-start.23
  123.2 1.5 collective-permute-start.24
  124.7 1.9 fusion
  126.9 1.1 collective-permute-done.23.refs_6_
  128.7 1.5 shard_map.127
  130.3 2.6 %multiply_reduce_fusion = f32[1152]{0:T(1024)S(1)} fusion(f32[1152,896]{1,0:T(8,128)} %shard_map.121.refs_8_, bf16[36,32,896]{2,1,0:T(8,128)(2,1)S(1)} %copy.25), kind=kLoop, calls=%fused_computation.1 | loop fusion | flops 3095424 | bytes 6197760 | tf_op jit(solution)/shard_map/reduce_sum | solution.py:389
  133.7 6.1 %shard_map.124.refs_0_ = bf16[4,1152,256]{2,1,0:T(8,128)(2,1)} custom-call(s32[2]{0:T(128)S(1)} %pad_add_fusion.first_ref, bf16[1152,896]{1,0:T(8,128)(2,1)S(1)} %bitcast.65, bf16[2048,896]{1,0:T(8,128)(2,1)} %bitcast.68, f32[32,2,40]{2,1,0:T(2,128)} %shard_map.123.refs_0_), custom_call_target="tpu_custom_call" | custom-call | flops 2113929216 | bytes 6300000 | tf_op jit(solution)/shard_map/pallas_call | solution.py:94
  140.0 8.4 %all-to-all-start.1 = ((f32[32,2,40]{2,1,0:T(2,128)}), f32[32,2,40]{2,1,0:T(2,128)S(1)}, u32[]{:S(2)}, u32[]{:S(2)}) async-start(f32[32,2,40]{2,1,0:T(2,128)} %shard_map.123.refs_0_), calls=%async_computation.2 | async-start | bytes 65536 | tf_op jit(solution)/shard_map/all_to_all | solution.py:164
  148.4 5.1 %shard_map.125.refs_1_ = bf16[4,1152,256]{2,1,0:T(8,128)(2,1)S(1)} custom-call(s32[2]{0:T(128)S(1)} %pad_add_fusion.1.first_ref, bf16[1152,896]{1,0:T(8,128)(2,1)S(1)} %bitcast.66, bf16[2048,896]{1,0:T(8,128)(2,1)} %bitcast.69, bf16[4,1152,256]{2,1,0:T(8,128)(2,1)} %shard_map.124.refs_0_), custom_call_target="tpu_custom_call" | custom-call | flops 2113929216 | bytes 6300000 | tf_op jit(solution)/shard_map/pallas_call | solution.py:94
  153.6 1.4 copy-done
  155.0 3.2 %all-to-all-done.1 = f32[32,2,40]{2,1,0:T(2,128)S(1)} async-done(((f32[32,2,40]{2,1,0:T(2,128)}), f32[32,2,40]{2,1,0:T(2,128)S(1)}, u32[]{:S(2)}, u32[]{:S(2)}) %all-to-all-start.1) | async-done | bytes 10272 | tf_op jit(solution)/shard_map/all_to_all | solution.py:164
  158.5 1.7 copy-done.1
  160.9 4.2 %all-to-all-start.2 = ((f32[8,32,128]{2,1,0:T(8,128)}), f32[8,32,128]{2,1,0:T(8,128)S(1)}, u32[]{:S(2)}, u32[]{:S(2)}) async-start(f32[8,32,128]{2,1,0:T(8,128)} %broadcast_in_dim.72), calls=%async_computation.3 | async-start | bytes 262144 | tf_op jit(solution)/shard_map/all_to_all | solution.py:164
  165.8 10.5 %shard_map.126.after_ref = bf16[1,2048,896]{2,1,0:T(8,128)(2,1)} custom-call(bf16[8,1152,256]{2,1,0:T(8,128)(2,1)} %bitcast.83, bf16[1152,896]{1,0:T(8,128)(2,1)S(1)} %bitcast.67, f32[1152,1]{1,0:T(8,128)S(1)} %reshape.76.gate_ref), custom_call_target="tpu_custom_call" | custom-call | flops 4227858432 | bytes 12500000 | tf_op jit(solution)/shard_map/pallas_call | solution.py:145
  176.4 2.2 copy-done.5
  179.1 2.2 add_convert_fusion
  181.4 1.8 collective-permute-start.15
  183.2 0.7 collective-permute-start.16
  183.9 2.5 %collective-permute-start.17 = (bf16[1152,256]{1,0:T(8,128)(2,1)S(1)}, bf16[1152,256]{1,0:T(8,128)(2,1)}, u32[]{:S(2)}, u32[]{:S(2)}) collective-permute-start(bf16[1152,256]{1,0:T(8,128)(2,1)S(1)} %get-tuple-element.35), channel_id=1, source_target_pairs={{0,192},{64,0},{128,64},{192,128},{1,193},{65,1},{129,65},{193,129... | collective-permute-start | bytes 1769480 | tf_op jit(solution)/shard_map/ppermute | solution.py:174
  186.7 0.7 reshape.71
  187.4 6.5 %all-to-all-start.3 = ((f32[32,1,896]{2,1,0:T(1,128)}), f32[32,1,896]{2,1,0:T(1,128)S(1)}, u32[]{:S(2)}, u32[]{:S(2)}) async-start(f32[32,1,896]{2,1,0:T(1,128)} %reshape.71), calls=%async_computation.4 | async-start | bytes 229376 | tf_op jit(solution)/shard_map/all_to_all | solution.py:164
  194.0 1.3 convolution_convert_fusion
  195.2 2.0 copy-done.11
  197.2 6.3 %shard_map.130.after_ref = bf16[288,896]{1,0:T(8,128)(2,1)S(1)} custom-call(f32[8,288,288]{2,1,0:T(8,128)S(1)} %bitcast.73, bf16[288,896]{1,0:T(8,128)(2,1)S(1)} %get-tuple-element.30.whole_ref, f32[32,896]{1,0:T(8,128)S(1)} %fusion.10.after_ref), custom_call_target="tpu_custom_call" | custom-call | flops 3000000000 | bytes 3600000 | tf_op jit(solution)/shard_map/pallas_call | solution.py:286
  203.5 1.9 collective-permute-start.25
  205.4 2.7 %collective-permute-start.26 = (bf16[288,896]{1,0:T(8,128)(2,1)S(1)}, bf16[288,896]{1,0:T(8,128)(2,1)S(1)}, u32[]{:S(2)}, u32[]{:S(2)}) collective-permute-start(bf16[288,896]{1,0:T(8,128)(2,1)S(1)} %shard_map.130.after_ref), channel_id=1, source_target_pairs={{0,2},{1,3},{2,0},{3,1},{4,6},{5,7},{6,4},{7,5},{8,10},{9,11},{10,... | collective-permute-start | bytes 1548296 | tf_op jit(solution)/shard_map/ppermute | solution.py:174
  208.1 3.7 %collective-permute-done.17 = bf16[1152,256]{1,0:T(8,128)(2,1)} collective-permute-done((bf16[1152,256]{1,0:T(8,128)(2,1)S(1)}, bf16[1152,256]{1,0:T(8,128)(2,1)}, u32[]{:S(2)}, u32[]{:S(2)}) %collective-permute-start.17) | collective-permute-done | bytes 589856 | tf_op jit(solution)/shard_map/ppermute | solution.py:174
  211.8 2.7 %fusion.4 = bf16[1152,256]{1,0:T(8,128)(2,1)} fusion(bf16[1152,256]{1,0:T(8,128)(2,1)} %collective-permute-done.17, bf16[1152,256]{1,0:T(8,128)(2,1)} %collective-permute-done.16, bf16[1152,256]{1,0:T(8,128)(2,1)} %collective-permute-done.15, bf16[4,1152,256]{2,1,0:T(8,128)(2,1)} %copy-done.15, f32[1152]{0:T(1024)S(1)} %mul.61), kind=kLoop, calls=%fused_computation.9 | loop fusion | flops 2654208 | bytes 2953728 | tf_op jit(solution)/shard_map/convert_element_type | solution.py:406
  214.5 1.3 collective-permute-start.27
  215.9 0.7 broadcast_in_dim.74
  216.6 5.8 %all-to-all-start.4 = ((f32[32,1,896]{2,1,0:T(1,128)}), f32[32,1,896]{2,1,0:T(1,128)S(1)}, u32[]{:S(2)}, u32[]{:S(2)}) async-start(f32[32,1,896]{2,1,0:T(1,128)} %broadcast_in_dim.74), calls=%async_computation.5 | async-start | bytes 229376 | tf_op jit(solution)/shard_map/all_to_all | solution.py:164
  222.6 10.2 %all-to-all-done.4 = f32[32,1,896]{2,1,0:T(1,128)S(1)} async-done(((f32[32,1,896]{2,1,0:T(1,128)}), f32[32,1,896]{2,1,0:T(1,128)S(1)}, u32[]{:S(2)}, u32[]{:S(2)}) %all-to-all-start.4) | async-done | bytes 114720 | tf_op jit(solution)/shard_map/all_to_all | solution.py:164
  233.4 1.1 bitcast_dynamic-update-slice_fusion.2
  234.6 1.1 bitcast_dynamic-update-slice_fusion
  235.8 1.3 copy-done.16
  (99 shorter events, 9.4 us)
Async XLA Ops:
  8.0 6.6 %copy-start.6 = (bf16[1,32,36,256]{3,1,2,0:T(8,128)(2,1)S(1)}, bf16[1,32,36,256]{3,1,2,0:T(8,128)(2,1)}, u32[]{:S(2)}) copy-start(bf16[1,32,36,256]{3,1,2,0:T(8,128)(2,1)} %param.13) | copy-start | bytes 1769476
  8.0 54.5 %reduce-scatter.2.cloned.1.call-start = ((), (), s32[]{:S(2)}) async-start(), calls=%async_computation.6 | async-start | bytes 2580480 | tf_op jit(solution)/shard_map/reduce_scatter | solution.py:258
  8.7 100.2 %all-gather.5.cloned.1.call-start = ((), (), s32[]{:S(2)}) async-start(), calls=%async_computation.7 | async-start | bytes 5308416 | tf_op jit(solution)/shard_map/all_gather | solution.py:371
  8.8 0.9 copy-start.7
  9.7 0.9 copy-start.9
  10.6 0.9 copy-start.13
  11.6 0.7 copy-start.14
  15.4 109.3 %all-to-all-start = ((bf16[32,40,896]{2,1,0:T(8,128)(2,1)}), bf16[32,40,896]{2,1,0:T(8,128)(2,1)}, u32[]{:S(2)}, u32[]{:S(2)}) async-start(bf16[32,40,896]{2,1,0:T(8,128)(2,1)} %get-tuple-element.20), calls=%async_computation | async-start | bytes 4587520 | tf_op jit(solution)/shard_map/all_to_all | solution.py:164
  27.1 168.2 %all-gather.7.cloned.1.call-start = ((), (), s32[]{:S(2)}) async-start(), calls=%async_computation.8 | async-start | bytes 3981312 | tf_op jit(solution)/shard_map/all_gather | solution.py:388
  27.1 5.7 %collective-permute-start = (f32[32,128]{1,0:T(8,128)S(1)}, f32[32,128]{1,0:T(8,128)S(1)}, u32[]{:S(2)}, u32[]{:S(2)}) collective-permute-start(f32[32,128]{1,0:T(8,128)S(1)} %get-tuple-element.19), channel_id=1, source_target_pairs={{0,32},{32,64},{64,96},{96,128},{128,160},{160,192},{192,224},{224... | collective-permute-start | bytes 49160 | tf_op jit(solution)/shard_map/ppermute | solution.py:174
  27.1 7.8 %collective-permute-start.1 = (f32[32,128]{1,0:T(8,128)S(1)}, f32[32,128]{1,0:T(8,128)S(1)}, u32[]{:S(2)}, u32[]{:S(2)}) collective-permute-start(f32[32,128]{1,0:T(8,128)S(1)} %get-tuple-element.19), channel_id=1, source_target_pairs={{0,64},{32,96},{64,128},{96,160},{128,192},{160,224},{192,0},{224,... | collective-permute-start | bytes 49160 | tf_op jit(solution)/shard_map/ppermute | solution.py:174
  28.7 6.3 %collective-permute-start.2 = (f32[32,128]{1,0:T(8,128)S(1)}, f32[32,128]{1,0:T(8,128)S(1)}, u32[]{:S(2)}, u32[]{:S(2)}) collective-permute-start(f32[32,128]{1,0:T(8,128)S(1)} %get-tuple-element.19), channel_id=1, source_target_pairs={{0,96},{32,128},{64,160},{96,192},{128,224},{160,0},{192,32},{224,... | collective-permute-start | bytes 49160 | tf_op jit(solution)/shard_map/ppermute | solution.py:174
  29.7 5.4 %collective-permute-start.3 = (f32[32,128]{1,0:T(8,128)S(1)}, f32[32,128]{1,0:T(8,128)S(1)}, u32[]{:S(2)}, u32[]{:S(2)}) collective-permute-start(f32[32,128]{1,0:T(8,128)S(1)} %get-tuple-element.19), channel_id=1, source_target_pairs={{0,128},{32,160},{64,192},{96,224},{128,0},{160,32},{192,64},{224,... | collective-permute-start | bytes 49160 | tf_op jit(solution)/shard_map/ppermute | solution.py:174
  32.2 3.3 %collective-permute-start.4 = (f32[32,128]{1,0:T(8,128)S(1)}, f32[32,128]{1,0:T(8,128)S(1)}, u32[]{:S(2)}, u32[]{:S(2)}) collective-permute-start(f32[32,128]{1,0:T(8,128)S(1)} %get-tuple-element.19), channel_id=1, source_target_pairs={{0,160},{32,192},{64,224},{96,0},{128,32},{160,64},{192,96},{224,1... | collective-permute-start | bytes 49160 | tf_op jit(solution)/shard_map/ppermute | solution.py:174
  32.8 4.2 %collective-permute-start.5 = (f32[32,128]{1,0:T(8,128)S(1)}, f32[32,128]{1,0:T(8,128)S(1)}, u32[]{:S(2)}, u32[]{:S(2)}) collective-permute-start(f32[32,128]{1,0:T(8,128)S(1)} %get-tuple-element.19), channel_id=1, source_target_pairs={{0,192},{32,224},{64,0},{96,32},{128,64},{160,96},{192,128},{224,1... | collective-permute-start | bytes 49160 | tf_op jit(solution)/shard_map/ppermute | solution.py:174
  35.0 2.1 collective-permute-start.6
  62.5 1.0 copy-start.12
  64.1 21.7 %collective-permute-start.10 = (bf16[40,896]{1,0:T(8,128)(2,1)S(1)}, bf16[40,896]{1,0:T(8,128)(2,1)S(1)}, u32[]{:S(2)}, u32[]{:S(2)}) collective-permute-start(bf16[40,896]{1,0:T(8,128)(2,1)S(1)} %get-tuple-element.25), channel_id=1, source_target_pairs={{0,16},{4,20},{8,24},{12,28},{16,0},{20,4},{24,8},{28,12},{1,17},{... | collective-permute-start | bytes 215048 | tf_op jit(solution)/shard_map/ppermute | solution.py:174
  73.5 14.0 %collective-permute-start.11 = (bf16[40,896]{1,0:T(8,128)(2,1)S(1)}, bf16[40,896]{1,0:T(8,128)(2,1)S(1)}, u32[]{:S(2)}, u32[]{:S(2)}) collective-permute-start(bf16[40,896]{1,0:T(8,128)(2,1)S(1)} %get-tuple-element.26), channel_id=1, source_target_pairs={{0,20},{4,24},{8,28},{12,0},{16,4},{20,8},{24,12},{28,16},{1,21},{... | collective-permute-start | bytes 215048 | tf_op jit(solution)/shard_map/ppermute | solution.py:174
  73.5 18.3 %collective-permute-start.12 = (bf16[40,896]{1,0:T(8,128)(2,1)S(1)}, bf16[40,896]{1,0:T(8,128)(2,1)S(1)}, u32[]{:S(2)}, u32[]{:S(2)}) collective-permute-start(bf16[40,896]{1,0:T(8,128)(2,1)S(1)} %get-tuple-element.27), channel_id=1, source_target_pairs={{0,24},{4,28},{8,0},{12,4},{16,8},{20,12},{24,16},{28,20},{1,25},{... | collective-permute-start | bytes 215048 | tf_op jit(solution)/shard_map/ppermute | solution.py:174
  75.4 16.3 %collective-permute-start.13 = (bf16[40,896]{1,0:T(8,128)(2,1)S(1)}, bf16[40,896]{1,0:T(8,128)(2,1)S(1)}, u32[]{:S(2)}, u32[]{:S(2)}) collective-permute-start(bf16[40,896]{1,0:T(8,128)(2,1)S(1)} %get-tuple-element.28), channel_id=1, source_target_pairs={{0,28},{4,0},{8,4},{12,8},{16,12},{20,16},{24,20},{28,24},{1,29},{... | collective-permute-start | bytes 215048 | tf_op jit(solution)/shard_map/ppermute | solution.py:174
  77.6 14.2 %collective-permute-start.7 = (bf16[40,896]{1,0:T(8,128)(2,1)S(1)}, bf16[40,896]{1,0:T(8,128)(2,1)S(1)}, u32[]{:S(2)}, u32[]{:S(2)}) collective-permute-start(bf16[40,896]{1,0:T(8,128)(2,1)S(1)} %get-tuple-element.22), channel_id=1, source_target_pairs={{0,4},{4,8},{8,12},{12,16},{16,20},{20,24},{24,28},{28,0},{1,5},{5... | collective-permute-start | bytes 215048 | tf_op jit(solution)/shard_map/ppermute | solution.py:174
  85.8 7.9 %collective-permute-start.8 = (bf16[40,896]{1,0:T(8,128)(2,1)S(1)}, bf16[40,896]{1,0:T(8,128)(2,1)S(1)}, u32[]{:S(2)}, u32[]{:S(2)}) collective-permute-start(bf16[40,896]{1,0:T(8,128)(2,1)S(1)} %get-tuple-element.23), channel_id=1, source_target_pairs={{0,8},{4,12},{8,16},{12,20},{16,24},{20,28},{24,0},{28,4},{1,9},{5... | collective-permute-start | bytes 215048 | tf_op jit(solution)/shard_map/ppermute | solution.py:174
  87.5 7.3 %collective-permute-start.9 = (bf16[40,896]{1,0:T(8,128)(2,1)S(1)}, bf16[40,896]{1,0:T(8,128)(2,1)S(1)}, u32[]{:S(2)}, u32[]{:S(2)}) collective-permute-start(bf16[40,896]{1,0:T(8,128)(2,1)S(1)} %get-tuple-element.24), channel_id=1, source_target_pairs={{0,12},{4,16},{8,20},{12,24},{16,28},{20,0},{24,4},{28,8},{1,13},{... | collective-permute-start | bytes 215048 | tf_op jit(solution)/shard_map/ppermute | solution.py:174
  94.9 26.0 %collective-permute-start.18 = (bf16[40,896]{1,0:T(8,128)(2,1)S(1)}, bf16[40,896]{1,0:T(8,128)(2,1)S(1)}, u32[]{:S(2)}, u32[]{:S(2)}) collective-permute-start(bf16[40,896]{1,0:T(8,128)(2,1)S(1)} %add_convert_fusion.1.refs_0_), channel_id=1, source_target_pairs={{0,4},{4,8},{8,12},{12,16},{16,20},{20,24},{24,28},{28,0},{1,5},{5... | collective-permute-start | bytes 215048 | tf_op jit(solution)/shard_map/ppermute | solution.py:174
  100.7 22.5 %collective-permute-start.19 = (bf16[40,896]{1,0:T(8,128)(2,1)S(1)}, bf16[40,896]{1,0:T(8,128)(2,1)S(1)}, u32[]{:S(2)}, u32[]{:S(2)}) collective-permute-start(bf16[40,896]{1,0:T(8,128)(2,1)S(1)} %add_convert_fusion.1.refs_0_), channel_id=1, source_target_pairs={{0,8},{4,12},{8,16},{12,20},{16,24},{20,28},{24,0},{28,4},{1,9},{5... | collective-permute-start | bytes 215048 | tf_op jit(solution)/shard_map/ppermute | solution.py:174
  100.7 26.1 %collective-permute-start.20 = (bf16[40,896]{1,0:T(8,128)(2,1)S(1)}, bf16[40,896]{1,0:T(8,128)(2,1)S(1)}, u32[]{:S(2)}, u32[]{:S(2)}) collective-permute-start(bf16[40,896]{1,0:T(8,128)(2,1)S(1)} %add_convert_fusion.1.refs_0_), channel_id=1, source_target_pairs={{0,12},{4,16},{8,20},{12,24},{16,28},{20,0},{24,4},{28,8},{1,13},{... | collective-permute-start | bytes 215048 | tf_op jit(solution)/shard_map/ppermute | solution.py:174
  102.9 23.9 %collective-permute-start.21 = (bf16[40,896]{1,0:T(8,128)(2,1)S(1)}, bf16[40,896]{1,0:T(8,128)(2,1)S(1)}, u32[]{:S(2)}, u32[]{:S(2)}) collective-permute-start(bf16[40,896]{1,0:T(8,128)(2,1)S(1)} %add_convert_fusion.1.refs_0_), channel_id=1, source_target_pairs={{0,16},{4,20},{8,24},{12,28},{16,0},{20,4},{24,8},{28,12},{1,17},{... | collective-permute-start | bytes 215048 | tf_op jit(solution)/shard_map/ppermute | solution.py:174
  106.9 20.0 %collective-permute-start.22 = (bf16[40,896]{1,0:T(8,128)(2,1)S(1)}, bf16[40,896]{1,0:T(8,128)(2,1)S(1)}, u32[]{:S(2)}, u32[]{:S(2)}) collective-permute-start(bf16[40,896]{1,0:T(8,128)(2,1)S(1)} %add_convert_fusion.1.refs_0_), channel_id=1, source_target_pairs={{0,20},{4,24},{8,28},{12,0},{16,4},{20,8},{24,12},{28,16},{1,21},{... | collective-permute-start | bytes 215048 | tf_op jit(solution)/shard_map/ppermute | solution.py:174
  108.9 2.0 copy-start.4
  121.0 7.1 %collective-permute-start.23 = (bf16[40,896]{1,0:T(8,128)(2,1)S(1)}, bf16[40,896]{1,0:T(8,128)(2,1)S(1)}, u32[]{:S(2)}, u32[]{:S(2)}) collective-permute-start(bf16[40,896]{1,0:T(8,128)(2,1)S(1)} %add_convert_fusion.1.refs_0_), channel_id=1, source_target_pairs={{0,24},{4,28},{8,0},{12,4},{16,8},{20,12},{24,16},{28,20},{1,25},{... | collective-permute-start | bytes 215048 | tf_op jit(solution)/shard_map/ppermute | solution.py:174
  123.2 5.3 %collective-permute-start.24 = (bf16[40,896]{1,0:T(8,128)(2,1)S(1)}, bf16[40,896]{1,0:T(8,128)(2,1)S(1)}, u32[]{:S(2)}, u32[]{:S(2)}) collective-permute-start(bf16[40,896]{1,0:T(8,128)(2,1)S(1)} %add_convert_fusion.1.refs_0_), channel_id=1, source_target_pairs={{0,28},{4,0},{8,4},{12,8},{16,12},{20,16},{24,20},{28,24},{1,29},{... | collective-permute-start | bytes 215048 | tf_op jit(solution)/shard_map/ppermute | solution.py:174
  126.6 2.2 copy-start.3
  139.9 38.8 %collective-permute-start.14 = (bf16[4,1152,256]{2,1,0:T(8,128)(2,1)}, bf16[4,1152,256]{2,1,0:T(8,128)(2,1)}, u32[]{:S(2)}, u32[]{:S(2)}) collective-permute-start(bf16[4,1152,256]{2,1,0:T(8,128)(2,1)} %shard_map.124.refs_0_), channel_id=1, source_target_pairs={{0,32},{32,0},{1,33},{33,1},{2,34},{34,2},{3,35},{35,3},{4,36},{36... | collective-permute-start | bytes 7077896 | tf_op jit(solution)/shard_map/ppermute | solution.py:399
  140.0 18.2 %all-to-all-start.1 = ((f32[32,2,40]{2,1,0:T(2,128)}), f32[32,2,40]{2,1,0:T(2,128)S(1)}, u32[]{:S(2)}, u32[]{:S(2)}) async-start(f32[32,2,40]{2,1,0:T(2,128)} %shard_map.123.refs_0_), calls=%async_computation.2 | async-start | bytes 65536 | tf_op jit(solution)/shard_map/all_to_all | solution.py:164
  153.6 1.4 copy-start
  158.5 1.7 copy-start.1
  160.9 15.5 %all-to-all-start.2 = ((f32[8,32,128]{2,1,0:T(8,128)}), f32[8,32,128]{2,1,0:T(8,128)S(1)}, u32[]{:S(2)}, u32[]{:S(2)}) async-start(f32[8,32,128]{2,1,0:T(8,128)} %broadcast_in_dim.72), calls=%async_computation.3 | async-start | bytes 262144 | tf_op jit(solution)/shard_map/all_to_all | solution.py:164
  165.8 12.8 %copy-start.17 = (f32[128,32]{0,1:T(8,128)S(1)}, f32[128,32]{0,1:T(8,128)}, u32[]{:S(2)}) copy-start(f32[128,32]{0,1:T(8,128)} %param.12) | copy-start | bytes 49156
  176.3 2.8 %copy-start.2 = (bf16[4,1152,256]{2,1,0:T(8,128)(2,1)S(1)}, bf16[4,1152,256]{2,1,0:T(8,128)(2,1)}, u32[]{:S(2)}) copy-start(bf16[4,1152,256]{2,1,0:T(8,128)(2,1)} %copy-done) | copy-start | bytes 7077892
  176.4 2.2 copy-start.5
  181.3 5.4 %copy-start.15 = (bf16[4,1152,256]{2,1,0:T(8,128)(2,1)}, bf16[4,1152,256]{2,1,0:T(8,128)(2,1)S(1)}, u32[]{:S(2)}) copy-start(bf16[4,1152,256]{2,1,0:T(8,128)(2,1)S(1)} %add_convert_fusion) | copy-start | bytes 7077892
  181.3 5.2 %copy-start.8 = (bf16[128,896]{1,0:T(8,128)(2,1)S(1)}, bf16[128,896]{1,0:T(8,128)(2,1)}, u32[]{:S(2)}) copy-start(bf16[128,896]{1,0:T(8,128)(2,1)} %input_ref.1) | copy-start | bytes 688132
  181.3 12.7 %copy-start.10 = (f32[896,32]{0,1:T(8,128)S(1)}, f32[896,32]{0,1:T(8,128)}, u32[]{:S(2)}) copy-start(f32[896,32]{0,1:T(8,128)} %param.10) | copy-start | bytes 344068
  181.4 26.6 %collective-permute-start.15 = (bf16[1152,256]{1,0:T(8,128)(2,1)S(1)}, bf16[1152,256]{1,0:T(8,128)(2,1)}, u32[]{:S(2)}, u32[]{:S(2)}) collective-permute-start(bf16[1152,256]{1,0:T(8,128)(2,1)S(1)} %get-tuple-element.34), channel_id=1, source_target_pairs={{0,64},{64,128},{128,192},{192,0},{1,65},{65,129},{129,193},{193,1... | collective-permute-start | bytes 1769480 | tf_op jit(solution)/shard_map/ppermute | solution.py:174
  183.2 24.9 %collective-permute-start.16 = (bf16[1152,256]{1,0:T(8,128)(2,1)S(1)}, bf16[1152,256]{1,0:T(8,128)(2,1)}, u32[]{:S(2)}, u32[]{:S(2)}) collective-permute-start(bf16[1152,256]{1,0:T(8,128)(2,1)S(1)} %get-tuple-element.36), channel_id=1, source_target_pairs={{0,128},{64,192},{128,0},{192,64},{1,129},{65,193},{129,1},{193,65... | collective-permute-start | bytes 1769480 | tf_op jit(solution)/shard_map/ppermute | solution.py:174
  183.9 27.8 %collective-permute-start.17 = (bf16[1152,256]{1,0:T(8,128)(2,1)S(1)}, bf16[1152,256]{1,0:T(8,128)(2,1)}, u32[]{:S(2)}, u32[]{:S(2)}) collective-permute-start(bf16[1152,256]{1,0:T(8,128)(2,1)S(1)} %get-tuple-element.35), channel_id=1, source_target_pairs={{0,192},{64,0},{128,64},{192,128},{1,193},{65,1},{129,65},{193,129... | collective-permute-start | bytes 1769480 | tf_op jit(solution)/shard_map/ppermute | solution.py:174
  187.4 28.4 %all-to-all-start.3 = ((f32[32,1,896]{2,1,0:T(1,128)}), f32[32,1,896]{2,1,0:T(1,128)S(1)}, u32[]{:S(2)}, u32[]{:S(2)}) async-start(f32[32,1,896]{2,1,0:T(1,128)} %reshape.71), calls=%async_computation.4 | async-start | bytes 229376 | tf_op jit(solution)/shard_map/all_to_all | solution.py:164
  195.2 2.0 copy-start.11
  203.5 29.9 %collective-permute-start.25 = (bf16[288,896]{1,0:T(8,128)(2,1)S(1)}, bf16[288,896]{1,0:T(8,128)(2,1)}, u32[]{:S(2)}, u32[]{:S(2)}) collective-permute-start(bf16[288,896]{1,0:T(8,128)(2,1)S(1)} %shard_map.130.after_ref), channel_id=1, source_target_pairs={{0,1},{1,2},{2,3},{3,0},{4,5},{5,6},{6,7},{7,4},{8,9},{9,10},{10,1... | collective-permute-start | bytes 1548296 | tf_op jit(solution)/shard_map/ppermute | solution.py:174
  205.4 29.1 %collective-permute-start.26 = (bf16[288,896]{1,0:T(8,128)(2,1)S(1)}, bf16[288,896]{1,0:T(8,128)(2,1)S(1)}, u32[]{:S(2)}, u32[]{:S(2)}) collective-permute-start(bf16[288,896]{1,0:T(8,128)(2,1)S(1)} %shard_map.130.after_ref), channel_id=1, source_target_pairs={{0,2},{1,3},{2,0},{3,1},{4,6},{5,7},{6,4},{7,5},{8,10},{9,11},{10,... | collective-permute-start | bytes 1548296 | tf_op jit(solution)/shard_map/ppermute | solution.py:174
  214.5 20.1 %collective-permute-start.27 = (bf16[288,896]{1,0:T(8,128)(2,1)S(1)}, bf16[288,896]{1,0:T(8,128)(2,1)}, u32[]{:S(2)}, u32[]{:S(2)}) collective-permute-start(bf16[288,896]{1,0:T(8,128)(2,1)S(1)} %shard_map.130.after_ref), channel_id=1, source_target_pairs={{0,3},{1,0},{2,1},{3,2},{4,7},{5,4},{6,5},{7,6},{8,11},{9,8},{10,9... | collective-permute-start | bytes 1548296 | tf_op jit(solution)/shard_map/ppermute | solution.py:174
  216.6 16.2 %all-to-all-start.4 = ((f32[32,1,896]{2,1,0:T(1,128)}), f32[32,1,896]{2,1,0:T(1,128)S(1)}, u32[]{:S(2)}, u32[]{:S(2)}) async-start(f32[32,1,896]{2,1,0:T(1,128)} %broadcast_in_dim.74), calls=%async_computation.5 | async-start | bytes 229376 | tf_op jit(solution)/shard_map/all_to_all | solution.py:164
  235.7 1.3 copy-start.16
Sparse Core Ops, SparseCore 0:
  11.4 51.0 reduce-scatter.1
Sparse Core Ops, SparseCore 1:
  15.5 39.9 all-gather.4
  130.4 30.0 all-gather.6
where the time goes:
time: 246 us; the launch traced here: 244 us
  starting transfers between devices  90 us (37%)
  waiting for transfers between devices  59.3 us (24%)
  Pallas kernels  42 us (17%)
  local copies, waits for them, and re-layouts  24 us (10%)
  between operations  17.2 us (7%)
  other arithmetic  10.4 us (4%)
    ppermute x27, starting transfers between devices, swap(): lax.ppermute(pieces[k], axes, [(i, (i + k) % size) for i in range(size)])  53.3 us
    all_to_all x5, starting transfers between devices, exchange(): return lax.all_to_all(value, axes, split_axis=0, concat_axis=0, tiled=True)  36.6 us
    reduce_scatter x1, waiting for transfers between devices, muon_blocks(): part = lax.psum_scatter(attention, 'y', scatter_dimension=0, tiled=True)[0]  25.1 us
    ppermute x27, waiting for transfers between devices, swap(): lax.ppermute(pieces[k], axes, [(i, (i + k) % size) for i in range(size)])  20 us
    unnamed x37, local copies, waits for them, and re-layouts  16.4 us
    all_to_all x5, waiting for transfers between devices, exchange(): return lax.all_to_all(value, axes, split_axis=0, concat_axis=0, tiled=True)  13.4 us
    pallas_call x2, Pallas kernels, upstream_partial(): pl.pallas_call(upstream_kernel, grid_spec=grid_spec, out_shape=jax.ShapeD...  11.3 us
    pallas_call x1, Pallas kernels, grad_down_of(): pl.pallas_call(grad_down_kernel, grid=(parts,), in_specs=[pl.BlockSpec((1...  10.5 us
  transfers between devices with their start and end apart: 36, of which 14 were waited for; matrix products, arithmetic and copies ran while one was open for 8% of the time, Pallas kernels for 17%

commit v1 on v0

--- a/solution.py
+++ b/solution.py
@@ -168,11 +168,16 @@
     return exchange(jnp.broadcast_to(value[None], (copies,) + value.shape), axes)
 
 
-def swap(pieces, axes, size):
+def swap(pieces, axes, size, stride=1):
     got = [pieces[0]]
-    for k in range(1, size):
-        got.append(lax.ppermute(pieces[k], axes, [(i, (i + k) % size) for i in range(size)]))
+    for k in range(1, size // stride):
+        pairs = [(i, (i + k * stride) % size) for i in range(size)]
+        got.append(lax.ppermute(pieces[k], axes, pairs))
     return got
+
+
+def to_neighbour(value):
+    return lax.ppermute(value, "z", [(i, i ^ 1) for i in range(8)])
 
 
 def total_of(pieces):
@@ -187,30 +192,34 @@
 SHARE = LATENT // 8
 
 
-def cut_kernel(z_ref, *refs):
-    total, outs = refs[0][...], refs[2:]
+def block_of(piece, z_at, sign):
+    base = z_at + sign * 2 * (piece // 2)
+    base = jnp.where(base >= 8, base - 8, jnp.where(base < 0, base + 8, base))
+    other = jnp.where(base % 2 == 0, base + 1, base - 1)
+    return jnp.where(piece % 2 == 0, base, other)
+
+
+def cut_kernel(z_ref, total_ref, after_ref, *outs):
     row = lax.broadcasted_iota(jnp.int32, (PADDED, LATENT), 0)
     column = lax.broadcasted_iota(jnp.int32, (PADDED, LATENT), 1)
-    shift = row // BLOCK
-    within = row - shift * BLOCK
-    block = shift + z_ref[0]
-    block = jnp.where(block >= 8, block - 8, block)
+    piece = row // BLOCK
+    within = row - piece * BLOCK
+    block = block_of(piece, z_ref[0], 1)
     source = jnp.where(within < SHARE, block * SHARE + within, -1)
     pick = jnp.where(source == column, 1.0, 0.0).astype(bf16)
-    rows = jnp.dot(pick, total, preferred_element_type=f32)
-    for k in range(8):
-        outs[k][...] = rows[k * BLOCK : (k + 1) * BLOCK].astype(bf16)
+    rows = jnp.dot(pick, total_ref[...], preferred_element_type=f32)
+    for k in range(4):
+        outs[k][...] = rows[2 * k * BLOCK : 2 * (k + 1) * BLOCK].astype(bf16)
 
 
 def gram_kernel(z_ref, *refs):
-    parts, whole_ref, gram_ref = refs[:8], refs[9], refs[10]
+    parts, whole_ref, gram_ref = refs[:4], refs[6], refs[7]
     rows = jnp.concatenate([part[...].astype(f32) for part in parts], axis=0).astype(bf16)
     row = lax.broadcasted_iota(jnp.int32, (LATENT, PADDED), 0)
     column = lax.broadcasted_iota(jnp.int32, (LATENT, PADDED), 1)
-    shift = column // BLOCK
-    within = column - shift * BLOCK
-    block = z_ref[0] - shift
-    block = jnp.where(block < 0, block + 8, block)
+    piece = column // BLOCK
+    within = column - piece * BLOCK
+    block = block_of(piece, z_ref[0], -1)
     target = jnp.where(within < SHARE, block * SHARE + within, -1)
     pick = jnp.where(target == row, 1.0, 0.0).astype(bf16)
     whole = jnp.dot(pick, rows, preferred_element_type=f32).astype(bf16)
@@ -249,29 +258,29 @@
 WHOLE = pl.BlockSpec(memory_space=pltpu.VMEM)
 
 
-PIECE = jax.ShapeDtypeStruct((BLOCK, D // 8), bf16)
+PAIR = jax.ShapeDtypeStruct((2 * BLOCK, D // 8), bf16)
 AFTER = pl.BlockSpec(memory_space=pl.ANY)
 PARAMS = pltpu.CompilerParams(vmem_limit_bytes=VMEM_LIMIT)
 
 
 def muon_blocks(attention, after):
     part = lax.psum_scatter(attention, "y", scatter_dimension=0, tiled=True)[0]
-    blocks = pl.pallas_call(
+    return pl.pallas_call(
         cut_kernel,
         in_specs=[SMEM, WHOLE, AFTER],
-        out_specs=[WHOLE] * 8,
-        out_shape=[PIECE] * 8,
+        out_specs=[WHOLE] * 4,
+        out_shape=[PAIR] * 4,
         compiler_params=PARAMS,
         cost_estimate=pl.CostEstimate(flops=170_000_000, bytes_accessed=1_200_000, transcendentals=0),
     )(lax.axis_index("z")[None], part, after)
-    return total_of(swap(blocks, "z", 8)).astype(bf16)
-
-
-def muon_gram(row_block, after):
-    gathered = swap([row_block] * 8, "z", 8)
+
+
+def muon_gram(row_block, first, second):
+    pair = jnp.concatenate([row_block, to_neighbour(row_block)], axis=0)
+    gathered = swap([pair] * 4, "z", 8, 2)
     return pl.pallas_call(
         gram_kernel,
-        in_specs=[SMEM] + [WHOLE] * 8 + [AFTER],
+        in_specs=[SMEM] + [WHOLE] * 4 + [AFTER] * 2,
         out_specs=[WHOLE] * 2,
         out_shape=[
             jax.ShapeDtypeStruct((LATENT, D // 8), bf16),
@@ -279,7 +288,7 @@
         ],
         compiler_params=PARAMS,
         cost_estimate=pl.CostEstimate(flops=300_000_000, bytes_accessed=1_600_000, transcendentals=0),
-    )(lax.axis_index("z")[None], *gathered, after)
+    )(lax.axis_index("z")[None], *gathered, first, second)
 
 
 def muon_update_of(whole, grams, after):
@@ -332,21 +341,21 @@
     )(value, *after)
 
 
-def add_kernel(values_ref, after_ref, out_ref):
+def add_kernel(values_ref, *refs):
     total = values_ref[0]
     for i in range(1, values_ref.shape[0]):
         total = total + values_ref[i]
-    out_ref[...] = total
-
-
-def add_up(values, after):
+    refs[-1][...] = total
+
+
+def add_up(values, *after):
     return pl.pallas_call(
         add_kernel,
-        in_specs=[WHOLE, AFTER],
+        in_specs=[WHOLE] + [AFTER] * len(after),
         out_specs=WHOLE,
         out_shape=jax.ShapeDtypeStruct(values.shape[1:], values.dtype),
         compiler_params=PARAMS,
-    )(values, after)
+    )(values, *after)
 
 
 def on_device(
@@ -368,7 +377,7 @@
     packed, position, partial_logits = pack(routes.T, out_grad, router_input, weight_t)
     rows_got = exchange(packed, EP)
     hidden_share = jnp.swapaxes(saved_hidden[0], 0, 1).reshape(count, share)
-    hidden = lax.all_gather(hand(hidden_share, position), FS, axis=0, tiled=False)
+    hidden = lax.all_gather(hidden_share, FS, axis=0, tiled=False)
     logits = total_of(swap([partial_logits] * 8, FS, 8))
 
     scores = jax.nn.sigmoid(logits)
@@ -380,12 +389,13 @@
     matches = position[:, None, :] == slot_ids[None, :, None]
     slot_gates = jnp.sum(jnp.where(matches, gates[:, None, :], 0.0), axis=2)
     back = hidden_times_down(hidden, down)
-    row_block = muon_blocks(attention_grads[0], slot_gates)
-    ready = (row_block[0, 0] < f32(jnp.inf)) & (back[0, 0] < f32(jnp.inf))
+    blocks = muon_blocks(attention_grads[0], slot_gates)
+    pair_sum = total_of(swap(blocks, "z", 8, 2))
+    for_next = to_neighbour(pair_sum[BLOCK:].astype(bf16))
+    row_block = (pair_sum[:BLOCK] + for_next.astype(f32)).astype(bf16)
+    ready = (blocks[0][0, 0] < f32(jnp.inf)) & (back[0, 0] < f32(jnp.inf))
     keep = jnp.where(ready, 1.0, 0.0).astype(bf16)
     rows = jnp.swapaxes(rows_got[:, :CAP] * keep, 0, 1).reshape(count, width)
-    whole, gram = muon_gram(row_block, back)
-    grams = lax.all_gather(gram, FS, axis=0, tiled=False)
     gate_part = jnp.sum(back * rows.astype(f32), axis=1)
     gate_part_t = jnp.pad(gate_part.reshape(CAP, EXPERTS).T, ((0, 0), (0, SLOTS - CAP)))
     joined = join(slot_gates, gate_part_t, position)
@@ -398,9 +408,11 @@
     for_other = upstream_partial(rows, down, x_at, 1 - core_at, joined)
     from_other = lax.ppermute(for_other, "c", [(0, 1), (1, 0)])
     for_own = upstream_partial(rows, down, x_at, core_at, for_other)
+    whole, gram = muon_gram(row_block, both_got, for_own)
+    grams = lax.all_gather(gram, FS, axis=0, tiled=False)
     both_cores = (from_other.astype(f32) + for_own.astype(f32)).astype(bf16)
     upstream = total_of(swap([both_cores[k] for k in range(4)], "x", 4))
-    back_parts = spread(hand(back_part, gram, for_own), FS, 8)
+    back_parts = spread(hand(back_part, gram), FS, 8)
     gate_back = add_up(back_parts, grad_down)
 
     grad_hidden = (gate_column * upstream).astype(bf16)

time: 246 us -> 246 us (level)
  the two profiles are of different devices: /device:TPU:2 before, /device:TPU:9 now
where the time goes in v1:
time: 246 us; the launch traced here: 245 us
  starting transfers between devices  82.9 us (34%)
  waiting for transfers between devices  70 us (28%)
  Pallas kernels  40.5 us (16%)
  local copies, waits for them, and re-layouts  24.6 us (10%)
  between operations  17.2 us (7%)
  other arithmetic  8.36 us (3%)
    all_to_all x5, starting transfers between devices, exchange(): return lax.all_to_all(value, axes, split_axis=0, concat_axis=0, tiled=True)  41 us
    ppermute x19, starting transfers between devices, swap(): got.append(lax.ppermute(pieces[k], axes, pairs))  32 us
    reduce_scatter x1, waiting for transfers between devices, muon_blocks(): part = lax.psum_scatter(attention, 'y', scatter_dimension=0, tiled=True)[0]  25.6 us
    ppermute x19, waiting for transfers between devices, swap(): got.append(lax.ppermute(pieces[k], axes, pairs))  18.8 us
    unnamed x37, local copies, waits for them, and re-layouts  17 us
    all_to_all x5, waiting for transfers between devices, exchange(): return lax.all_to_all(value, axes, split_axis=0, concat_axis=0, tiled=True)  12.5 us
    pallas_call x1, Pallas kernels, grad_down_of(): pl.pallas_call(grad_down_kernel, grid=(parts,), in_specs=[pl.BlockSpec((1...  10.5 us
    pallas_call x2, Pallas kernels, upstream_partial(): pl.pallas_call(upstream_kernel, grid_spec=grid_spec, out_shape=jax.ShapeD...  10.2 us
  transfers between devices with their start and end apart: 30, of which 10 were waited for; matrix products, arithmetic and copies ran while one was open for 7% of the time, Pallas kernels for 16%

profile of v1, /device:TPU:9, one launch (start us, length us, event | category | flops | bytes accessed | tf_op | source)
XLA Modules:
  0.0 245.0 jit_solution(4056015329135849905)
XLA Ops:
  8.1 0.7 reduce-scatter.2.cloned.1.call-update
  9.4 2.3 shard_map.119
  11.7 11.2 %all-to-all-start = ((bf16[32,40,896]{2,1,0:T(8,128)(2,1)}), bf16[32,40,896]{2,1,0:T(8,128)(2,1)}, u32[]{:S(2)}, u32[]{:S(2)}) async-start(bf16[32,40,896]{2,1,0:T(8,128)(2,1)} %get-tuple-element.16), calls=%async_computation | async-start | bytes 4587520 | tf_op jit(solution)/shard_map/all_to_all | solution.py:164
  22.9 1.2 collective-permute-start.6
  24.1 2.5 %collective-permute-start.5 = (f32[32,128]{1,0:T(8,128)S(1)}, f32[32,128]{1,0:T(8,128)S(1)}, u32[]{:S(2)}, u32[]{:S(2)}) collective-permute-start(f32[32,128]{1,0:T(8,128)S(1)} %get-tuple-element.15), channel_id=1, source_target_pairs={{0,192},{32,224},{64,0},{96,32},{128,64},{160,96},{192,128},{224,1... | collective-permute-start | bytes 49160 | tf_op jit(solution)/shard_map/ppermute | solution.py:175
  26.6 0.8 collective-permute-start.4
  27.4 1.8 collective-permute-start.3
  29.2 1.5 collective-permute-start.2
  31.3 0.9 collective-permute-start
  32.2 2.1 collective-permute-done.2
  34.3 1.2 collective-permute-done.1
  35.9 25.6 %reduce-scatter.2.cloned.1.call-done = bf16[1,288,896]{2,1,0:T(8,128)(2,1)} async-done(((bf16[4,288,896]{2,1,0:T(8,128)(2,1)}), bf16[1,288,896]{2,1,0:T(8,128)(2,1)}) %reduce-scatter.2.cloned.1.call-update) | async-done | bytes 516112 | tf_op jit(solution)/shard_map/reduce_scatter | solution.py:267
  61.5 1.0 copy-done.11
  62.5 0.7 shard_map.121
  63.3 4.2 %collective-permute-start.13 = (bf16[80,896]{1,0:T(8,128)(2,1)S(1)}, bf16[80,896]{1,0:T(8,128)(2,1)S(1)}, u32[]{:S(2)}, u32[]{:S(2)}) collective-permute-start(bf16[80,896]{1,0:T(8,128)(2,1)S(1)} %get-tuple-element.20), channel_id=1, source_target_pairs={{0,24},{4,28},{8,0},{12,4},{16,8},{20,12},{24,16},{28,20},{1,25},{... | collective-permute-start | bytes 430088 | tf_op jit(solution)/shard_map/ppermute | solution.py:175
  67.4 2.2 collective-permute-start.12
  69.6 2.3 collective-permute-start.11
  71.9 4.6 %collective-permute-done.13 = bf16[80,896]{1,0:T(8,128)(2,1)S(1)} collective-permute-done((bf16[80,896]{1,0:T(8,128)(2,1)S(1)}, bf16[80,896]{1,0:T(8,128)(2,1)S(1)}, u32[]{:S(2)}, u32[]{:S(2)}) %collective-permute-start.13) | collective-permute-done | bytes 143392 | tf_op jit(solution)/shard_map/ppermute | solution.py:175
  76.4 4.8 %collective-permute-done.12 = bf16[80,896]{1,0:T(8,128)(2,1)S(1)} collective-permute-done((bf16[80,896]{1,0:T(8,128)(2,1)S(1)}, bf16[80,896]{1,0:T(8,128)(2,1)S(1)}, u32[]{:S(2)}, u32[]{:S(2)}) %collective-permute-start.12) | collective-permute-done | bytes 143392 | tf_op jit(solution)/shard_map/ppermute | solution.py:175
  81.2 6.1 %collective-permute-done.11 = bf16[80,896]{1,0:T(8,128)(2,1)S(1)} collective-permute-done((bf16[80,896]{1,0:T(8,128)(2,1)S(1)}, bf16[80,896]{1,0:T(8,128)(2,1)S(1)}, u32[]{:S(2)}, u32[]{:S(2)}) %collective-permute-start.11) | collective-permute-done | bytes 143392 | tf_op jit(solution)/shard_map/ppermute | solution.py:175
  87.5 2.4 collective-permute-start.14
  89.9 1.6 collective-permute-done.14
  91.6 1.5 collective-permute-start.15
  94.9 1.0 collective-permute-start.16
  95.8 2.3 collective-permute-start.17
  98.1 3.0 %collective-permute-start.18 = (bf16[80,896]{1,0:T(8,128)(2,1)S(1)}, bf16[80,896]{1,0:T(8,128)(2,1)S(1)}, u32[]{:S(2)}, u32[]{:S(2)}) collective-permute-start(bf16[80,896]{1,0:T(8,128)(2,1)S(1)} %pad_maximum_fusion.refs_0_), channel_id=1, source_target_pairs={{0,24},{4,28},{8,0},{12,4},{16,8},{20,12},{24,16},{28,20},{1,25},{... | collective-permute-start | bytes 430088 | tf_op jit(solution)/shard_map/ppermute | solution.py:175
  101.0 2.0 copy-done.3
  103.1 8.2 %shard_map.120 = f32[1152,896]{1,0:T(8,128)} custom-call(bf16[8,1152,256]{2,1,0:T(8,128)(2,1)} %all-gather.4.cloned.1.call-done.hidden_ref, bf16[2048,896]{1,0:T(8,128)(2,1)S(1)} %bitcast.69), custom_call_target="tpu_custom_call" | custom-call | flops 4227858432 | bytes 12500000 | tf_op jit(solution)/shard_map/pallas_call | solution.py:116
  111.3 1.2 slice.46
  113.2 1.9 fusion
  115.3 1.9 copy-done.15
  117.9 0.6 shard_map.122.refs_0_
  118.6 7.7 %all-to-all-start.1 = ((f32[32,2,40]{2,1,0:T(2,128)}), f32[32,2,40]{2,1,0:T(2,128)S(1)}, u32[]{:S(2)}, u32[]{:S(2)}) async-start(f32[32,2,40]{2,1,0:T(2,128)} %shard_map.122.refs_0_), calls=%async_computation.2 | async-start | bytes 65536 | tf_op jit(solution)/shard_map/all_to_all | solution.py:164
  126.3 5.1 %shard_map.123.refs_0_ = bf16[4,1152,256]{2,1,0:T(8,128)(2,1)S(1)} custom-call(s32[2]{0:T(128)S(1)} %pad_add_fusion.first_ref, bf16[1152,896]{1,0:T(8,128)(2,1)S(1)} %bitcast.64, bf16[2048,896]{1,0:T(8,128)(2,1)} %bitcast.67, f32[32,2,40]{2,1,0:T(2,128)} %shard_map.122.refs_0_), custom_call_target="tpu_custom_call" | custom-call | flops 2113929216 | bytes 6300000 | tf_op jit(solution)/shard_map/pallas_call | solution.py:94
  131.4 1.4 copy-done.4
  132.9 5.1 %shard_map.124.refs_5_ = bf16[4,1152,256]{2,1,0:T(8,128)(2,1)S(1)} custom-call(s32[2]{0:T(128)S(1)} %pad_add_fusion.1.first_ref, bf16[1152,896]{1,0:T(8,128)(2,1)S(1)} %bitcast.65, bf16[2048,896]{1,0:T(8,128)(2,1)} %bitcast.68, bf16[4,1152,256]{2,1,0:T(8,128)(2,1)} %copy-done.4), custom_call_target="tpu_custom_call" | custom-call | flops 2113929216 | bytes 6300000 | tf_op jit(solution)/shard_map/pallas_call | solution.py:94
  138.0 1.5 copy-done
  139.5 1.7 copy-done.1
  141.2 1.5 shard_map.126
  142.7 0.8 copy-done.9
  143.5 5.8 %collective-permute-start.7 = (bf16[4,1152,256]{2,1,0:T(8,128)(2,1)}, bf16[4,1152,256]{2,1,0:T(8,128)(2,1)}, u32[]{:S(2)}, u32[]{:S(2)}) collective-permute-start(bf16[4,1152,256]{2,1,0:T(8,128)(2,1)} %copy-done.4), channel_id=1, source_target_pairs={{0,32},{32,0},{1,33},{33,1},{2,34},{34,2},{3,35},{35,3},{4,36},{36... | collective-permute-start | bytes 7077896 | tf_op jit(solution)/shard_map/ppermute | solution.py:409
  150.4 0.7 broadcast_in_dim.72
  151.0 4.4 %all-to-all-start.2 = ((f32[8,32,128]{2,1,0:T(8,128)}), f32[8,32,128]{2,1,0:T(8,128)S(1)}, u32[]{:S(2)}, u32[]{:S(2)}) async-start(f32[8,32,128]{2,1,0:T(8,128)} %broadcast_in_dim.72), calls=%async_computation.3 | async-start | bytes 262144 | tf_op jit(solution)/shard_map/all_to_all | solution.py:164
  155.4 10.5 %shard_map.125.refs_0_ = bf16[1,2048,896]{2,1,0:T(8,128)(2,1)} custom-call(bf16[8,1152,256]{2,1,0:T(8,128)(2,1)} %all-gather.4.cloned.1.call-done.hidden_ref, bf16[1152,896]{1,0:T(8,128)(2,1)S(1)} %bitcast.66, f32[1152,1]{1,0:T(8,128)S(1)} %reshape.71.gate_ref), custom_call_target="tpu_custom_call" | custom-call | flops 4227858432 | bytes 12500000 | tf_op jit(solution)/shard_map/pallas_call | solution.py:145
  166.0 2.2 copy-done.5
  168.8 2.2 add_convert_fusion
  171.2 2.8 %collective-permute-start.10 = (bf16[1152,256]{1,0:T(8,128)(2,1)S(1)}, bf16[1152,256]{1,0:T(8,128)(2,1)}, u32[]{:S(2)}, u32[]{:S(2)}) collective-permute-start(bf16[1152,256]{1,0:T(8,128)(2,1)S(1)} %get-tuple-element.27), channel_id=1, source_target_pairs={{0,192},{64,0},{128,64},{192,128},{1,193},{65,1},{129,65},{193,129... | collective-permute-start | bytes 1769480 | tf_op jit(solution)/shard_map/ppermute | solution.py:175
  175.3 0.7 reshape.67
  176.1 9.2 %all-to-all-start.3 = ((f32[32,1,896]{2,1,0:T(1,128)}), f32[32,1,896]{2,1,0:T(1,128)S(1)}, u32[]{:S(2)}, u32[]{:S(2)}) async-start(f32[32,1,896]{2,1,0:T(1,128)} %reshape.67), calls=%async_computation.4 | async-start | bytes 229376 | tf_op jit(solution)/shard_map/all_to_all | solution.py:164
  185.3 1.3 convolution_convert_fusion
  186.5 9.7 %all-gather.6.cloned.1.call-done = f32[2304,288]{1,0:T(8,128)} async-done(((f32[288,288]{1,0:T(8,128)}), f32[2304,288]{1,0:T(8,128)}) %all-gather.6.cloned.1.call-update) | async-done | bytes 2654224 | tf_op jit(solution)/shard_map/all_gather | solution.py:412
  196.3 2.0 copy-done.8
  198.3 6.3 %shard_map.129.refs_0_ = bf16[288,896]{1,0:T(8,128)(2,1)S(1)} custom-call(f32[8,288,288]{2,1,0:T(8,128)S(1)} %bitcast.71, bf16[288,896]{1,0:T(8,128)(2,1)S(1)} %copy-done.10, f32[32,896]{1,0:T(8,128)S(1)} %fusion.11.after_ref), custom_call_target="tpu_custom_call" | custom-call | flops 3000000000 | bytes 3600000 | tf_op jit(solution)/shard_map/pallas_call | solution.py:295
  204.6 1.3 collective-permute-start.19
  205.9 1.1 collective-permute-start.20
  207.0 2.7 %fusion.4 = bf16[1152,256]{1,0:T(8,128)(2,1)} fusion(bf16[1152,256]{1,0:T(8,128)(2,1)} %collective-permute-done.10, bf16[1152,256]{1,0:T(8,128)(2,1)} %collective-permute-done.9, bf16[1152,256]{1,0:T(8,128)(2,1)} %collective-permute-done.8, bf16[4,1152,256]{2,1,0:T(8,128)(2,1)} %copy-done.14, f32[1152]{0:T(1024)S(1)} %mul.61), kind=kLoop, calls=%fused_computation.9 | loop fusion | flops 2654208 | bytes 2953728 | tf_op jit(solution)/shard_map/convert_element_type | solution.py:418
  209.8 1.6 collective-permute-start.21
  211.4 0.7 broadcast_in_dim.74
  212.1 8.5 %all-to-all-start.4 = ((f32[32,1,896]{2,1,0:T(1,128)}), f32[32,1,896]{2,1,0:T(1,128)S(1)}, u32[]{:S(2)}, u32[]{:S(2)}) async-start(f32[32,1,896]{2,1,0:T(1,128)} %broadcast_in_dim.74), calls=%async_computation.5 | async-start | bytes 229376 | tf_op jit(solution)/shard_map/all_to_all | solution.py:164
  220.8 12.5 %all-to-all-done.4 = f32[32,1,896]{2,1,0:T(1,128)S(1)} async-done(((f32[32,1,896]{2,1,0:T(1,128)}), f32[32,1,896]{2,1,0:T(1,128)S(1)}, u32[]{:S(2)}, u32[]{:S(2)}) %all-to-all-start.4) | async-done | bytes 114720 | tf_op jit(solution)/shard_map/all_to_all | solution.py:164
  233.3 0.7 copy.31
  234.0 1.1 bitcast_dynamic-update-slice_fusion.2
  235.1 1.1 bitcast_dynamic-update-slice_fusion.1
  236.3 1.3 copy-done.16
  (89 shorter events, 7.3 us)
Async XLA Ops:
  8.0 1.4 copy-start.13
  8.0 1.4 copy-start.12
  8.0 1.4 copy-start.6
  8.0 1.4 copy-start.7
  8.0 53.4 %reduce-scatter.2.cloned.1.call-start = ((), (), s32[]{:S(2)}) async-start(), calls=%async_computation.7 | async-start | bytes 2580480 | tf_op jit(solution)/shard_map/reduce_scatter | solution.py:267
  8.8 92.3 %all-gather.4.cloned.1.call-start = ((), (), s32[]{:S(2)}) async-start(), calls=%async_computation.6 | async-start | bytes 5308416 | tf_op jit(solution)/shard_map/all_gather | solution.py:380
  11.7 101.4 %all-to-all-start = ((bf16[32,40,896]{2,1,0:T(8,128)(2,1)}), bf16[32,40,896]{2,1,0:T(8,128)(2,1)}, u32[]{:S(2)}, u32[]{:S(2)}) async-start(bf16[32,40,896]{2,1,0:T(8,128)(2,1)} %get-tuple-element.16), calls=%async_computation | async-start | bytes 4587520 | tf_op jit(solution)/shard_map/all_to_all | solution.py:164
  22.9 7.8 %collective-permute-start.6 = (f32[32,128]{1,0:T(8,128)S(1)}, f32[32,128]{1,0:T(8,128)S(1)}, u32[]{:S(2)}, u32[]{:S(2)}) collective-permute-start(f32[32,128]{1,0:T(8,128)S(1)} %get-tuple-element.15), channel_id=1, source_target_pairs={{0,224},{32,0},{64,32},{96,64},{128,96},{160,128},{192,160},{224,1... | collective-permute-start | bytes 49160 | tf_op jit(solution)/shard_map/ppermute | solution.py:175
  24.1 7.2 %collective-permute-start.5 = (f32[32,128]{1,0:T(8,128)S(1)}, f32[32,128]{1,0:T(8,128)S(1)}, u32[]{:S(2)}, u32[]{:S(2)}) collective-permute-start(f32[32,128]{1,0:T(8,128)S(1)} %get-tuple-element.15), channel_id=1, source_target_pairs={{0,192},{32,224},{64,0},{96,32},{128,64},{160,96},{192,128},{224,1... | collective-permute-start | bytes 49160 | tf_op jit(solution)/shard_map/ppermute | solution.py:175
  26.6 5.5 %collective-permute-start.4 = (f32[32,128]{1,0:T(8,128)S(1)}, f32[32,128]{1,0:T(8,128)S(1)}, u32[]{:S(2)}, u32[]{:S(2)}) collective-permute-start(f32[32,128]{1,0:T(8,128)S(1)} %get-tuple-element.15), channel_id=1, source_target_pairs={{0,160},{32,192},{64,224},{96,0},{128,32},{160,64},{192,96},{224,1... | collective-permute-start | bytes 49160 | tf_op jit(solution)/shard_map/ppermute | solution.py:175
  27.4 4.7 %collective-permute-start.3 = (f32[32,128]{1,0:T(8,128)S(1)}, f32[32,128]{1,0:T(8,128)S(1)}, u32[]{:S(2)}, u32[]{:S(2)}) collective-permute-start(f32[32,128]{1,0:T(8,128)S(1)} %get-tuple-element.15), channel_id=1, source_target_pairs={{0,128},{32,160},{64,192},{96,224},{128,0},{160,32},{192,64},{224,... | collective-permute-start | bytes 49160 | tf_op jit(solution)/shard_map/ppermute | solution.py:175
  29.2 5.1 %collective-permute-start.2 = (f32[32,128]{1,0:T(8,128)S(1)}, f32[32,128]{1,0:T(8,128)S(1)}, u32[]{:S(2)}, u32[]{:S(2)}) collective-permute-start(f32[32,128]{1,0:T(8,128)S(1)} %get-tuple-element.15), channel_id=1, source_target_pairs={{0,96},{32,128},{64,160},{96,192},{128,224},{160,0},{192,32},{224,... | collective-permute-start | bytes 49160 | tf_op jit(solution)/shard_map/ppermute | solution.py:175
  30.7 4.8 %collective-permute-start.1 = (f32[32,128]{1,0:T(8,128)S(1)}, f32[32,128]{1,0:T(8,128)S(1)}, u32[]{:S(2)}, u32[]{:S(2)}) collective-permute-start(f32[32,128]{1,0:T(8,128)S(1)} %get-tuple-element.15), channel_id=1, source_target_pairs={{0,64},{32,96},{64,128},{96,160},{128,192},{160,224},{192,0},{224,... | collective-permute-start | bytes 49160 | tf_op jit(solution)/shard_map/ppermute | solution.py:175
  31.3 4.2 %collective-permute-start = (f32[32,128]{1,0:T(8,128)S(1)}, f32[32,128]{1,0:T(8,128)S(1)}, u32[]{:S(2)}, u32[]{:S(2)}) collective-permute-start(f32[32,128]{1,0:T(8,128)S(1)} %get-tuple-element.15), channel_id=1, source_target_pairs={{0,32},{32,64},{64,96},{96,128},{128,160},{160,192},{192,224},{224... | collective-permute-start | bytes 49160 | tf_op jit(solution)/shard_map/ppermute | solution.py:175
  61.5 1.0 copy-start.11
  63.3 13.2 %collective-permute-start.13 = (bf16[80,896]{1,0:T(8,128)(2,1)S(1)}, bf16[80,896]{1,0:T(8,128)(2,1)S(1)}, u32[]{:S(2)}, u32[]{:S(2)}) collective-permute-start(bf16[80,896]{1,0:T(8,128)(2,1)S(1)} %get-tuple-element.20), channel_id=1, source_target_pairs={{0,24},{4,28},{8,0},{12,4},{16,8},{20,12},{24,16},{28,20},{1,25},{... | collective-permute-start | bytes 430088 | tf_op jit(solution)/shard_map/ppermute | solution.py:175
  67.4 13.8 %collective-permute-start.12 = (bf16[80,896]{1,0:T(8,128)(2,1)S(1)}, bf16[80,896]{1,0:T(8,128)(2,1)S(1)}, u32[]{:S(2)}, u32[]{:S(2)}) collective-permute-start(bf16[80,896]{1,0:T(8,128)(2,1)S(1)} %get-tuple-element.19), channel_id=1, source_target_pairs={{0,16},{4,20},{8,24},{12,28},{16,0},{20,4},{24,8},{28,12},{1,17},{... | collective-permute-start | bytes 430088 | tf_op jit(solution)/shard_map/ppermute | solution.py:175
  69.6 17.7 %collective-permute-start.11 = (bf16[80,896]{1,0:T(8,128)(2,1)S(1)}, bf16[80,896]{1,0:T(8,128)(2,1)S(1)}, u32[]{:S(2)}, u32[]{:S(2)}) collective-permute-start(bf16[80,896]{1,0:T(8,128)(2,1)S(1)} %get-tuple-element.18), channel_id=1, source_target_pairs={{0,8},{4,12},{8,16},{12,20},{16,24},{20,28},{24,0},{28,4},{1,9},{5... | collective-permute-start | bytes 430088 | tf_op jit(solution)/shard_map/ppermute | solution.py:175
  87.5 4.1 %collective-permute-start.14 = (bf16[40,896]{1,0:T(8,128)(2,1)S(1)}, bf16[40,896]{1,0:T(8,128)(2,1)S(1)}, u32[]{:S(2)}, u32[]{:S(2)}) collective-permute-start(bf16[40,896]{1,0:T(8,128)(2,1)S(1)} %slice.68), channel_id=1, source_target_pairs={{0,4},{4,0},{8,12},{12,8},{16,20},{20,16},{24,28},{28,24},{1,5},{5... | collective-permute-start | bytes 215048 | tf_op jit(solution)/shard_map/ppermute | solution.py:180
  91.6 3.3 %collective-permute-start.15 = (bf16[40,896]{1,0:T(8,128)(2,1)S(1)}, bf16[40,896]{1,0:T(8,128)(2,1)S(1)}, u32[]{:S(2)}, u32[]{:S(2)}) collective-permute-start(bf16[40,896]{1,0:T(8,128)(2,1)S(1)} %fusion.7), channel_id=1, source_target_pairs={{0,4},{4,0},{8,12},{12,8},{16,20},{20,16},{24,28},{28,24},{1,5},{5... | collective-permute-start | bytes 215048 | tf_op jit(solution)/shard_map/ppermute | solution.py:180
  94.9 44.6 %collective-permute-start.16 = (bf16[80,896]{1,0:T(8,128)(2,1)S(1)}, bf16[80,896]{1,0:T(8,128)(2,1)S(1)}, u32[]{:S(2)}, u32[]{:S(2)}) collective-permute-start(bf16[80,896]{1,0:T(8,128)(2,1)S(1)} %pad_maximum_fusion.refs_0_), channel_id=1, source_target_pairs={{0,8},{4,12},{8,16},{12,20},{16,24},{20,28},{24,0},{28,4},{1,9},{5... | collective-permute-start | bytes 430088 | tf_op jit(solution)/shard_map/ppermute | solution.py:175
  95.8 43.7 %collective-permute-start.17 = (bf16[80,896]{1,0:T(8,128)(2,1)S(1)}, bf16[80,896]{1,0:T(8,128)(2,1)S(1)}, u32[]{:S(2)}, u32[]{:S(2)}) collective-permute-start(bf16[80,896]{1,0:T(8,128)(2,1)S(1)} %pad_maximum_fusion.refs_0_), channel_id=1, source_target_pairs={{0,16},{4,20},{8,24},{12,28},{16,0},{20,4},{24,8},{28,12},{1,17},{... | collective-permute-start | bytes 430088 | tf_op jit(solution)/shard_map/ppermute | solution.py:175
  98.1 41.4 %collective-permute-start.18 = (bf16[80,896]{1,0:T(8,128)(2,1)S(1)}, bf16[80,896]{1,0:T(8,128)(2,1)S(1)}, u32[]{:S(2)}, u32[]{:S(2)}) collective-permute-start(bf16[80,896]{1,0:T(8,128)(2,1)S(1)} %pad_maximum_fusion.refs_0_), channel_id=1, source_target_pairs={{0,24},{4,28},{8,0},{12,4},{16,8},{20,12},{24,16},{28,20},{1,25},{... | collective-permute-start | bytes 430088 | tf_op jit(solution)/shard_map/ppermute | solution.py:175
  101.0 2.0 copy-start.3
  115.0 2.2 copy-start.15
  118.6 20.9 %all-to-all-start.1 = ((f32[32,2,40]{2,1,0:T(2,128)}), f32[32,2,40]{2,1,0:T(2,128)S(1)}, u32[]{:S(2)}, u32[]{:S(2)}) async-start(f32[32,2,40]{2,1,0:T(2,128)} %shard_map.122.refs_0_), calls=%async_computation.2 | async-start | bytes 65536 | tf_op jit(solution)/shard_map/all_to_all | solution.py:164
  126.3 70.0 %all-gather.6.cloned.1.call-start = ((), (), s32[]{:S(2)}) async-start(), calls=%async_computation.8 | async-start | bytes 3981312 | tf_op jit(solution)/shard_map/all_gather | solution.py:412
  131.4 1.5 copy-start.4
  138.0 1.5 copy-start
  139.5 1.7 copy-start.1
  142.7 0.8 copy-start.9
  143.5 24.8 %collective-permute-start.7 = (bf16[4,1152,256]{2,1,0:T(8,128)(2,1)}, bf16[4,1152,256]{2,1,0:T(8,128)(2,1)}, u32[]{:S(2)}, u32[]{:S(2)}) collective-permute-start(bf16[4,1152,256]{2,1,0:T(8,128)(2,1)} %copy-done.4), channel_id=1, source_target_pairs={{0,32},{32,0},{1,33},{33,1},{2,34},{34,2},{3,35},{35,3},{4,36},{36... | collective-permute-start | bytes 7077896 | tf_op jit(solution)/shard_map/ppermute | solution.py:409
  151.0 15.0 %all-to-all-start.2 = ((f32[8,32,128]{2,1,0:T(8,128)}), f32[8,32,128]{2,1,0:T(8,128)S(1)}, u32[]{:S(2)}, u32[]{:S(2)}) async-start(f32[8,32,128]{2,1,0:T(8,128)} %broadcast_in_dim.72), calls=%async_computation.3 | async-start | bytes 262144 | tf_op jit(solution)/shard_map/all_to_all | solution.py:164
  155.4 12.9 %copy-start.17 = (f32[128,32]{0,1:T(8,128)S(1)}, f32[128,32]{0,1:T(8,128)}, u32[]{:S(2)}) copy-start(f32[128,32]{0,1:T(8,128)} %param.12) | copy-start | bytes 49156
  165.9 2.8 %copy-start.2 = (bf16[4,1152,256]{2,1,0:T(8,128)(2,1)S(1)}, bf16[4,1152,256]{2,1,0:T(8,128)(2,1)}, u32[]{:S(2)}) copy-start(bf16[4,1152,256]{2,1,0:T(8,128)(2,1)} %copy-done) | copy-start | bytes 7077892
  166.0 2.2 copy-start.5
  171.0 4.3 %copy-start.14 = (bf16[4,1152,256]{2,1,0:T(8,128)(2,1)}, bf16[4,1152,256]{2,1,0:T(8,128)(2,1)S(1)}, u32[]{:S(2)}) copy-start(bf16[4,1152,256]{2,1,0:T(8,128)(2,1)S(1)} %add_convert_fusion) | copy-start | bytes 7077892
  171.0 25.3 %copy-start.10 = (bf16[288,896]{1,0:T(8,128)(2,1)S(1)}, bf16[288,896]{1,0:T(8,128)(2,1)}, u32[]{:S(2)}) copy-start(bf16[288,896]{1,0:T(8,128)(2,1)} %copy-done.9) | copy-start | bytes 1548292
  171.2 35.9 %collective-permute-start.10 = (bf16[1152,256]{1,0:T(8,128)(2,1)S(1)}, bf16[1152,256]{1,0:T(8,128)(2,1)}, u32[]{:S(2)}, u32[]{:S(2)}) collective-permute-start(bf16[1152,256]{1,0:T(8,128)(2,1)S(1)} %get-tuple-element.27), channel_id=1, source_target_pairs={{0,192},{64,0},{128,64},{192,128},{1,193},{65,1},{129,65},{193,129... | collective-permute-start | bytes 1769480 | tf_op jit(solution)/shard_map/ppermute | solution.py:175
  173.9 33.1 %collective-permute-start.9 = (bf16[1152,256]{1,0:T(8,128)(2,1)S(1)}, bf16[1152,256]{1,0:T(8,128)(2,1)}, u32[]{:S(2)}, u32[]{:S(2)}) collective-permute-start(bf16[1152,256]{1,0:T(8,128)(2,1)S(1)} %get-tuple-element.28), channel_id=1, source_target_pairs={{0,128},{64,192},{128,0},{192,64},{1,129},{65,193},{129,1},{193,65... | collective-permute-start | bytes 1769480 | tf_op jit(solution)/shard_map/ppermute | solution.py:175
  174.5 32.5 %collective-permute-start.8 = (bf16[1152,256]{1,0:T(8,128)(2,1)S(1)}, bf16[1152,256]{1,0:T(8,128)(2,1)}, u32[]{:S(2)}, u32[]{:S(2)}) collective-permute-start(bf16[1152,256]{1,0:T(8,128)(2,1)S(1)} %get-tuple-element.26), channel_id=1, source_target_pairs={{0,64},{64,128},{128,192},{192,0},{1,65},{65,129},{129,193},{193,1... | collective-permute-start | bytes 1769480 | tf_op jit(solution)/shard_map/ppermute | solution.py:175
  176.1 35.3 %all-to-all-start.3 = ((f32[32,1,896]{2,1,0:T(1,128)}), f32[32,1,896]{2,1,0:T(1,128)S(1)}, u32[]{:S(2)}, u32[]{:S(2)}) async-start(f32[32,1,896]{2,1,0:T(1,128)} %reshape.67), calls=%async_computation.4 | async-start | bytes 229376 | tf_op jit(solution)/shard_map/all_to_all | solution.py:164
  196.3 2.0 copy-start.8
  204.6 29.4 %collective-permute-start.19 = (bf16[288,896]{1,0:T(8,128)(2,1)S(1)}, bf16[288,896]{1,0:T(8,128)(2,1)}, u32[]{:S(2)}, u32[]{:S(2)}) collective-permute-start(bf16[288,896]{1,0:T(8,128)(2,1)S(1)} %shard_map.129.refs_0_), channel_id=1, source_target_pairs={{0,1},{1,2},{2,3},{3,0},{4,5},{5,6},{6,7},{7,4},{8,9},{9,10},{10,1... | collective-permute-start | bytes 1548296 | tf_op jit(solution)/shard_map/ppermute | solution.py:175
  205.9 29.2 %collective-permute-start.20 = (bf16[288,896]{1,0:T(8,128)(2,1)S(1)}, bf16[288,896]{1,0:T(8,128)(2,1)}, u32[]{:S(2)}, u32[]{:S(2)}) collective-permute-start(bf16[288,896]{1,0:T(8,128)(2,1)S(1)} %shard_map.129.refs_0_), channel_id=1, source_target_pairs={{0,2},{1,3},{2,0},{3,1},{4,6},{5,7},{6,4},{7,5},{8,10},{9,11},{10,... | collective-permute-start | bytes 1548296 | tf_op jit(solution)/shard_map/ppermute | solution.py:175
  209.8 26.4 %collective-permute-start.21 = (bf16[288,896]{1,0:T(8,128)(2,1)S(1)}, bf16[288,896]{1,0:T(8,128)(2,1)S(1)}, u32[]{:S(2)}, u32[]{:S(2)}) collective-permute-start(bf16[288,896]{1,0:T(8,128)(2,1)S(1)} %shard_map.129.refs_0_), channel_id=1, source_target_pairs={{0,3},{1,0},{2,1},{3,2},{4,7},{5,4},{6,5},{7,6},{8,11},{9,8},{10,9... | collective-permute-start | bytes 1548296 | tf_op jit(solution)/shard_map/ppermute | solution.py:175
  212.1 21.2 %all-to-all-start.4 = ((f32[32,1,896]{2,1,0:T(1,128)}), f32[32,1,896]{2,1,0:T(1,128)S(1)}, u32[]{:S(2)}, u32[]{:S(2)}) async-start(f32[32,1,896]{2,1,0:T(1,128)} %broadcast_in_dim.74), calls=%async_computation.5 | async-start | bytes 229376 | tf_op jit(solution)/shard_map/all_to_all | solution.py:164
  236.3 1.3 copy-start.16
Sparse Core Ops, SparseCore 0:
  11.5 49.9 reduce-scatter.1
Sparse Core Ops, SparseCore 1:
  11.2 41.3 all-gather.3
  143.6 52.7 all-gather.5

commit v2 on v0

--- a/solution.py
+++ b/solution.py
@@ -185,33 +185,32 @@
 BLOCK = 40
 PADDED = 8 * BLOCK
 SHARE = LATENT // 8
-
-
-def cut_kernel(z_ref, *refs):
-    total, outs = refs[0][...], refs[2:]
-    row = lax.broadcasted_iota(jnp.int32, (PADDED, LATENT), 0)
-    column = lax.broadcasted_iota(jnp.int32, (PADDED, LATENT), 1)
-    shift = row // BLOCK
-    within = row - shift * BLOCK
-    block = shift + z_ref[0]
-    block = jnp.where(block >= 8, block - 8, block)
+HALF = LATENT // 2
+
+
+def cut_kernel(y_ref, half_ref, after_ref, *outs):
+    row = lax.broadcasted_iota(jnp.int32, (4 * BLOCK, HALF), 0)
+    column = lax.broadcasted_iota(jnp.int32, (4 * BLOCK, HALF), 1)
+    piece = row // BLOCK
+    within = row - piece * BLOCK
+    block = (piece + y_ref[0]) % 4
     source = jnp.where(within < SHARE, block * SHARE + within, -1)
     pick = jnp.where(source == column, 1.0, 0.0).astype(bf16)
-    rows = jnp.dot(pick, total, preferred_element_type=f32)
-    for k in range(8):
+    rows = jnp.dot(pick, half_ref[...], preferred_element_type=f32)
+    for k in range(4):
         outs[k][...] = rows[k * BLOCK : (k + 1) * BLOCK].astype(bf16)
 
 
-def gram_kernel(z_ref, *refs):
-    parts, whole_ref, gram_ref = refs[:8], refs[9], refs[10]
+def gram_kernel(place_ref, *refs):
+    parts, whole_ref, gram_ref = refs[:4], refs[5], refs[6]
     rows = jnp.concatenate([part[...].astype(f32) for part in parts], axis=0).astype(bf16)
     row = lax.broadcasted_iota(jnp.int32, (LATENT, PADDED), 0)
     column = lax.broadcasted_iota(jnp.int32, (LATENT, PADDED), 1)
-    shift = column // BLOCK
-    within = column - shift * BLOCK
-    block = z_ref[0] - shift
-    block = jnp.where(block < 0, block + 8, block)
-    target = jnp.where(within < SHARE, block * SHARE + within, -1)
+    piece = column // BLOCK
+    within = column - piece * BLOCK
+    block = (place_ref[0] + 4 - piece // 2) % 4
+    half = (place_ref[1] + piece) % 2
+    target = jnp.where(within < SHARE, half * HALF + block * SHARE + within, -1)
     pick = jnp.where(target == row, 1.0, 0.0).astype(bf16)
     whole = jnp.dot(pick, rows, preferred_element_type=f32).astype(bf16)
     whole_ref[...] = whole
@@ -220,7 +219,7 @@
     )
 
 
-def newton_kernel(grams_ref, whole_ref, after_ref, out_ref):
+def newton_kernel(half_ref, grams_ref, whole_ref, after_ref, out_ref, scratch):
     gram = total_of([grams_ref[g] for g in range(grams_ref.shape[0])])
     row = lax.broadcasted_iota(jnp.int32, (LATENT, LATENT), 0)
     column = lax.broadcasted_iota(jnp.int32, (LATENT, LATENT), 1)
@@ -235,7 +234,8 @@
     second = dot(poly_first, dot(first, poly_first))
     poly_second = COEF_A * eye + COEF_B * second + COEF_C * dot(second, second)
     factor = 0.2 * float(D) ** 0.5
-    both = dot(poly_second, poly_first) * (factor * inverse)
+    scratch[...] = dot(poly_second, poly_first) * (factor * inverse)
+    both = scratch[pl.ds(pl.multiple_of(half_ref[0] * HALF, 8), HALF), :]
     high = both.astype(bf16)
     low = (both - high.astype(f32)).astype(bf16)
     whole = whole_ref[...]
@@ -254,24 +254,30 @@
 PARAMS = pltpu.CompilerParams(vmem_limit_bytes=VMEM_LIMIT)
 
 
-def muon_blocks(attention, after):
-    part = lax.psum_scatter(attention, "y", scatter_dimension=0, tiled=True)[0]
+def muon_pair(attention, after):
+    mats, latent, width = attention.shape
+    half = lax.psum_scatter(
+        attention.reshape(mats * latent, width), "z", scatter_dimension=0, tiled=True
+    )
     blocks = pl.pallas_call(
         cut_kernel,
         in_specs=[SMEM, WHOLE, AFTER],
-        out_specs=[WHOLE] * 8,
-        out_shape=[PIECE] * 8,
-        compiler_params=PARAMS,
-        cost_estimate=pl.CostEstimate(flops=170_000_000, bytes_accessed=1_200_000, transcendentals=0),
-    )(lax.axis_index("z")[None], part, after)
-    return total_of(swap(blocks, "z", 8)).astype(bf16)
-
-
-def muon_gram(row_block, after):
-    gathered = swap([row_block] * 8, "z", 8)
+        out_specs=[WHOLE] * 4,
+        out_shape=[PIECE] * 4,
+        compiler_params=PARAMS,
+        cost_estimate=pl.CostEstimate(flops=50_000_000, bytes_accessed=600_000, transcendentals=0),
+    )(lax.axis_index("y")[None], half, after)
+    block = total_of(swap(blocks, "y", 4)).astype(bf16)
+    other = lax.ppermute(block, "z", [(i, i ^ 1) for i in range(8)])
+    return jnp.concatenate([block, other], axis=0)
+
+
+def muon_gram(pair, after):
+    gathered = swap([pair] * 4, "y", 4)
+    place = jnp.stack([lax.axis_index("y"), lax.rem(lax.axis_index("z"), 2)])
     return pl.pallas_call(
         gram_kernel,
-        in_specs=[SMEM] + [WHOLE] * 8 + [AFTER],
+        in_specs=[SMEM] + [WHOLE] * 4 + [AFTER],
         out_specs=[WHOLE] * 2,
         out_shape=[
             jax.ShapeDtypeStruct((LATENT, D // 8), bf16),
@@ -279,28 +285,21 @@
         ],
         compiler_params=PARAMS,
         cost_estimate=pl.CostEstimate(flops=300_000_000, bytes_accessed=1_600_000, transcendentals=0),
-    )(lax.axis_index("z")[None], *gathered, after)
+    )(place, *gathered, after)
 
 
 def muon_update_of(whole, grams, after):
     return pl.pallas_call(
         newton_kernel,
-        in_specs=[WHOLE, WHOLE, AFTER],
+        in_specs=[SMEM, WHOLE, WHOLE, AFTER],
         out_specs=WHOLE,
-        out_shape=jax.ShapeDtypeStruct((LATENT, D // 8), bf16),
+        out_shape=jax.ShapeDtypeStruct((HALF, D // 8), bf16),
+        scratch_shapes=[pltpu.VMEM((LATENT, LATENT), f32)],
         compiler_params=PARAMS,
         cost_estimate=pl.CostEstimate(
             flops=3_000_000_000, bytes_accessed=3_600_000, transcendentals=0
         ),
-    )(grams, whole, after)
-
-
-def muon_spread(update):
-    y_at = lax.axis_index("y")
-    out = jnp.zeros((4,) + update.shape, bf16)
-    for k, got in enumerate(swap([update] * 4, "y", 4)):
-        out = lax.dynamic_update_index_in_dim(out, got, lax.rem(y_at + 4 - k, 4), 0)
-    return out
+    )(lax.rem(lax.axis_index("z"), 2)[None], grams, whole, after)
 
 
 def join_kernel(first_ref, second_ref, after_ref, out_ref):
@@ -332,21 +331,21 @@
     )(value, *after)
 
 
-def add_kernel(values_ref, after_ref, out_ref):
+def add_kernel(values_ref, *refs):
     total = values_ref[0]
     for i in range(1, values_ref.shape[0]):
         total = total + values_ref[i]
-    out_ref[...] = total
-
-
-def add_up(values, after):
+    refs[-1][...] = total
+
+
+def add_up(values, *after):
     return pl.pallas_call(
         add_kernel,
-        in_specs=[WHOLE, AFTER],
+        in_specs=[WHOLE] + [AFTER] * len(after),
         out_specs=WHOLE,
         out_shape=jax.ShapeDtypeStruct(values.shape[1:], values.dtype),
         compiler_params=PARAMS,
-    )(values, after)
+    )(values, *after)
 
 
 def on_device(
@@ -368,7 +367,7 @@
     packed, position, partial_logits = pack(routes.T, out_grad, router_input, weight_t)
     rows_got = exchange(packed, EP)
     hidden_share = jnp.swapaxes(saved_hidden[0], 0, 1).reshape(count, share)
-    hidden = lax.all_gather(hand(hidden_share, position), FS, axis=0, tiled=False)
+    hidden = lax.all_gather(hidden_share, FS, axis=0, tiled=False)
     logits = total_of(swap([partial_logits] * 8, FS, 8))
 
     scores = jax.nn.sigmoid(logits)
@@ -380,12 +379,12 @@
     matches = position[:, None, :] == slot_ids[None, :, None]
     slot_gates = jnp.sum(jnp.where(matches, gates[:, None, :], 0.0), axis=2)
     back = hidden_times_down(hidden, down)
-    row_block = muon_blocks(attention_grads[0], slot_gates)
-    ready = (row_block[0, 0] < f32(jnp.inf)) & (back[0, 0] < f32(jnp.inf))
+    pair = muon_pair(attention_grads[0], slot_gates)
+    whole, gram = muon_gram(pair, back)
+    grams = lax.all_gather(gram, FS, axis=0, tiled=False)
+    ready = (pair[0, 0] < f32(jnp.inf)) & (back[0, 0] < f32(jnp.inf))
     keep = jnp.where(ready, 1.0, 0.0).astype(bf16)
     rows = jnp.swapaxes(rows_got[:, :CAP] * keep, 0, 1).reshape(count, width)
-    whole, gram = muon_gram(row_block, back)
-    grams = lax.all_gather(gram, FS, axis=0, tiled=False)
     gate_part = jnp.sum(back * rows.astype(f32), axis=1)
     gate_part_t = jnp.pad(gate_part.reshape(CAP, EXPERTS).T, ((0, 0), (0, SLOTS - CAP)))
     joined = join(slot_gates, gate_part_t, position)
@@ -400,7 +399,7 @@
     for_own = upstream_partial(rows, down, x_at, core_at, for_other)
     both_cores = (from_other.astype(f32) + for_own.astype(f32)).astype(bf16)
     upstream = total_of(swap([both_cores[k] for k in range(4)], "x", 4))
-    back_parts = spread(hand(back_part, gram, for_own), FS, 8)
+    back_parts = spread(hand(back_part, for_own), FS, 8)
     gate_back = add_up(back_parts, grad_down)
 
     grad_hidden = (gate_column * upstream).astype(bf16)
@@ -412,7 +411,7 @@
     router_part = jnp.dot(logit_grad, input_f, precision=lax.Precision.HIGHEST)
     router_got = exchange(router_part.reshape(EXPERTS, 1, width), EP)
     update = muon_update_of(whole, grams, router_part)
-    muon_update = muon_spread(update)
+    muon_update = lax.all_gather(update, "z", axis=0, tiled=True).reshape(4, LATENT, width)
     router_row = add_up(router_got, update)
     router_grad = spread(router_row, EP, EXPERTS).reshape(EXPERTS, width).T
     token_grad = lax.dot_general(

time: 246 us -> 247 us (level)
  waiting for transfers between devices: 59.3 us -> 85.7 us
  starting transfers between devices: 90 us -> 64.4 us
  local copies, waits for them, and re-layouts: 24 us -> 26.9 us
    reduce_scatter x1, waiting for transfers between devices: 25.1 us -> 57.9 us  [muon_pair(): lax.psum_scatter(attention.reshape(mats * latent, width), 'z', scatter_di...]
    ppermute x27 -> x16, starting transfers between devices: 53.3 us -> 24.2 us  [swap(): lax.ppermute(pieces[k], axes, [(i, (i + k) % size) for i in range(size)])]
    ppermute x27 -> x16, waiting for transfers between devices: 20 us -> 4.47 us  [swap(): lax.ppermute(pieces[k], axes, [(i, (i + k) % size) for i in range(size)])]
    unnamed x37 -> x36, local copies, waits for them, and re-layouts: 16.4 us -> 21.8 us
    all_to_all x5, waiting for transfers between devices: 13.4 us -> 18.7 us  [exchange(): return lax.all_to_all(value, axes, split_axis=0, concat_axis=0, tiled=True)]
    ppermute x0 -> x1, waiting for transfers between devices: none -> 3.32 us  [muon_pair(): other = lax.ppermute(block, 'z', [(i, i ^ 1) for i in range(8)])]
    all_to_all x5, starting transfers between devices: 36.6 us -> 39.1 us  [exchange(): return lax.all_to_all(value, axes, split_axis=0, concat_axis=0, tiled=True)]
  transfers between devices with their start and end apart: 36 -> 27, of which waited for: 14 -> 10; matrix products, arithmetic and copies ran while one was open for 8% -> 6% of each run, Pallas kernels for 17% -> 17%
where the time goes in v2:
time: 247 us; the launch traced here: 246 us
  waiting for transfers between devices  85.7 us (35%)
  starting transfers between devices  64.4 us (26%)
  Pallas kernels  42.1 us (17%)
  local copies, waits for them, and re-layouts  26.9 us (11%)
  between operations  17.2 us (7%)
  other arithmetic  8.03 us (3%)
    reduce_scatter x1, waiting for transfers between devices, muon_pair(): lax.psum_scatter(attention.reshape(mats * latent, width), 'z', scatter_di...  57.9 us
    all_to_all x5, starting transfers between devices, exchange(): return lax.all_to_all(value, axes, split_axis=0, concat_axis=0, tiled=True)  39.1 us
    ppermute x16, starting transfers between devices, swap(): lax.ppermute(pieces[k], axes, [(i, (i + k) % size) for i in range(size)])  24.2 us
    unnamed x36, local copies, waits for them, and re-layouts  21.8 us
    all_to_all x5, waiting for transfers between devices, exchange(): return lax.all_to_all(value, axes, split_axis=0, concat_axis=0, tiled=True)  18.7 us
    pallas_call x2, Pallas kernels, upstream_partial(): pl.pallas_call(upstream_kernel, grid_spec=grid_spec, out_shape=jax.ShapeD...  11.3 us
    pallas_call x1, Pallas kernels, grad_down_of(): pl.pallas_call(grad_down_kernel, grid=(parts,), in_specs=[pl.BlockSpec((1...  10.5 us
    pallas_call x1, Pallas kernels, hidden_times_down(): pl.pallas_call(back_kernel, grid=(steps,), in_specs=[pl.BlockSpec((parts,...  8.11 us
  transfers between devices with their start and end apart: 27, of which 10 were waited for; matrix products, arithmetic and copies ran while one was open for 6% of the time, Pallas kernels for 17%

profile of v2, /device:TPU:2, one launch (start us, length us, event | category | flops | bytes accessed | tf_op | source)
XLA Modules:
  0.0 245.7 jit_solution(9688883483345843426)
XLA Ops:
  8.1 0.7 reduce-scatter.2.cloned.1.call-update
  8.8 0.5 all-gather.5.cloned.1.call-update
  9.4 2.3 shard_map.119
  11.7 11.6 %all-to-all-start = ((bf16[32,40,896]{2,1,0:T(8,128)(2,1)}), bf16[32,40,896]{2,1,0:T(8,128)(2,1)}, u32[]{:S(2)}, u32[]{:S(2)}) async-start(bf16[32,40,896]{2,1,0:T(8,128)(2,1)} %get-tuple-element.16), calls=%async_computation | async-start | bytes 4587520 | tf_op jit(solution)/shard_map/all_to_all | solution.py:164
  23.4 2.4 collective-permute-start.5
  25.8 0.3 collective-permute-start.4
  26.2 1.1 collective-permute-start.3
  27.3 1.2 collective-permute-start.2
  28.5 1.8 collective-permute-start.1
  30.3 1.1 collective-permute-start
  31.5 0.7 collective-permute-done.2
  32.2 1.4 collective-permute-done.1
  33.9 0.3 fusion.5.after_ref.first_ref
  34.2 57.9 %reduce-scatter.2.cloned.1.call-done.half_ref = bf16[144,896]{1,0:T(8,128)(2,1)} async-done(((bf16[1152,896]{1,0:T(8,128)(2,1)}), bf16[144,896]{1,0:T(8,128)(2,1)}) %reduce-scatter.2.cloned.1.call-update) | async-done | bytes 258064 | tf_op jit(solution)/shard_map/reduce_scatter | solution.py:259
  92.1 0.9 copy-done.7
  93.3 2.3 collective-permute-start.7
  95.6 2.6 %collective-permute-start.8 = (bf16[40,896]{1,0:T(8,128)(2,1)S(1)}, bf16[40,896]{1,0:T(8,128)(2,1)S(1)}, u32[]{:S(2)}, u32[]{:S(2)}) collective-permute-start(bf16[40,896]{1,0:T(8,128)(2,1)S(1)} %get-tuple-element.19), channel_id=1, source_target_pairs={{0,2},{1,3},{2,0},{3,1},{4,6},{5,7},{6,4},{7,5},{8,10},{9,11},{10,... | collective-permute-start | bytes 215048 | tf_op jit(solution)/shard_map/ppermute | solution.py:174
  98.2 2.5 %collective-permute-start.9 = (bf16[40,896]{1,0:T(8,128)(2,1)S(1)}, bf16[40,896]{1,0:T(8,128)(2,1)S(1)}, u32[]{:S(2)}, u32[]{:S(2)}) collective-permute-start(bf16[40,896]{1,0:T(8,128)(2,1)S(1)} %get-tuple-element.20), channel_id=1, source_target_pairs={{0,3},{1,0},{2,1},{3,2},{4,7},{5,4},{6,5},{7,6},{8,11},{9,8},{10,9... | collective-permute-start | bytes 215048 | tf_op jit(solution)/shard_map/ppermute | solution.py:174
  100.7 1.4 collective-permute-done.8
  102.1 0.6 collective-permute-done.9
  102.7 1.0 collective-permute-start.14
  103.8 3.3 %collective-permute-done.14 = bf16[40,896]{1,0:T(8,128)(2,1)S(1)} collective-permute-done((bf16[40,896]{1,0:T(8,128)(2,1)S(1)}, bf16[40,896]{1,0:T(8,128)(2,1)S(1)}, u32[]{:S(2)}, u32[]{:S(2)}) %collective-permute-start.14) | collective-permute-done | bytes 71712 | tf_op jit(solution)/shard_map/ppermute | solution.py:271
  107.1 3.7 %collective-permute-start.17 = (bf16[80,896]{1,0:T(8,128)(2,1)S(1)}, bf16[80,896]{1,0:T(8,128)(2,1)S(1)}, u32[]{:S(2)}, u32[]{:S(2)}) collective-permute-start(bf16[80,896]{1,0:T(8,128)(2,1)S(1)} %pad_maximum_fusion.refs_0_), channel_id=1, source_target_pairs={{0,3},{1,0},{2,1},{3,2},{4,7},{5,4},{6,5},{7,6},{8,11},{9,8},{10,9... | collective-permute-start | bytes 430088 | tf_op jit(solution)/shard_map/ppermute | solution.py:174
  110.9 0.9 collective-permute-start.15
  111.8 2.0 copy-done.5
  113.8 8.1 %shard_map.120.refs_4_ = f32[1152,896]{1,0:T(8,128)} custom-call(bf16[8,1152,256]{2,1,0:T(8,128)(2,1)} %all-gather.5.cloned.1.call-done.hidden_ref, bf16[2048,896]{1,0:T(8,128)(2,1)S(1)} %bitcast.62), custom_call_target="tpu_custom_call" | custom-call | flops 4227858432 | bytes 12500000 | tf_op jit(solution)/shard_map/pallas_call | solution.py:116
  121.9 2.2 copy-done.3
  124.1 2.1 shard_map.128
  126.2 0.8 copy-done.11
  127.1 0.5 slice.37
  128.3 1.2 slice.38
  130.2 1.9 fusion
  132.3 1.9 copy-done.4
  134.2 0.6 multiply_reduce_fusion
  134.9 0.6 shard_map.122.refs_0_
  135.6 8.9 %all-to-all-start.1 = ((f32[32,2,40]{2,1,0:T(2,128)}), f32[32,2,40]{2,1,0:T(2,128)S(1)}, u32[]{:S(2)}, u32[]{:S(2)}) async-start(f32[32,2,40]{2,1,0:T(2,128)} %shard_map.122.refs_0_), calls=%async_computation.2 | async-start | bytes 65536 | tf_op jit(solution)/shard_map/all_to_all | solution.py:164
  144.5 6.2 %shard_map.123.refs_0_ = bf16[4,1152,256]{2,1,0:T(8,128)(2,1)} custom-call(s32[2]{0:T(128)S(1)} %pad_add_fusion.first_ref, bf16[1152,896]{1,0:T(8,128)(2,1)S(1)} %bitcast.57, bf16[2048,896]{1,0:T(8,128)(2,1)} %bitcast.60, f32[32,2,40]{2,1,0:T(2,128)} %shard_map.122.refs_0_), custom_call_target="tpu_custom_call" | custom-call | flops 2113929216 | bytes 6300000 | tf_op jit(solution)/shard_map/pallas_call | solution.py:94
  150.7 5.1 %shard_map.124.refs_0_ = bf16[4,1152,256]{2,1,0:T(8,128)(2,1)S(1)} custom-call(s32[2]{0:T(128)S(1)} %pad_add_fusion.1.first_ref, bf16[1152,896]{1,0:T(8,128)(2,1)S(1)} %bitcast.58, bf16[2048,896]{1,0:T(8,128)(2,1)} %bitcast.61, bf16[4,1152,256]{2,1,0:T(8,128)(2,1)} %shard_map.123.refs_0_), custom_call_target="tpu_custom_call" | custom-call | flops 2113929216 | bytes 6300000 | tf_op jit(solution)/shard_map/pallas_call | solution.py:94
  155.8 1.4 copy-done
  157.3 0.6 reshape.75.gate_ref
  158.2 1.7 copy-done.1
  159.8 0.7 broadcast_in_dim.58
  160.5 4.9 %all-to-all-start.2 = ((f32[8,32,128]{2,1,0:T(8,128)}), f32[8,32,128]{2,1,0:T(8,128)S(1)}, u32[]{:S(2)}, u32[]{:S(2)}) async-start(f32[8,32,128]{2,1,0:T(8,128)} %broadcast_in_dim.58), calls=%async_computation.3 | async-start | bytes 262144 | tf_op jit(solution)/shard_map/all_to_all | solution.py:164
  165.4 10.5 %shard_map.125.refs_0_ = bf16[1,2048,896]{2,1,0:T(8,128)(2,1)} custom-call(bf16[8,1152,256]{2,1,0:T(8,128)(2,1)} %all-gather.5.cloned.1.call-done.hidden_ref, bf16[1152,896]{1,0:T(8,128)(2,1)S(1)} %bitcast.59, f32[1152,1]{1,0:T(8,128)S(1)} %reshape.75.gate_ref), custom_call_target="tpu_custom_call" | custom-call | flops 4227858432 | bytes 12500000 | tf_op jit(solution)/shard_map/pallas_call | solution.py:145
  175.9 2.0 copy-done.6
  178.0 0.7 copy-done.16
  179.0 2.0 copy-done.10
  181.0 1.0 copy-done.12
  182.0 6.9 %shard_map.129.refs_0_ = bf16[144,896]{1,0:T(8,128)(2,1)} custom-call(s32[1]{0:T(128)} %bitcast.27.half_ref, f32[8,288,288]{2,1,0:T(8,128)S(1)} %bitcast.64, bf16[288,896]{1,0:T(8,128)(2,1)S(1)} %copy-done.12, f32[32,896]{1,0:T(8,128)S(1)} %fusion.10.after_ref), custom_call_target="tpu_custom_call" | custom-call | flops 3000000000 | bytes 3600000 | tf_op jit(solution)/shard_map/pallas_call | solution.py:292
  188.9 2.2 add_convert_fusion
  191.2 1.4 copy-done.15
  192.7 1.5 collective-permute-start.11
  194.2 0.6 collective-permute-start.13
  194.8 2.1 collective-permute-start.12
  197.0 0.7 reshape.70
  197.7 9.8 %all-to-all-start.3 = ((f32[32,1,896]{2,1,0:T(1,128)}), f32[32,1,896]{2,1,0:T(1,128)S(1)}, u32[]{:S(2)}, u32[]{:S(2)}) async-start(f32[32,1,896]{2,1,0:T(1,128)} %reshape.70), calls=%async_computation.4 | async-start | bytes 229376 | tf_op jit(solution)/shard_map/all_to_all | solution.py:164
  207.5 1.3 convolution_convert_fusion
  208.7 9.7 %all-to-all-done.3.values_ref = f32[32,1,896]{2,1,0:T(1,128)S(1)} async-done(((f32[32,1,896]{2,1,0:T(1,128)}), f32[32,1,896]{2,1,0:T(1,128)S(1)}, u32[]{:S(2)}, u32[]{:S(2)}) %all-to-all-start.3) | async-done | bytes 114720 | tf_op jit(solution)/shard_map/all_to_all | solution.py:164
  218.5 0.7 broadcast_in_dim.61
  219.2 3.9 %all-to-all-start.4 = ((f32[32,1,896]{2,1,0:T(1,128)}), f32[32,1,896]{2,1,0:T(1,128)S(1)}, u32[]{:S(2)}, u32[]{:S(2)}) async-start(f32[32,1,896]{2,1,0:T(1,128)} %broadcast_in_dim.61), calls=%async_computation.5 | async-start | bytes 229376 | tf_op jit(solution)/shard_map/all_to_all | solution.py:164
  223.1 2.4 fusion.4
  225.5 9.0 %all-to-all-done.4 = f32[32,1,896]{2,1,0:T(1,128)S(1)} async-done(((f32[32,1,896]{2,1,0:T(1,128)}), f32[32,1,896]{2,1,0:T(1,128)S(1)}, u32[]{:S(2)}, u32[]{:S(2)}) %all-to-all-start.4) | async-done | bytes 114720 | tf_op jit(solution)/shard_map/all_to_all | solution.py:164
  234.6 0.7 copy.32
  235.2 3.0 %copy.34 = bf16[4,288,896]{2,1,0:T(8,128)(2,1)} copy(bf16[4,288,896]{2,1,0:T(8,128)(2,1)} %bitcast.67) | data formatting | bytes 4128768
  (77 shorter events, 2.7 us)
Async XLA Ops:
  8.0 1.4 copy-start.8
  8.0 1.4 copy-start.9
  8.0 1.4 copy-start.14
  8.0 1.4 copy-start.13
  8.0 84.0 %reduce-scatter.2.cloned.1.call-start = ((), (), s32[]{:S(2)}) async-start(), calls=%async_computation.7 | async-start | bytes 2322432 | tf_op jit(solution)/shard_map/reduce_scatter | solution.py:259
  8.8 103.0 %all-gather.5.cloned.1.call-start = ((), (), s32[]{:S(2)}) async-start(), calls=%async_computation.6 | async-start | bytes 5308416 | tf_op jit(solution)/shard_map/all_gather | solution.py:370
  11.7 118.5 %all-to-all-start = ((bf16[32,40,896]{2,1,0:T(8,128)(2,1)}), bf16[32,40,896]{2,1,0:T(8,128)(2,1)}, u32[]{:S(2)}, u32[]{:S(2)}) async-start(bf16[32,40,896]{2,1,0:T(8,128)(2,1)} %get-tuple-element.16), calls=%async_computation | async-start | bytes 4587520 | tf_op jit(solution)/shard_map/all_to_all | solution.py:164
  23.3 155.6 %all-gather.9.cloned.1.call-start = ((), (), s32[]{:S(2)}) async-start(), calls=%async_computation.9 | async-start | bytes 3981312 | tf_op jit(solution)/shard_map/all_gather | solution.py:384
  23.4 5.1 %collective-permute-start.6 = (f32[32,128]{1,0:T(8,128)S(1)}, f32[32,128]{1,0:T(8,128)S(1)}, u32[]{:S(2)}, u32[]{:S(2)}) collective-permute-start(f32[32,128]{1,0:T(8,128)S(1)} %get-tuple-element.15), channel_id=1, source_target_pairs={{0,224},{32,0},{64,32},{96,64},{128,96},{160,128},{192,160},{224,1... | collective-permute-start | bytes 49160 | tf_op jit(solution)/shard_map/ppermute | solution.py:174
  23.4 6.9 %collective-permute-start.5 = (f32[32,128]{1,0:T(8,128)S(1)}, f32[32,128]{1,0:T(8,128)S(1)}, u32[]{:S(2)}, u32[]{:S(2)}) collective-permute-start(f32[32,128]{1,0:T(8,128)S(1)} %get-tuple-element.15), channel_id=1, source_target_pairs={{0,192},{32,224},{64,0},{96,32},{128,64},{160,96},{192,128},{224,1... | collective-permute-start | bytes 49160 | tf_op jit(solution)/shard_map/ppermute | solution.py:174
  25.8 5.5 %collective-permute-start.4 = (f32[32,128]{1,0:T(8,128)S(1)}, f32[32,128]{1,0:T(8,128)S(1)}, u32[]{:S(2)}, u32[]{:S(2)}) collective-permute-start(f32[32,128]{1,0:T(8,128)S(1)} %get-tuple-element.15), channel_id=1, source_target_pairs={{0,160},{32,192},{64,224},{96,0},{128,32},{160,64},{192,96},{224,1... | collective-permute-start | bytes 49160 | tf_op jit(solution)/shard_map/ppermute | solution.py:174
  26.2 5.4 %collective-permute-start.3 = (f32[32,128]{1,0:T(8,128)S(1)}, f32[32,128]{1,0:T(8,128)S(1)}, u32[]{:S(2)}, u32[]{:S(2)}) collective-permute-start(f32[32,128]{1,0:T(8,128)S(1)} %get-tuple-element.15), channel_id=1, source_target_pairs={{0,128},{32,160},{64,192},{96,224},{128,0},{160,32},{192,64},{224,... | collective-permute-start | bytes 49160 | tf_op jit(solution)/shard_map/ppermute | solution.py:174
  27.3 4.9 %collective-permute-start.2 = (f32[32,128]{1,0:T(8,128)S(1)}, f32[32,128]{1,0:T(8,128)S(1)}, u32[]{:S(2)}, u32[]{:S(2)}) collective-permute-start(f32[32,128]{1,0:T(8,128)S(1)} %get-tuple-element.15), channel_id=1, source_target_pairs={{0,96},{32,128},{64,160},{96,192},{128,224},{160,0},{192,32},{224,... | collective-permute-start | bytes 49160 | tf_op jit(solution)/shard_map/ppermute | solution.py:174
  28.5 5.1 %collective-permute-start.1 = (f32[32,128]{1,0:T(8,128)S(1)}, f32[32,128]{1,0:T(8,128)S(1)}, u32[]{:S(2)}, u32[]{:S(2)}) collective-permute-start(f32[32,128]{1,0:T(8,128)S(1)} %get-tuple-element.15), channel_id=1, source_target_pairs={{0,64},{32,96},{64,128},{96,160},{128,192},{160,224},{192,0},{224,... | collective-permute-start | bytes 49160 | tf_op jit(solution)/shard_map/ppermute | solution.py:174
  30.3 3.5 %collective-permute-start = (f32[32,128]{1,0:T(8,128)S(1)}, f32[32,128]{1,0:T(8,128)S(1)}, u32[]{:S(2)}, u32[]{:S(2)}) collective-permute-start(f32[32,128]{1,0:T(8,128)S(1)} %get-tuple-element.15), channel_id=1, source_target_pairs={{0,32},{32,64},{64,96},{96,128},{128,160},{160,192},{192,224},{224... | collective-permute-start | bytes 49160 | tf_op jit(solution)/shard_map/ppermute | solution.py:174
  92.1 0.9 copy-start.7
  93.3 7.4 %collective-permute-start.7 = (bf16[40,896]{1,0:T(8,128)(2,1)S(1)}, bf16[40,896]{1,0:T(8,128)(2,1)S(1)}, u32[]{:S(2)}, u32[]{:S(2)}) collective-permute-start(bf16[40,896]{1,0:T(8,128)(2,1)S(1)} %get-tuple-element.18), channel_id=1, source_target_pairs={{0,1},{1,2},{2,3},{3,0},{4,5},{5,6},{6,7},{7,4},{8,9},{9,10},{10,1... | collective-permute-start | bytes 215048 | tf_op jit(solution)/shard_map/ppermute | solution.py:174
  95.6 6.5 %collective-permute-start.8 = (bf16[40,896]{1,0:T(8,128)(2,1)S(1)}, bf16[40,896]{1,0:T(8,128)(2,1)S(1)}, u32[]{:S(2)}, u32[]{:S(2)}) collective-permute-start(bf16[40,896]{1,0:T(8,128)(2,1)S(1)} %get-tuple-element.19), channel_id=1, source_target_pairs={{0,2},{1,3},{2,0},{3,1},{4,6},{5,7},{6,4},{7,5},{8,10},{9,11},{10,... | collective-permute-start | bytes 215048 | tf_op jit(solution)/shard_map/ppermute | solution.py:174
  98.2 4.5 %collective-permute-start.9 = (bf16[40,896]{1,0:T(8,128)(2,1)S(1)}, bf16[40,896]{1,0:T(8,128)(2,1)S(1)}, u32[]{:S(2)}, u32[]{:S(2)}) collective-permute-start(bf16[40,896]{1,0:T(8,128)(2,1)S(1)} %get-tuple-element.20), channel_id=1, source_target_pairs={{0,3},{1,0},{2,1},{3,2},{4,7},{5,4},{6,5},{7,6},{8,11},{9,8},{10,9... | collective-permute-start | bytes 215048 | tf_op jit(solution)/shard_map/ppermute | solution.py:174
  102.7 4.4 %collective-permute-start.14 = (bf16[40,896]{1,0:T(8,128)(2,1)S(1)}, bf16[40,896]{1,0:T(8,128)(2,1)S(1)}, u32[]{:S(2)}, u32[]{:S(2)}) collective-permute-start(bf16[40,896]{1,0:T(8,128)(2,1)S(1)} %add_convert_fusion.1), channel_id=1, source_target_pairs={{0,4},{4,0},{8,12},{12,8},{16,20},{20,16},{24,28},{28,24},{1,5},{5... | collective-permute-start | bytes 215048 | tf_op jit(solution)/shard_map/ppermute | solution.py:271
  107.1 14.8 %collective-permute-start.17 = (bf16[80,896]{1,0:T(8,128)(2,1)S(1)}, bf16[80,896]{1,0:T(8,128)(2,1)S(1)}, u32[]{:S(2)}, u32[]{:S(2)}) collective-permute-start(bf16[80,896]{1,0:T(8,128)(2,1)S(1)} %pad_maximum_fusion.refs_0_), channel_id=1, source_target_pairs={{0,3},{1,0},{2,1},{3,2},{4,7},{5,4},{6,5},{7,6},{8,11},{9,8},{10,9... | collective-permute-start | bytes 430088 | tf_op jit(solution)/shard_map/ppermute | solution.py:174
  110.8 11.1 %collective-permute-start.16 = (bf16[80,896]{1,0:T(8,128)(2,1)S(1)}, bf16[80,896]{1,0:T(8,128)(2,1)S(1)}, u32[]{:S(2)}, u32[]{:S(2)}) collective-permute-start(bf16[80,896]{1,0:T(8,128)(2,1)S(1)} %pad_maximum_fusion.refs_0_), channel_id=1, source_target_pairs={{0,2},{1,3},{2,0},{3,1},{4,6},{5,7},{6,4},{7,5},{8,10},{9,11},{10,... | collective-permute-start | bytes 430088 | tf_op jit(solution)/shard_map/ppermute | solution.py:174
  110.9 11.1 %collective-permute-start.15 = (bf16[80,896]{1,0:T(8,128)(2,1)S(1)}, bf16[80,896]{1,0:T(8,128)(2,1)S(1)}, u32[]{:S(2)}, u32[]{:S(2)}) collective-permute-start(bf16[80,896]{1,0:T(8,128)(2,1)S(1)} %pad_maximum_fusion.refs_0_), channel_id=1, source_target_pairs={{0,1},{1,2},{2,3},{3,0},{4,5},{5,6},{6,7},{7,4},{8,9},{9,10},{10,1... | collective-permute-start | bytes 430088 | tf_op jit(solution)/shard_map/ppermute | solution.py:174
  111.8 2.0 copy-start.5
  121.9 2.2 copy-start.3
  126.2 0.8 copy-start.11
  132.0 2.2 copy-start.4
  135.6 21.6 %all-to-all-start.1 = ((f32[32,2,40]{2,1,0:T(2,128)}), f32[32,2,40]{2,1,0:T(2,128)S(1)}, u32[]{:S(2)}, u32[]{:S(2)}) async-start(f32[32,2,40]{2,1,0:T(2,128)} %shard_map.122.refs_0_), calls=%async_computation.2 | async-start | bytes 65536 | tf_op jit(solution)/shard_map/all_to_all | solution.py:164
  150.7 38.3 %collective-permute-start.10 = (bf16[4,1152,256]{2,1,0:T(8,128)(2,1)}, bf16[4,1152,256]{2,1,0:T(8,128)(2,1)}, u32[]{:S(2)}, u32[]{:S(2)}) collective-permute-start(bf16[4,1152,256]{2,1,0:T(8,128)(2,1)} %shard_map.123.refs_0_), channel_id=1, source_target_pairs={{0,32},{32,0},{1,33},{33,1},{2,34},{34,2},{3,35},{35,3},{4,36},{36... | collective-permute-start | bytes 7077896 | tf_op jit(solution)/shard_map/ppermute | solution.py:398
  155.8 1.4 copy-start
  158.2 1.7 copy-start.1
  160.5 15.4 %all-to-all-start.2 = ((f32[8,32,128]{2,1,0:T(8,128)}), f32[8,32,128]{2,1,0:T(8,128)S(1)}, u32[]{:S(2)}, u32[]{:S(2)}) async-start(f32[8,32,128]{2,1,0:T(8,128)} %broadcast_in_dim.58), calls=%async_computation.3 | async-start | bytes 262144 | tf_op jit(solution)/shard_map/all_to_all | solution.py:164
  165.4 69.8 %all-gather.7.cloned.1.call-start = ((), (), s32[]{:S(2)}) async-start(), calls=%async_computation.8 | async-start | bytes 2322432 | tf_op jit(solution)/shard_map/all_gather | solution.py:414
  175.9 2.0 copy-start.6
  178.0 0.7 copy-start.16
  178.9 2.0 copy-start.10
  181.0 1.0 copy-start.12
  182.0 6.9 %copy-start.2 = (bf16[4,1152,256]{2,1,0:T(8,128)(2,1)S(1)}, bf16[4,1152,256]{2,1,0:T(8,128)(2,1)}, u32[]{:S(2)}) copy-start(bf16[4,1152,256]{2,1,0:T(8,128)(2,1)} %copy-done) | copy-start | bytes 7077892
  191.2 1.4 copy-start.15
  192.7 30.4 %collective-permute-start.11 = (bf16[1152,256]{1,0:T(8,128)(2,1)S(1)}, bf16[1152,256]{1,0:T(8,128)(2,1)S(1)}, u32[]{:S(2)}, u32[]{:S(2)}) collective-permute-start(bf16[1152,256]{1,0:T(8,128)(2,1)S(1)} %get-tuple-element.26), channel_id=1, source_target_pairs={{0,64},{64,128},{128,192},{192,0},{1,65},{65,129},{129,193},{193,1... | collective-permute-start | bytes 1769480 | tf_op jit(solution)/shard_map/ppermute | solution.py:174
  194.2 28.9 %collective-permute-start.13 = (bf16[1152,256]{1,0:T(8,128)(2,1)S(1)}, bf16[1152,256]{1,0:T(8,128)(2,1)S(1)}, u32[]{:S(2)}, u32[]{:S(2)}) collective-permute-start(bf16[1152,256]{1,0:T(8,128)(2,1)S(1)} %get-tuple-element.27), channel_id=1, source_target_pairs={{0,192},{64,0},{128,64},{192,128},{1,193},{65,1},{129,65},{193,129... | collective-permute-start | bytes 1769480 | tf_op jit(solution)/shard_map/ppermute | solution.py:174
  194.8 28.3 %collective-permute-start.12 = (bf16[1152,256]{1,0:T(8,128)(2,1)S(1)}, bf16[1152,256]{1,0:T(8,128)(2,1)}, u32[]{:S(2)}, u32[]{:S(2)}) collective-permute-start(bf16[1152,256]{1,0:T(8,128)(2,1)S(1)} %get-tuple-element.28), channel_id=1, source_target_pairs={{0,128},{64,192},{128,0},{192,64},{1,129},{65,193},{129,1},{193,65... | collective-permute-start | bytes 1769480 | tf_op jit(solution)/shard_map/ppermute | solution.py:174
  197.7 20.7 %all-to-all-start.3 = ((f32[32,1,896]{2,1,0:T(1,128)}), f32[32,1,896]{2,1,0:T(1,128)S(1)}, u32[]{:S(2)}, u32[]{:S(2)}) async-start(f32[32,1,896]{2,1,0:T(1,128)} %reshape.70), calls=%async_computation.4 | async-start | bytes 229376 | tf_op jit(solution)/shard_map/all_to_all | solution.py:164
  219.2 15.4 %all-to-all-start.4 = ((f32[32,1,896]{2,1,0:T(1,128)}), f32[32,1,896]{2,1,0:T(1,128)S(1)}, u32[]{:S(2)}, u32[]{:S(2)}) async-start(f32[32,1,896]{2,1,0:T(1,128)} %broadcast_in_dim.61), calls=%async_computation.5 | async-start | bytes 229376 | tf_op jit(solution)/shard_map/all_to_all | solution.py:164
Sparse Core Ops, SparseCore 0:
  11.4 80.6 reduce-scatter.1
  189.0 45.6 all-gather.6
Sparse Core Ops, SparseCore 1:
  11.1 39.2 all-gather.4
  127.1 31.0 all-gather.8

commit v3 on v1

--- a/solution.py
+++ b/solution.py
@@ -24,29 +24,12 @@
 VMEM_LIMIT = 48 * 1024 * 1024
 
 
-def pack_kernel(routes_ref, tokens_ref, input_ref, weight_ref, out_ref, pos_ref, logit_ref):
+def place_kernel(routes_ref, input_ref, weight_ref, pos_ref, logit_ref):
     expert_ids = lax.broadcasted_iota(jnp.int32, (EXPERTS, TOK), 0)
     chosen = jnp.zeros((EXPERTS, TOK), f32)
     for k in range(routes_ref.shape[0]):
         chosen = chosen + jnp.where(routes_ref[k : k + 1, :] == expert_ids, 1.0, 0.0)
-    before = lax.broadcasted_iota(jnp.int32, (TOK, TOK), 0)
-    after = lax.broadcasted_iota(jnp.int32, (TOK, TOK), 1)
-    upper = jnp.where(before <= after, 1.0, 0.0).astype(bf16)
-    counted = jnp.dot(chosen.astype(bf16), upper, preferred_element_type=f32)
-    position = jnp.where(chosen > 0.0, counted - 1.0, -1.0)
-    pos_ref[...] = position
-    slot_ids = lax.broadcasted_iota(jnp.int32, (SLOTS, TOK), 0).astype(f32)
-    tokens = tokens_ref[...]
-    group = 8
-    for start in range(0, EXPERTS, group):
-        picks = [
-            jnp.where(slot_ids == position[e : e + 1, :], 1.0, 0.0)
-            for e in range(start, start + group)
-        ]
-        pick = jnp.concatenate(picks, axis=0).astype(bf16)
-        rows = jnp.dot(pick, tokens, preferred_element_type=f32)
-        for i in range(group):
-            out_ref[start + i] = rows[i * SLOTS : (i + 1) * SLOTS].astype(bf16)
+    pos_ref[...] = slots_of(chosen)
     rest = weight_ref[...]
     logits = jnp.zeros((EXPERTS, TOK), f32)
     for _ in range(3):
@@ -58,18 +41,59 @@
     logit_ref[...] = logits
 
 
-def pack(routes_t, tokens, router_input, weight_t):
-    width = tokens.shape[1]
-    return pl.pallas_call(
-        pack_kernel,
+def slots_of(chosen):
+    before = lax.broadcasted_iota(jnp.int32, (TOK, TOK), 0)
+    after = lax.broadcasted_iota(jnp.int32, (TOK, TOK), 1)
+    upper = jnp.where(before <= after, 1.0, 0.0).astype(bf16)
+    counted = jnp.dot(chosen.astype(bf16), upper, preferred_element_type=f32)
+    return jnp.where(chosen > 0.0, counted - 1.0, -1.0)
+
+
+def place(routes_t, router_input, weight_t):
+    return pl.pallas_call(
+        place_kernel,
         out_shape=(
-            jax.ShapeDtypeStruct((EXPERTS, SLOTS, width), bf16),
             jax.ShapeDtypeStruct((EXPERTS, TOK), f32),
             jax.ShapeDtypeStruct((EXPERTS, TOK), f32),
         ),
         compiler_params=pltpu.CompilerParams(vmem_limit_bytes=VMEM_LIMIT),
-        cost_estimate=pl.CostEstimate(flops=300_000_000, bytes_accessed=2_800_000, transcendentals=0),
-    )(routes_t, tokens, router_input, weight_t)
+        cost_estimate=pl.CostEstimate(flops=30_000_000, bytes_accessed=400_000, transcendentals=0),
+    )(routes_t, router_input, weight_t)
+
+
+def pack_kernel(z_ref, blocks_ref, out_ref):
+    expert = lax.broadcasted_iota(jnp.int32, (4, TOK), 0) + 4 * z_ref[0]
+    expert = expert.astype(f32)
+    picked = []
+    for s in range(8):
+        routes = blocks_ref[s, TOK:, :TOK].astype(f32)
+        chosen = jnp.zeros((4, TOK), f32)
+        for k in range(8):
+            chosen = chosen + jnp.where(routes[k : k + 1, :] == expert, 1.0, 0.0)
+        picked.append(chosen)
+    position = slots_of(jnp.concatenate(picked, axis=0))
+    slot_ids = lax.broadcasted_iota(jnp.int32, (SLOTS, TOK), 0).astype(f32)
+    for s in range(8):
+        picks = [
+            jnp.where(slot_ids == position[4 * s + y : 4 * s + y + 1, :], 1.0, 0.0)
+            for y in range(4)
+        ]
+        pick = jnp.concatenate(picks, axis=0).astype(bf16)
+        rows = jnp.dot(pick, blocks_ref[s, :TOK, :], preferred_element_type=f32)
+        for y in range(4):
+            out_ref[y, s] = rows[y * SLOTS : (y + 1) * SLOTS].astype(bf16)
+
+
+def pack(blocks, z_at):
+    width = blocks.shape[2]
+    return pl.pallas_call(
+        pack_kernel,
+        in_specs=[pl.BlockSpec(memory_space=pltpu.SMEM), pl.BlockSpec(memory_space=pltpu.VMEM)],
+        out_specs=pl.BlockSpec(memory_space=pltpu.VMEM),
+        out_shape=jax.ShapeDtypeStruct((4, 8, SLOTS, width), bf16),
+        compiler_params=pltpu.CompilerParams(vmem_limit_bytes=VMEM_LIMIT),
+        cost_estimate=pl.CostEstimate(flops=300_000_000, bytes_accessed=4_500_000, transcendentals=0),
+    )(z_at[None], blocks)
 
 
 def upstream_kernel(first_ref, rows_ref, down_ref, *refs):
@@ -199,7 +223,8 @@
     return jnp.where(piece % 2 == 0, base, other)
 
 
-def cut_kernel(z_ref, total_ref, after_ref, *outs):
+def cut_kernel(z_ref, total_ref, *refs):
+    outs = refs[2:]
     row = lax.broadcasted_iota(jnp.int32, (PADDED, LATENT), 0)
     column = lax.broadcasted_iota(jnp.int32, (PADDED, LATENT), 1)
     piece = row // BLOCK
@@ -213,7 +238,7 @@
 
 
 def gram_kernel(z_ref, *refs):
-    parts, whole_ref, gram_ref = refs[:4], refs[6], refs[7]
+    parts, whole_ref, gram_ref = refs[:4], refs[4], refs[5]
     rows = jnp.concatenate([part[...].astype(f32) for part in parts], axis=0).astype(bf16)
     row = lax.broadcasted_iota(jnp.int32, (LATENT, PADDED), 0)
     column = lax.broadcasted_iota(jnp.int32, (LATENT, PADDED), 1)
@@ -263,24 +288,24 @@
 PARAMS = pltpu.CompilerParams(vmem_limit_bytes=VMEM_LIMIT)
 
 
-def muon_blocks(attention, after):
+def muon_blocks(attention, *after):
     part = lax.psum_scatter(attention, "y", scatter_dimension=0, tiled=True)[0]
     return pl.pallas_call(
         cut_kernel,
-        in_specs=[SMEM, WHOLE, AFTER],
+        in_specs=[SMEM, WHOLE, AFTER, AFTER],
         out_specs=[WHOLE] * 4,
         out_shape=[PAIR] * 4,
         compiler_params=PARAMS,
         cost_estimate=pl.CostEstimate(flops=170_000_000, bytes_accessed=1_200_000, transcendentals=0),
-    )(lax.axis_index("z")[None], part, after)
-
-
-def muon_gram(row_block, first, second):
+    )(lax.axis_index("z")[None], part, *after)
+
+
+def muon_gram(row_block):
     pair = jnp.concatenate([row_block, to_neighbour(row_block)], axis=0)
     gathered = swap([pair] * 4, "z", 8, 2)
     return pl.pallas_call(
         gram_kernel,
-        in_specs=[SMEM] + [WHOLE] * 4 + [AFTER] * 2,
+        in_specs=[SMEM] + [WHOLE] * 4,
         out_specs=[WHOLE] * 2,
         out_shape=[
             jax.ShapeDtypeStruct((LATENT, D // 8), bf16),
@@ -288,7 +313,7 @@
         ],
         compiler_params=PARAMS,
         cost_estimate=pl.CostEstimate(flops=300_000_000, bytes_accessed=1_600_000, transcendentals=0),
-    )(lax.axis_index("z")[None], *gathered, first, second)
+    )(lax.axis_index("z")[None], *gathered)
 
 
 def muon_update_of(whole, grams, after):
@@ -374,10 +399,13 @@
     count = CAP * EXPERTS
     weight_t = router_weight.T
     input_f = router_input.astype(f32)
-    packed, position, partial_logits = pack(routes.T, out_grad, router_input, weight_t)
-    rows_got = exchange(packed, EP)
-    hidden_share = jnp.swapaxes(saved_hidden[0], 0, 1).reshape(count, share)
-    hidden = lax.all_gather(hidden_share, FS, axis=0, tiled=False)
+    routes_t = routes.T
+    routes_rows = jnp.pad(routes_t.astype(bf16), ((0, 8), (0, width - TOK)))
+    tokens = jnp.concatenate([out_grad, routes_rows], axis=0)
+    blocks_got = lax.all_gather(tokens, "z", axis=0, tiled=False)
+    packed = pack(blocks_got, lax.axis_index("z"))
+    rows_got = exchange(packed, "y")
+    position, partial_logits = place(routes_t, router_input, weight_t)
     logits = total_of(swap([partial_logits] * 8, FS, 8))
 
     scores = jax.nn.sigmoid(logits)
@@ -388,14 +416,17 @@
     slot_ids = jnp.arange(SLOTS, dtype=jnp.int32).astype(f32)
     matches = position[:, None, :] == slot_ids[None, :, None]
     slot_gates = jnp.sum(jnp.where(matches, gates[:, None, :], 0.0), axis=2)
+    hidden_share = jnp.swapaxes(saved_hidden[0], 0, 1).reshape(count, share)
+    hidden = lax.all_gather(hand(hidden_share, slot_gates), FS, axis=0, tiled=False)
     back = hidden_times_down(hidden, down)
-    blocks = muon_blocks(attention_grads[0], slot_gates)
+    blocks = muon_blocks(attention_grads[0], slot_gates, packed)
     pair_sum = total_of(swap(blocks, "z", 8, 2))
     for_next = to_neighbour(pair_sum[BLOCK:].astype(bf16))
     row_block = (pair_sum[:BLOCK] + for_next.astype(f32)).astype(bf16)
-    ready = (blocks[0][0, 0] < f32(jnp.inf)) & (back[0, 0] < f32(jnp.inf))
-    keep = jnp.where(ready, 1.0, 0.0).astype(bf16)
-    rows = jnp.swapaxes(rows_got[:, :CAP] * keep, 0, 1).reshape(count, width)
+    whole, gram = muon_gram(row_block)
+    grams = lax.all_gather(gram, FS, axis=0, tiled=False)
+    keep = jnp.where(back[0, 0] < f32(jnp.inf), 1.0, 0.0).astype(bf16)
+    rows = jnp.transpose(rows_got[:, :, :CAP] * keep, (2, 1, 0, 3)).reshape(count, width)
     gate_part = jnp.sum(back * rows.astype(f32), axis=1)
     gate_part_t = jnp.pad(gate_part.reshape(CAP, EXPERTS).T, ((0, 0), (0, SLOTS - CAP)))
     joined = join(slot_gates, gate_part_t, position)
@@ -408,12 +439,10 @@
     for_other = upstream_partial(rows, down, x_at, 1 - core_at, joined)
     from_other = lax.ppermute(for_other, "c", [(0, 1), (1, 0)])
     for_own = upstream_partial(rows, down, x_at, core_at, for_other)
-    whole, gram = muon_gram(row_block, both_got, for_own)
-    grams = lax.all_gather(gram, FS, axis=0, tiled=False)
     both_cores = (from_other.astype(f32) + for_own.astype(f32)).astype(bf16)
     upstream = total_of(swap([both_cores[k] for k in range(4)], "x", 4))
-    back_parts = spread(hand(back_part, gram), FS, 8)
-    gate_back = add_up(back_parts, grad_down)
+    back_parts = spread(hand(back_part, for_own), FS, 8)
+    gate_back = add_up(back_parts, grad_down, both_cores)
 
     grad_hidden = (gate_column * upstream).astype(bf16)
     grad_hidden = jnp.swapaxes(grad_hidden.reshape(CAP, EXPERTS, share), 0, 1)[None]
@@ -425,7 +454,7 @@
     router_got = exchange(router_part.reshape(EXPERTS, 1, width), EP)
     update = muon_update_of(whole, grams, router_part)
     muon_update = muon_spread(update)
-    router_row = add_up(router_got, update)
+    router_row = add_up(router_got, update, upstream)
     router_grad = spread(router_row, EP, EXPERTS).reshape(EXPERTS, width).T
     token_grad = lax.dot_general(
         logit_grad, weight_t, (((0,), (0,)), ((), ())), precision=lax.Precision.HIGHEST

time: 246 us -> 265 us (1.077)
  the two profiles are of different devices: /device:TPU:9 before, /device:TPU:2 now
where the time goes in v3:
time: 265 us; the launch traced here: 261 us
  waiting for transfers between devices  87.3 us (33%)
  starting transfers between devices  67.9 us (26%)
  Pallas kernels  44.4 us (17%)
  local copies, waits for them, and re-layouts  32.6 us (12%)
  between operations  16.2 us (6%)
  other arithmetic  11.5 us (4%)
    ppermute x19, waiting for transfers between devices, swap(): got.append(lax.ppermute(pieces[k], axes, pairs))  36.5 us
    all_to_all x5, starting transfers between devices, exchange(): return lax.all_to_all(value, axes, split_axis=0, concat_axis=0, tiled=True)  34.5 us
    ppermute x19, starting transfers between devices, swap(): got.append(lax.ppermute(pieces[k], axes, pairs))  31.4 us
    all_gather x1, waiting for transfers between devices, on_device(): blocks_got = lax.all_gather(tokens, 'z', axis=0, tiled=False)  31.3 us
    unnamed x33, local copies, waits for them, and re-layouts  15.9 us
    all_to_all x5, waiting for transfers between devices, exchange(): return lax.all_to_all(value, axes, split_axis=0, concat_axis=0, tiled=True)  11.8 us
    pallas_call x2, Pallas kernels, upstream_partial(): pl.pallas_call(upstream_kernel, grid_spec=grid_spec, out_shape=jax.ShapeD...  11.2 us
    pallas_call x1, Pallas kernels, grad_down_of(): pl.pallas_call(grad_down_kernel, grid=(parts,), in_specs=[pl.BlockSpec((1...  10.6 us
  transfers between devices with their start and end apart: 31, of which 16 were waited for; matrix products, arithmetic and copies ran while one was open for 10% of the time, Pallas kernels for 14%

profile of v3, /device:TPU:2, one launch (start us, length us, event | category | flops | bytes accessed | tf_op | source)
XLA Modules:
  0.0 261.4 jit_solution(9918009905324716749)
XLA Ops:
  8.9 1.7 fusion.6
  11.6 1.6 collective-permute-start.1
  13.1 2.8 %collective-permute-start.2 = (f32[32,128]{1,0:T(8,128)S(1)}, f32[32,128]{1,0:T(8,128)S(1)}, u32[]{:S(2)}, u32[]{:S(2)}) collective-permute-start(f32[32,128]{1,0:T(8,128)S(1)} %get-tuple-element.14), channel_id=1, source_target_pairs={{0,96},{32,128},{64,160},{96,192},{128,224},{160,0},{192,32},{224,... | collective-permute-start | bytes 49160 | tf_op jit(solution)/shard_map/ppermute | solution.py:199
  16.6 2.4 collective-permute-start.4
  19.4 1.0 collective-permute-start.6
  21.2 1.5 collective-permute-done.5
  24.0 31.3 %all-gather.9.cloned.1.call-done = bf16[1152,896]{1,0:T(8,128)(2,1)} async-done(((bf16[144,896]{1,0:T(8,128)(2,1)}), bf16[1152,896]{1,0:T(8,128)(2,1)}) %all-gather.9.cloned.1.call-update) | async-done | bytes 2064400 | tf_op jit(solution)/shard_map/all_gather | solution.py:405
  55.3 1.6 copy-done.5
  56.8 2.3 shard_map.122.refs_1_
  59.1 4.5 %all-to-all-start = ((bf16[4,8,40,896]{3,2,1,0:T(8,128)(2,1)}), bf16[4,8,40,896]{3,2,1,0:T(8,128)(2,1)}, u32[]{:S(2)}, u32[]{:S(2)}) async-start(bf16[4,8,40,896]{3,2,1,0:T(8,128)(2,1)} %shard_map.122.refs_1_), calls=%async_computation | async-start | bytes 4587520 | tf_op jit(solution)/shard_map/all_to_all | solution.py:188
  63.7 1.0 copy-done.8
  65.5 1.4 collective-permute-start.11
  66.9 3.0 %collective-permute-start.12 = (bf16[80,896]{1,0:T(8,128)(2,1)S(1)}, bf16[80,896]{1,0:T(8,128)(2,1)S(1)}, u32[]{:S(2)}, u32[]{:S(2)}) collective-permute-start(bf16[80,896]{1,0:T(8,128)(2,1)S(1)} %get-tuple-element.17), channel_id=1, source_target_pairs={{0,16},{4,20},{8,24},{12,28},{16,0},{20,4},{24,8},{28,12},{1,17},{... | collective-permute-start | bytes 430088 | tf_op jit(solution)/shard_map/ppermute | solution.py:199
  69.9 2.7 %collective-permute-start.13 = (bf16[80,896]{1,0:T(8,128)(2,1)S(1)}, bf16[80,896]{1,0:T(8,128)(2,1)S(1)}, u32[]{:S(2)}, u32[]{:S(2)}) collective-permute-start(bf16[80,896]{1,0:T(8,128)(2,1)S(1)} %get-tuple-element.18), channel_id=1, source_target_pairs={{0,24},{4,28},{8,0},{12,4},{16,8},{20,12},{24,16},{28,20},{1,25},{... | collective-permute-start | bytes 430088 | tf_op jit(solution)/shard_map/ppermute | solution.py:199
  72.6 3.0 %collective-permute-done.11 = bf16[80,896]{1,0:T(8,128)(2,1)S(1)} collective-permute-done((bf16[80,896]{1,0:T(8,128)(2,1)S(1)}, bf16[80,896]{1,0:T(8,128)(2,1)S(1)}, u32[]{:S(2)}, u32[]{:S(2)}) %collective-permute-start.11) | collective-permute-done | bytes 143392 | tf_op jit(solution)/shard_map/ppermute | solution.py:199
  75.6 1.5 collective-permute-done.12
  77.1 4.1 %collective-permute-done.13 = bf16[80,896]{1,0:T(8,128)(2,1)S(1)} collective-permute-done((bf16[80,896]{1,0:T(8,128)(2,1)S(1)}, bf16[80,896]{1,0:T(8,128)(2,1)S(1)}, u32[]{:S(2)}, u32[]{:S(2)}) %collective-permute-start.13) | collective-permute-done | bytes 143392 | tf_op jit(solution)/shard_map/ppermute | solution.py:199
  81.3 0.9 collective-permute-start.14
  82.2 3.5 %collective-permute-done.14 = bf16[40,896]{1,0:T(8,128)(2,1)S(1)} collective-permute-done((bf16[40,896]{1,0:T(8,128)(2,1)S(1)}, bf16[40,896]{1,0:T(8,128)(2,1)S(1)}, u32[]{:S(2)}, u32[]{:S(2)}) %collective-permute-start.14) | collective-permute-done | bytes 71712 | tf_op jit(solution)/shard_map/ppermute | solution.py:204
  85.7 0.9 collective-permute-start.15
  86.6 3.5 %collective-permute-done.15 = bf16[40,896]{1,0:T(8,128)(2,1)S(1)} collective-permute-done((bf16[40,896]{1,0:T(8,128)(2,1)S(1)}, bf16[40,896]{1,0:T(8,128)(2,1)S(1)}, u32[]{:S(2)}, u32[]{:S(2)}) %collective-permute-start.15) | collective-permute-done | bytes 71712 | tf_op jit(solution)/shard_map/ppermute | solution.py:204
  90.1 2.0 collective-permute-start.16
  92.1 3.2 %collective-permute-start.17 = (bf16[80,896]{1,0:T(8,128)(2,1)S(1)}, bf16[80,896]{1,0:T(8,128)(2,1)S(1)}, u32[]{:S(2)}, u32[]{:S(2)}) collective-permute-start(bf16[80,896]{1,0:T(8,128)(2,1)S(1)} %pad_maximum_fusion.refs_0_), channel_id=1, source_target_pairs={{0,16},{4,20},{8,24},{12,28},{16,0},{20,4},{24,8},{28,12},{1,17},{... | collective-permute-start | bytes 430088 | tf_op jit(solution)/shard_map/ppermute | solution.py:199
  95.3 2.2 collective-permute-start.18
  97.5 2.3 collective-permute-done.16.refs_1_
  99.8 4.1 %collective-permute-done.17.refs_2_ = bf16[80,896]{1,0:T(8,128)(2,1)S(1)} collective-permute-done((bf16[80,896]{1,0:T(8,128)(2,1)S(1)}, bf16[80,896]{1,0:T(8,128)(2,1)S(1)}, u32[]{:S(2)}, u32[]{:S(2)}) %collective-permute-start.17) | collective-permute-done | bytes 143392 | tf_op jit(solution)/shard_map/ppermute | solution.py:199
  104.6 1.5 shard_map.130
  107.0 2.0 copy-done.3
  109.0 8.1 %shard_map.121 = f32[1152,896]{1,0:T(8,128)} custom-call(bf16[8,1152,256]{2,1,0:T(8,128)(2,1)} %bitcast.81, bf16[2048,896]{1,0:T(8,128)(2,1)S(1)} %bitcast.68), custom_call_target="tpu_custom_call" | custom-call | flops 4227858432 | bytes 12500000 | tf_op jit(solution)/shard_map/pallas_call | solution.py:140
  117.2 1.2 slice.42
  119.0 2.0 fusion
  121.1 2.9 %copy.25 = bf16[36,8,4,896]{3,2,1,0:T(4,128)(2,1)} copy(bf16[36,8,4,896]{3,0,1,2:T(8,128)(2,1)S(1)} %fusion) | data formatting | bytes 4128768 | tf_op jit(solution)/shard_map/transpose | solution.py:429
  124.0 3.1 %reshape.63.rows_ref = bf16[1152,896]{1,0:T(8,128)(2,1)S(1)} reshape(bf16[36,8,4,896]{3,2,1,0:T(4,128)(2,1)} %copy.25) | data formatting | bytes 4128768 | tf_op jit(solution)/shard_map/reshape | solution.py:429
  127.0 2.7 %multiply_reduce_fusion = f32[1152]{0:T(1024)S(1)} fusion(f32[1152,896]{1,0:T(8,128)} %shard_map.121, bf16[1152,896]{1,0:T(8,128)(2,1)S(1)} %reshape.63.rows_ref), kind=kLoop, calls=%fused_computation.1 | loop fusion | flops 3095424 | bytes 6197760 | tf_op jit(solution)/shard_map/reduce_sum | solution.py:430
  130.6 6.1 %shard_map.124.refs_0_ = bf16[4,1152,256]{2,1,0:T(8,128)(2,1)} custom-call(s32[2]{0:T(128)S(1)} %pad_add_fusion.first_ref, bf16[1152,896]{1,0:T(8,128)(2,1)S(1)} %reshape.63.rows_ref, bf16[2048,896]{1,0:T(8,128)(2,1)} %bitcast.66, f32[32,2,40]{2,1,0:T(2,128)} %shard_map.123.refs_0_), custom_call_target="tpu_custom_call" | custom-call | flops 2113929216 | bytes 6300000 | tf_op jit(solution)/shard_map/pallas_call | solution.py:118
  136.8 9.4 %all-to-all-start.1 = ((f32[32,2,40]{2,1,0:T(2,128)}), f32[32,2,40]{2,1,0:T(2,128)S(1)}, u32[]{:S(2)}, u32[]{:S(2)}) async-start(f32[32,2,40]{2,1,0:T(2,128)} %shard_map.123.refs_0_), calls=%async_computation.1 | async-start | bytes 65536 | tf_op jit(solution)/shard_map/all_to_all | solution.py:188
  146.2 5.1 %shard_map.125.refs_0_ = bf16[4,1152,256]{2,1,0:T(8,128)(2,1)S(1)} custom-call(s32[2]{0:T(128)S(1)} %pad_add_fusion.1.first_ref, bf16[1152,896]{1,0:T(8,128)(2,1)S(1)} %reshape.63.rows_ref, bf16[2048,896]{1,0:T(8,128)(2,1)} %bitcast.67, bf16[4,1152,256]{2,1,0:T(8,128)(2,1)} %shard_map.124.refs_0_), custom_call_target="tpu_custom_call" | custom-call | flops 2113929216 | bytes 6300000 | tf_op jit(solution)/shard_map/pallas_call | solution.py:118
  151.3 1.4 copy-done
  152.7 3.3 %all-to-all-done.1 = f32[32,2,40]{2,1,0:T(2,128)S(1)} async-done(((f32[32,2,40]{2,1,0:T(2,128)}), f32[32,2,40]{2,1,0:T(2,128)S(1)}, u32[]{:S(2)}, u32[]{:S(2)}) %all-to-all-start.1) | async-done | bytes 10272 | tf_op jit(solution)/shard_map/all_to_all | solution.py:188
  157.1 1.7 copy-done.1
  159.4 4.8 %all-to-all-start.2 = ((f32[8,32,128]{2,1,0:T(8,128)}), f32[8,32,128]{2,1,0:T(8,128)S(1)}, u32[]{:S(2)}, u32[]{:S(2)}) async-start(f32[8,32,128]{2,1,0:T(8,128)} %broadcast_in_dim.73), calls=%async_computation.2 | async-start | bytes 262144 | tf_op jit(solution)/shard_map/all_to_all | solution.py:188
  164.2 10.6 %shard_map.126.refs_0_ = bf16[1,2048,896]{2,1,0:T(8,128)(2,1)} custom-call(bf16[8,1152,256]{2,1,0:T(8,128)(2,1)} %bitcast.82, bf16[1152,896]{1,0:T(8,128)(2,1)S(1)} %reshape.63.rows_ref, f32[1152,1]{1,0:T(8,128)S(1)} %reshape.73.gate_ref), custom_call_target="tpu_custom_call" | custom-call | flops 4227858432 | bytes 12500000 | tf_op jit(solution)/shard_map/pallas_call | solution.py:169
  174.9 2.2 add_convert_fusion.refs_1_
  177.1 2.0 copy-done.4
  180.1 2.0 copy-done.11
  182.1 1.0 copy-done.13
  183.2 7.1 %shard_map.131.refs_0_ = bf16[288,896]{1,0:T(8,128)(2,1)} custom-call(f32[8,288,288]{2,1,0:T(8,128)S(1)} %bitcast.74, bf16[288,896]{1,0:T(8,128)(2,1)S(1)} %copy-done.13, f32[32,896]{1,0:T(8,128)S(1)} %fusion.12.after_ref), custom_call_target="tpu_custom_call" | custom-call | flops 3000000000 | bytes 3600000 | tf_op jit(solution)/shard_map/pallas_call | solution.py:320
  190.9 2.2 collective-permute-start.20
  193.1 1.1 slice_bitcast_fusion.2
  194.2 1.3 convolution_convert_fusion
  196.2 6.4 %all-to-all-start.3 = ((f32[32,1,896]{2,1,0:T(1,128)}), f32[32,1,896]{2,1,0:T(1,128)}, u32[]{:S(2)}, u32[]{:S(2)}) async-start(f32[32,1,896]{2,1,0:T(1,128)} %reshape.67), calls=%async_computation.3 | async-start | bytes 229376 | tf_op jit(solution)/shard_map/all_to_all | solution.py:188
  202.7 2.0 collective-permute-start.8
  204.7 3.3 %collective-permute-start.9 = (bf16[1152,256]{1,0:T(8,128)(2,1)S(1)}, bf16[1152,256]{1,0:T(8,128)(2,1)S(1)}, u32[]{:S(2)}, u32[]{:S(2)}) collective-permute-start(bf16[1152,256]{1,0:T(8,128)(2,1)S(1)} %get-tuple-element.28), channel_id=1, source_target_pairs={{0,128},{64,192},{128,0},{192,64},{1,129},{65,193},{129,1},{193,65... | collective-permute-start | bytes 1769480 | tf_op jit(solution)/shard_map/ppermute | solution.py:199
  208.2 1.1 bitcast_dynamic-update-slice_fusion.3
  209.3 8.6 %collective-permute-done.19 = bf16[288,896]{1,0:T(8,128)(2,1)} collective-permute-done((bf16[288,896]{1,0:T(8,128)(2,1)}, bf16[288,896]{1,0:T(8,128)(2,1)}, u32[]{:S(2)}, u32[]{:S(2)}) %collective-permute-start.19) | collective-permute-done | bytes 516128 | tf_op jit(solution)/shard_map/ppermute | solution.py:199
  217.8 1.1 bitcast_dynamic-update-slice_fusion.2
  219.0 1.1 bitcast_dynamic-update-slice_fusion.1
  220.4 1.0 copy-done.14
  221.4 9.6 %collective-permute-done.9 = bf16[1152,256]{1,0:T(8,128)(2,1)S(1)} collective-permute-done((bf16[1152,256]{1,0:T(8,128)(2,1)S(1)}, bf16[1152,256]{1,0:T(8,128)(2,1)S(1)}, u32[]{:S(2)}, u32[]{:S(2)}) %collective-permute-start.9) | collective-permute-done | bytes 589856 | tf_op jit(solution)/shard_map/ppermute | solution.py:199
  231.0 1.2 multiply_convert_fusion
  232.1 0.9 shard_map.132
  233.8 9.4 %all-to-all-start.4 = ((f32[32,1,896]{2,1,0:T(1,128)}), f32[32,1,896]{2,1,0:T(1,128)S(1)}, u32[]{:S(2)}, u32[]{:S(2)}) async-start(f32[32,1,896]{2,1,0:T(1,128)} %broadcast_in_dim.75), calls=%async_computation.5 | async-start | bytes 229376 | tf_op jit(solution)/shard_map/all_to_all | solution.py:188
  243.3 1.9 bitcast_dynamic-update-slice_fusion
  245.1 8.5 %all-to-all-done.4 = f32[32,1,896]{2,1,0:T(1,128)S(1)} async-done(((f32[32,1,896]{2,1,0:T(1,128)}), f32[32,1,896]{2,1,0:T(1,128)S(1)}, u32[]{:S(2)}, u32[]{:S(2)}) %all-to-all-start.4) | async-done | bytes 114720 | tf_op jit(solution)/shard_map/all_to_all | solution.py:188
  (92 shorter events, 14.4 us)
Async XLA Ops:
  8.0 3.2 %copy-start.10 = (s32[128,8]{0,1:T(8,128)S(1)}, s32[128,8]{0,1:T(8,128)}, u32[]{:S(2)}) copy-start(s32[128,8]{0,1:T(8,128)} %param.11) | copy-start | bytes 12292
  8.0 3.2 %copy-start.9 = (f32[896,32]{0,1:T(8,128)S(1)}, f32[896,32]{0,1:T(8,128)}, u32[]{:S(2)}) copy-start(f32[896,32]{0,1:T(8,128)} %param.10) | copy-start | bytes 344068
  8.0 3.2 %copy-start.6 = (bf16[128,896]{1,0:T(8,128)(2,1)S(1)}, bf16[128,896]{1,0:T(8,128)(2,1)}, u32[]{:S(2)}) copy-start(bf16[128,896]{1,0:T(8,128)(2,1)} %input_ref.1) | copy-start | bytes 688132
  8.0 15.1 %copy-start.7 = (bf16[1,32,36,256]{3,1,2,0:T(8,128)(2,1)S(1)}, bf16[1,32,36,256]{3,1,2,0:T(8,128)(2,1)}, u32[]{:S(2)}) copy-start(bf16[1,32,36,256]{3,1,2,0:T(8,128)(2,1)} %param.13) | copy-start | bytes 1769476
  8.0 47.2 %all-gather.9.cloned.1.call-start = ((), (), s32[]{:S(2)}) async-start(), calls=%async_computation.8 | async-start | bytes 2322432 | tf_op jit(solution)/shard_map/all_gather | solution.py:405
  10.6 53.1 %reduce-scatter.2.cloned.1.call-start = ((), (), s32[]{:S(2)}) async-start(), calls=%async_computation.6 | async-start | bytes 2580480 | tf_op jit(solution)/shard_map/reduce_scatter | solution.py:292
  11.1 95.8 %all-gather.7.cloned.1.call-start = ((), (), s32[]{:S(2)}) async-start(), calls=%async_computation.7 | async-start | bytes 5308416 | tf_op jit(solution)/shard_map/all_gather | solution.py:420
  11.5 7.4 %collective-permute-start = (f32[32,128]{1,0:T(8,128)S(1)}, f32[32,128]{1,0:T(8,128)S(1)}, u32[]{:S(2)}, u32[]{:S(2)}) collective-permute-start(f32[32,128]{1,0:T(8,128)S(1)} %get-tuple-element.14), channel_id=1, source_target_pairs={{0,32},{32,64},{64,96},{96,128},{128,160},{160,192},{192,224},{224... | collective-permute-start | bytes 49160 | tf_op jit(solution)/shard_map/ppermute | solution.py:199
  11.6 7.8 %collective-permute-start.1 = (f32[32,128]{1,0:T(8,128)S(1)}, f32[32,128]{1,0:T(8,128)S(1)}, u32[]{:S(2)}, u32[]{:S(2)}) collective-permute-start(f32[32,128]{1,0:T(8,128)S(1)} %get-tuple-element.14), channel_id=1, source_target_pairs={{0,64},{32,96},{64,128},{96,160},{128,192},{160,224},{192,0},{224,... | collective-permute-start | bytes 49160 | tf_op jit(solution)/shard_map/ppermute | solution.py:199
  13.1 7.2 %collective-permute-start.2 = (f32[32,128]{1,0:T(8,128)S(1)}, f32[32,128]{1,0:T(8,128)S(1)}, u32[]{:S(2)}, u32[]{:S(2)}) collective-permute-start(f32[32,128]{1,0:T(8,128)S(1)} %get-tuple-element.14), channel_id=1, source_target_pairs={{0,96},{32,128},{64,160},{96,192},{128,224},{160,0},{192,32},{224,... | collective-permute-start | bytes 49160 | tf_op jit(solution)/shard_map/ppermute | solution.py:199
  15.9 5.3 %collective-permute-start.3 = (f32[32,128]{1,0:T(8,128)S(1)}, f32[32,128]{1,0:T(8,128)S(1)}, u32[]{:S(2)}, u32[]{:S(2)}) collective-permute-start(f32[32,128]{1,0:T(8,128)S(1)} %get-tuple-element.14), channel_id=1, source_target_pairs={{0,128},{32,160},{64,192},{96,224},{128,0},{160,32},{192,64},{224,... | collective-permute-start | bytes 49160 | tf_op jit(solution)/shard_map/ppermute | solution.py:199
  16.6 4.6 %collective-permute-start.4 = (f32[32,128]{1,0:T(8,128)S(1)}, f32[32,128]{1,0:T(8,128)S(1)}, u32[]{:S(2)}, u32[]{:S(2)}) collective-permute-start(f32[32,128]{1,0:T(8,128)S(1)} %get-tuple-element.14), channel_id=1, source_target_pairs={{0,160},{32,192},{64,224},{96,0},{128,32},{160,64},{192,96},{224,1... | collective-permute-start | bytes 49160 | tf_op jit(solution)/shard_map/ppermute | solution.py:199
  19.0 3.7 %collective-permute-start.5 = (f32[32,128]{1,0:T(8,128)S(1)}, f32[32,128]{1,0:T(8,128)S(1)}, u32[]{:S(2)}, u32[]{:S(2)}) collective-permute-start(f32[32,128]{1,0:T(8,128)S(1)} %get-tuple-element.14), channel_id=1, source_target_pairs={{0,192},{32,224},{64,0},{96,32},{128,64},{160,96},{192,128},{224,1... | collective-permute-start | bytes 49160 | tf_op jit(solution)/shard_map/ppermute | solution.py:199
  19.4 3.3 %collective-permute-start.6 = (f32[32,128]{1,0:T(8,128)S(1)}, f32[32,128]{1,0:T(8,128)S(1)}, u32[]{:S(2)}, u32[]{:S(2)}) collective-permute-start(f32[32,128]{1,0:T(8,128)S(1)} %get-tuple-element.14), channel_id=1, source_target_pairs={{0,224},{32,0},{64,32},{96,64},{128,96},{160,128},{192,160},{224,1... | collective-permute-start | bytes 49160 | tf_op jit(solution)/shard_map/ppermute | solution.py:199
  55.3 1.6 copy-start.5
  59.1 59.9 %all-to-all-start = ((bf16[4,8,40,896]{3,2,1,0:T(8,128)(2,1)}), bf16[4,8,40,896]{3,2,1,0:T(8,128)(2,1)}, u32[]{:S(2)}, u32[]{:S(2)}) async-start(bf16[4,8,40,896]{3,2,1,0:T(8,128)(2,1)} %shard_map.122.refs_1_), calls=%async_computation | async-start | bytes 4587520 | tf_op jit(solution)/shard_map/all_to_all | solution.py:188
  63.6 116.5 %all-gather.11.cloned.1.call-start = ((), (), s32[]{:S(2)}) async-start(), calls=%async_computation.9 | async-start | bytes 3981312 | tf_op jit(solution)/shard_map/all_gather | solution.py:427
  63.7 1.0 copy-start.8
  65.5 10.1 %collective-permute-start.11 = (bf16[80,896]{1,0:T(8,128)(2,1)S(1)}, bf16[80,896]{1,0:T(8,128)(2,1)S(1)}, u32[]{:S(2)}, u32[]{:S(2)}) collective-permute-start(bf16[80,896]{1,0:T(8,128)(2,1)S(1)} %get-tuple-element.16), channel_id=1, source_target_pairs={{0,8},{4,12},{8,16},{12,20},{16,24},{20,28},{24,0},{28,4},{1,9},{5... | collective-permute-start | bytes 430088 | tf_op jit(solution)/shard_map/ppermute | solution.py:199
  66.9 10.2 %collective-permute-start.12 = (bf16[80,896]{1,0:T(8,128)(2,1)S(1)}, bf16[80,896]{1,0:T(8,128)(2,1)S(1)}, u32[]{:S(2)}, u32[]{:S(2)}) collective-permute-start(bf16[80,896]{1,0:T(8,128)(2,1)S(1)} %get-tuple-element.17), channel_id=1, source_target_pairs={{0,16},{4,20},{8,24},{12,28},{16,0},{20,4},{24,8},{28,12},{1,17},{... | collective-permute-start | bytes 430088 | tf_op jit(solution)/shard_map/ppermute | solution.py:199
  69.9 11.3 %collective-permute-start.13 = (bf16[80,896]{1,0:T(8,128)(2,1)S(1)}, bf16[80,896]{1,0:T(8,128)(2,1)S(1)}, u32[]{:S(2)}, u32[]{:S(2)}) collective-permute-start(bf16[80,896]{1,0:T(8,128)(2,1)S(1)} %get-tuple-element.18), channel_id=1, source_target_pairs={{0,24},{4,28},{8,0},{12,4},{16,8},{20,12},{24,16},{28,20},{1,25},{... | collective-permute-start | bytes 430088 | tf_op jit(solution)/shard_map/ppermute | solution.py:199
  81.3 4.4 %collective-permute-start.14 = (bf16[40,896]{1,0:T(8,128)(2,1)S(1)}, bf16[40,896]{1,0:T(8,128)(2,1)S(1)}, u32[]{:S(2)}, u32[]{:S(2)}) collective-permute-start(bf16[40,896]{1,0:T(8,128)(2,1)S(1)} %slice.64), channel_id=1, source_target_pairs={{0,4},{4,0},{8,12},{12,8},{16,20},{20,16},{24,28},{28,24},{1,5},{5... | collective-permute-start | bytes 215048 | tf_op jit(solution)/shard_map/ppermute | solution.py:204
  85.7 4.4 %collective-permute-start.15 = (bf16[40,896]{1,0:T(8,128)(2,1)S(1)}, bf16[40,896]{1,0:T(8,128)(2,1)S(1)}, u32[]{:S(2)}, u32[]{:S(2)}) collective-permute-start(bf16[40,896]{1,0:T(8,128)(2,1)S(1)} %fusion.7), channel_id=1, source_target_pairs={{0,4},{4,0},{8,12},{12,8},{16,20},{20,16},{24,28},{28,24},{1,5},{5... | collective-permute-start | bytes 215048 | tf_op jit(solution)/shard_map/ppermute | solution.py:204
  90.1 9.7 %collective-permute-start.16 = (bf16[80,896]{1,0:T(8,128)(2,1)S(1)}, bf16[80,896]{1,0:T(8,128)(2,1)S(1)}, u32[]{:S(2)}, u32[]{:S(2)}) collective-permute-start(bf16[80,896]{1,0:T(8,128)(2,1)S(1)} %pad_maximum_fusion.refs_0_), channel_id=1, source_target_pairs={{0,8},{4,12},{8,16},{12,20},{16,24},{20,28},{24,0},{28,4},{1,9},{5... | collective-permute-start | bytes 430088 | tf_op jit(solution)/shard_map/ppermute | solution.py:199
  92.1 11.8 %collective-permute-start.17 = (bf16[80,896]{1,0:T(8,128)(2,1)S(1)}, bf16[80,896]{1,0:T(8,128)(2,1)S(1)}, u32[]{:S(2)}, u32[]{:S(2)}) collective-permute-start(bf16[80,896]{1,0:T(8,128)(2,1)S(1)} %pad_maximum_fusion.refs_0_), channel_id=1, source_target_pairs={{0,16},{4,20},{8,24},{12,28},{16,0},{20,4},{24,8},{28,12},{1,17},{... | collective-permute-start | bytes 430088 | tf_op jit(solution)/shard_map/ppermute | solution.py:199
  95.3 9.3 %collective-permute-start.18 = (bf16[80,896]{1,0:T(8,128)(2,1)S(1)}, bf16[80,896]{1,0:T(8,128)(2,1)S(1)}, u32[]{:S(2)}, u32[]{:S(2)}) collective-permute-start(bf16[80,896]{1,0:T(8,128)(2,1)S(1)} %pad_maximum_fusion.refs_0_), channel_id=1, source_target_pairs={{0,24},{4,28},{8,0},{12,4},{16,8},{20,12},{24,16},{28,20},{1,25},{... | collective-permute-start | bytes 430088 | tf_op jit(solution)/shard_map/ppermute | solution.py:199
  106.1 0.8 copy-start.12
  107.0 2.0 copy-start.3
  136.7 38.1 %collective-permute-start.7 = (bf16[4,1152,256]{2,1,0:T(8,128)(2,1)}, bf16[4,1152,256]{2,1,0:T(8,128)(2,1)}, u32[]{:S(2)}, u32[]{:S(2)}) collective-permute-start(bf16[4,1152,256]{2,1,0:T(8,128)(2,1)} %shard_map.124.refs_0_), channel_id=1, source_target_pairs={{0,32},{32,0},{1,33},{33,1},{2,34},{34,2},{3,35},{35,3},{4,36},{36... | collective-permute-start | bytes 7077896 | tf_op jit(solution)/shard_map/ppermute | solution.py:440
  136.8 19.2 %all-to-all-start.1 = ((f32[32,2,40]{2,1,0:T(2,128)}), f32[32,2,40]{2,1,0:T(2,128)S(1)}, u32[]{:S(2)}, u32[]{:S(2)}) async-start(f32[32,2,40]{2,1,0:T(2,128)} %shard_map.123.refs_0_), calls=%async_computation.1 | async-start | bytes 65536 | tf_op jit(solution)/shard_map/all_to_all | solution.py:188
  151.3 1.4 copy-start
  157.1 1.7 copy-start.1
  159.4 17.7 %all-to-all-start.2 = ((f32[8,32,128]{2,1,0:T(8,128)}), f32[8,32,128]{2,1,0:T(8,128)S(1)}, u32[]{:S(2)}, u32[]{:S(2)}) async-start(f32[8,32,128]{2,1,0:T(8,128)} %broadcast_in_dim.73), calls=%async_computation.2 | async-start | bytes 262144 | tf_op jit(solution)/shard_map/all_to_all | solution.py:188
  164.2 10.6 %copy-start.2 = (bf16[4,1152,256]{2,1,0:T(8,128)(2,1)S(1)}, bf16[4,1152,256]{2,1,0:T(8,128)(2,1)}, u32[]{:S(2)}) copy-start(bf16[4,1152,256]{2,1,0:T(8,128)(2,1)} %copy-done) | copy-start | bytes 7077892
  177.1 2.0 copy-start.4
  179.1 0.7 copy-start.15
  180.1 2.0 copy-start.11
  182.1 1.0 copy-start.13
  190.3 27.6 %collective-permute-start.19 = (bf16[288,896]{1,0:T(8,128)(2,1)}, bf16[288,896]{1,0:T(8,128)(2,1)}, u32[]{:S(2)}, u32[]{:S(2)}) collective-permute-start(bf16[288,896]{1,0:T(8,128)(2,1)} %shard_map.131.refs_0_), channel_id=1, source_target_pairs={{0,1},{1,2},{2,3},{3,0},{4,5},{5,6},{6,7},{7,4},{8,9},{9,10},{10,1... | collective-permute-start | bytes 1548296 | tf_op jit(solution)/shard_map/ppermute | solution.py:199
  190.9 28.1 %collective-permute-start.20 = (bf16[288,896]{1,0:T(8,128)(2,1)}, bf16[288,896]{1,0:T(8,128)(2,1)}, u32[]{:S(2)}, u32[]{:S(2)}) collective-permute-start(bf16[288,896]{1,0:T(8,128)(2,1)} %shard_map.131.refs_0_), channel_id=1, source_target_pairs={{0,2},{1,3},{2,0},{3,1},{4,6},{5,7},{6,4},{7,5},{8,10},{9,11},{10,... | collective-permute-start | bytes 1548296 | tf_op jit(solution)/shard_map/ppermute | solution.py:199
  196.2 35.9 %all-to-all-start.3 = ((f32[32,1,896]{2,1,0:T(1,128)}), f32[32,1,896]{2,1,0:T(1,128)}, u32[]{:S(2)}, u32[]{:S(2)}) async-start(f32[32,1,896]{2,1,0:T(1,128)} %reshape.67), calls=%async_computation.3 | async-start | bytes 229376 | tf_op jit(solution)/shard_map/all_to_all | solution.py:188
  202.6 17.5 %collective-permute-start.10 = (bf16[1152,256]{1,0:T(8,128)(2,1)}, bf16[1152,256]{1,0:T(8,128)(2,1)S(1)}, u32[]{:S(2)}, u32[]{:S(2)}) collective-permute-start(bf16[1152,256]{1,0:T(8,128)(2,1)} %get-tuple-element.27), channel_id=1, source_target_pairs={{0,192},{64,0},{128,64},{192,128},{1,193},{65,1},{129,65},{193,129... | collective-permute-start | bytes 1769480 | tf_op jit(solution)/shard_map/ppermute | solution.py:199
  202.7 17.7 %collective-permute-start.8 = (bf16[1152,256]{1,0:T(8,128)(2,1)}, bf16[1152,256]{1,0:T(8,128)(2,1)S(1)}, u32[]{:S(2)}, u32[]{:S(2)}) collective-permute-start(bf16[1152,256]{1,0:T(8,128)(2,1)} %get-tuple-element.26), channel_id=1, source_target_pairs={{0,64},{64,128},{128,192},{192,0},{1,65},{65,129},{129,193},{193,1... | collective-permute-start | bytes 1769480 | tf_op jit(solution)/shard_map/ppermute | solution.py:199
  204.7 26.3 %collective-permute-start.9 = (bf16[1152,256]{1,0:T(8,128)(2,1)S(1)}, bf16[1152,256]{1,0:T(8,128)(2,1)S(1)}, u32[]{:S(2)}, u32[]{:S(2)}) collective-permute-start(bf16[1152,256]{1,0:T(8,128)(2,1)S(1)} %get-tuple-element.28), channel_id=1, source_target_pairs={{0,128},{64,192},{128,0},{192,64},{1,129},{65,193},{129,1},{193,65... | collective-permute-start | bytes 1769480 | tf_op jit(solution)/shard_map/ppermute | solution.py:199
  217.8 25.4 %collective-permute-start.21 = (bf16[288,896]{1,0:T(8,128)(2,1)}, bf16[288,896]{1,0:T(8,128)(2,1)}, u32[]{:S(2)}, u32[]{:S(2)}) collective-permute-start(bf16[288,896]{1,0:T(8,128)(2,1)} %shard_map.131.refs_0_), channel_id=1, source_target_pairs={{0,3},{1,0},{2,1},{3,2},{4,7},{5,4},{6,5},{7,6},{8,11},{9,8},{10,9... | collective-permute-start | bytes 1548296 | tf_op jit(solution)/shard_map/ppermute | solution.py:199
  220.1 1.3 copy-start.14
  233.8 19.8 %all-to-all-start.4 = ((f32[32,1,896]{2,1,0:T(1,128)}), f32[32,1,896]{2,1,0:T(1,128)S(1)}, u32[]{:S(2)}, u32[]{:S(2)}) async-start(f32[32,1,896]{2,1,0:T(1,128)} %broadcast_in_dim.75), calls=%async_computation.5 | async-start | bytes 229376 | tf_op jit(solution)/shard_map/all_to_all | solution.py:188
Sparse Core Ops, SparseCore 0:
  11.2 43.9 all-gather.8
  57.7 34.5 all-gather.6
  107.1 34.1 all-gather.10
Sparse Core Ops, SparseCore 1:
  13.6 34.8 reduce-scatter.1

commit v4 on v1

--- a/solution.py
+++ b/solution.py
@@ -212,8 +212,14 @@
         outs[k][...] = rows[2 * k * BLOCK : 2 * (k + 1) * BLOCK].astype(bf16)
 
 
+def pair_kernel(*refs):
+    total = total_of([part[...] for part in refs[:4]])
+    refs[5][...] = total[:BLOCK]
+    refs[6][...] = total[BLOCK:].astype(bf16)
+
+
 def gram_kernel(z_ref, *refs):
-    parts, whole_ref, gram_ref = refs[:4], refs[6], refs[7]
+    parts, whole_ref, gram_ref = refs[:4], refs[5], refs[6]
     rows = jnp.concatenate([part[...].astype(f32) for part in parts], axis=0).astype(bf16)
     row = lax.broadcasted_iota(jnp.int32, (LATENT, PADDED), 0)
     column = lax.broadcasted_iota(jnp.int32, (LATENT, PADDED), 1)
@@ -226,7 +232,7 @@
     whole_ref[...] = whole
     gram_ref[...] = lax.dot_general(
         whole, whole, (((1,), (1,)), ((), ())), preferred_element_type=f32
-    )
+    ).astype(bf16)
 
 
 def newton_kernel(grams_ref, whole_ref, after_ref, out_ref):
@@ -275,20 +281,34 @@
     )(lax.axis_index("z")[None], part, after)
 
 
-def muon_gram(row_block, first, second):
+def pair_sums(parts, after):
+    width = parts[0].shape[1]
+    return pl.pallas_call(
+        pair_kernel,
+        in_specs=[WHOLE] * 4 + [AFTER],
+        out_specs=[WHOLE] * 2,
+        out_shape=[
+            jax.ShapeDtypeStruct((BLOCK, width), f32),
+            jax.ShapeDtypeStruct((BLOCK, width), bf16),
+        ],
+        compiler_params=PARAMS,
+    )(*parts, after)
+
+
+def muon_gram(row_block, after):
     pair = jnp.concatenate([row_block, to_neighbour(row_block)], axis=0)
     gathered = swap([pair] * 4, "z", 8, 2)
     return pl.pallas_call(
         gram_kernel,
-        in_specs=[SMEM] + [WHOLE] * 4 + [AFTER] * 2,
+        in_specs=[SMEM] + [WHOLE] * 4 + [AFTER],
         out_specs=[WHOLE] * 2,
         out_shape=[
             jax.ShapeDtypeStruct((LATENT, D // 8), bf16),
-            jax.ShapeDtypeStruct((LATENT, LATENT), f32),
+            jax.ShapeDtypeStruct((LATENT, LATENT), bf16),
         ],
         compiler_params=PARAMS,
         cost_estimate=pl.CostEstimate(flops=300_000_000, bytes_accessed=1_600_000, transcendentals=0),
-    )(lax.axis_index("z")[None], *gathered, first, second)
+    )(lax.axis_index("z")[None], *gathered, after)
 
 
 def muon_update_of(whole, grams, after):
@@ -390,9 +410,8 @@
     slot_gates = jnp.sum(jnp.where(matches, gates[:, None, :], 0.0), axis=2)
     back = hidden_times_down(hidden, down)
     blocks = muon_blocks(attention_grads[0], slot_gates)
-    pair_sum = total_of(swap(blocks, "z", 8, 2))
-    for_next = to_neighbour(pair_sum[BLOCK:].astype(bf16))
-    row_block = (pair_sum[:BLOCK] + for_next.astype(f32)).astype(bf16)
+    own_sum, next_sum = pair_sums(swap(blocks, "z", 8, 2), back)
+    row_block = (own_sum + to_neighbour(next_sum).astype(f32)).astype(bf16)
     ready = (blocks[0][0, 0] < f32(jnp.inf)) & (back[0, 0] < f32(jnp.inf))
     keep = jnp.where(ready, 1.0, 0.0).astype(bf16)
     rows = jnp.swapaxes(rows_got[:, :CAP] * keep, 0, 1).reshape(count, width)
@@ -408,11 +427,11 @@
     for_other = upstream_partial(rows, down, x_at, 1 - core_at, joined)
     from_other = lax.ppermute(for_other, "c", [(0, 1), (1, 0)])
     for_own = upstream_partial(rows, down, x_at, core_at, for_other)
-    whole, gram = muon_gram(row_block, both_got, for_own)
+    whole, gram = muon_gram(row_block, joined)
     grams = lax.all_gather(gram, FS, axis=0, tiled=False)
     both_cores = (from_other.astype(f32) + for_own.astype(f32)).astype(bf16)
     upstream = total_of(swap([both_cores[k] for k in range(4)], "x", 4))
-    back_parts = spread(hand(back_part, gram), FS, 8)
+    back_parts = spread(hand(back_part, for_own), FS, 8)
     gate_back = add_up(back_parts, grad_down)
 
     grad_hidden = (gate_column * upstream).astype(bf16)

time: 246 us -> 254 us (1.033)
  the two profiles are of different devices: /device:TPU:9 before, /device:TPU:38 now
where the time goes in v4:
time: 254 us; the launch traced here: 253 us
  starting transfers between devices  79.5 us (31%)
  waiting for transfers between devices  78.9 us (31%)
  Pallas kernels  43.1 us (17%)
  local copies, waits for them, and re-layouts  24.3 us (10%)
  between operations  17.3 us (7%)
  other arithmetic  8.27 us (3%)
    all_to_all x5, starting transfers between devices, exchange(): return lax.all_to_all(value, axes, split_axis=0, concat_axis=0, tiled=True)  46.5 us
    ppermute x19, starting transfers between devices, swap(): got.append(lax.ppermute(pieces[k], axes, pairs))  28.9 us
    reduce_scatter x1, waiting for transfers between devices, muon_blocks(): part = lax.psum_scatter(attention, 'y', scatter_dimension=0, tiled=True)[0]  27.6 us
    all_gather x1, waiting for transfers between devices, on_device(): grams = lax.all_gather(gram, FS, axis=0, tiled=False)  22.9 us
    unnamed x37, local copies, waits for them, and re-layouts  16.6 us
    ppermute x19, waiting for transfers between devices, swap(): got.append(lax.ppermute(pieces[k], axes, pairs))  14.2 us
    all_to_all x5, waiting for transfers between devices, exchange(): return lax.all_to_all(value, axes, split_axis=0, concat_axis=0, tiled=True)  13 us
    pallas_call x2, Pallas kernels, upstream_partial(): pl.pallas_call(upstream_kernel, grid_spec=grid_spec, out_shape=jax.ShapeD...  11.2 us
  transfers between devices with their start and end apart: 30, of which 8 were waited for; matrix products, arithmetic and copies ran while one was open for 6% of the time, Pallas kernels for 14%

profile of v4, /device:TPU:38, one launch (start us, length us, event | category | flops | bytes accessed | tf_op | source)
XLA Modules:
  0.0 252.8 jit_solution(4490926418400482113)
XLA Ops:
  8.1 0.7 reduce-scatter.2.cloned.1.call-update
  8.8 0.5 all-gather.4.cloned.1.call-update
  9.4 2.3 shard_map.119
  11.7 11.4 %all-to-all-start = ((bf16[32,40,896]{2,1,0:T(8,128)(2,1)}), bf16[32,40,896]{2,1,0:T(8,128)(2,1)}, u32[]{:S(2)}, u32[]{:S(2)}) async-start(bf16[32,40,896]{2,1,0:T(8,128)(2,1)} %get-tuple-element.18), calls=%async_computation | async-start | bytes 4587520 | tf_op jit(solution)/shard_map/all_to_all | solution.py:164
  23.1 0.9 collective-permute-start.5
  24.0 0.9 collective-permute-start.4
  24.9 2.4 collective-permute-start.3
  27.3 1.4 collective-permute-start.2
  28.8 1.0 collective-permute-start.1
  29.8 0.6 collective-permute-start
  30.5 1.8 collective-permute-done.2
  32.3 0.6 collective-permute-done.1
  33.0 0.4 collective-permute-done
  33.4 0.3 fusion.5.after_ref.first_ref
  33.7 27.6 %reduce-scatter.2.cloned.1.call-done = bf16[1,288,896]{2,1,0:T(8,128)(2,1)} async-done(((bf16[4,288,896]{2,1,0:T(8,128)(2,1)}), bf16[1,288,896]{2,1,0:T(8,128)(2,1)}) %reduce-scatter.2.cloned.1.call-update) | async-done | bytes 516112 | tf_op jit(solution)/shard_map/reduce_scatter | solution.py:273
  61.3 1.0 copy-done.10
  62.4 1.4 shard_map.121
  63.8 0.5 slice.28
  65.0 2.0 copy-done.5
  67.0 8.1 %shard_map.120.refs_4_ = f32[1152,896]{1,0:T(8,128)} custom-call(bf16[8,1152,256]{2,1,0:T(8,128)(2,1)} %all-gather.4.cloned.1.call-done.hidden_ref, bf16[2048,896]{1,0:T(8,128)(2,1)S(1)} %bitcast.69), custom_call_target="tpu_custom_call" | custom-call | flops 4227858432 | bytes 12500000 | tf_op jit(solution)/shard_map/pallas_call | solution.py:116
  75.1 1.2 slice.37
  77.0 1.9 fusion
  79.2 1.9 copy-done.3
  81.1 0.6 multiply_reduce_fusion
  81.8 0.6 shard_map.122.refs_0_.refs_4_
  82.5 6.1 %shard_map.123.refs_0_ = bf16[4,1152,256]{2,1,0:T(8,128)(2,1)} custom-call(s32[2]{0:T(128)S(1)} %pad_add_fusion.first_ref, bf16[1152,896]{1,0:T(8,128)(2,1)S(1)} %bitcast.64, bf16[2048,896]{1,0:T(8,128)(2,1)} %bitcast.67, f32[32,2,40]{2,1,0:T(2,128)} %shard_map.122.refs_0_.refs_4_), custom_call_target="tpu_custom_call" | custom-call | flops 2113929216 | bytes 6300000 | tf_op jit(solution)/shard_map/pallas_call | solution.py:94
  88.7 2.4 collective-permute-start.11
  91.0 4.6 %collective-permute-start.12 = (bf16[80,896]{1,0:T(8,128)(2,1)S(1)}, bf16[80,896]{1,0:T(8,128)(2,1)S(1)}, u32[]{:S(2)}, u32[]{:S(2)}) collective-permute-start(bf16[80,896]{1,0:T(8,128)(2,1)S(1)} %get-tuple-element.21), channel_id=1, source_target_pairs={{0,16},{4,20},{8,24},{12,28},{16,0},{20,4},{24,8},{28,12},{1,17},{... | collective-permute-start | bytes 430088 | tf_op jit(solution)/shard_map/ppermute | solution.py:175
  95.6 2.9 %collective-permute-start.13 = (bf16[80,896]{1,0:T(8,128)(2,1)S(1)}, bf16[80,896]{1,0:T(8,128)(2,1)S(1)}, u32[]{:S(2)}, u32[]{:S(2)}) collective-permute-start(bf16[80,896]{1,0:T(8,128)(2,1)S(1)} %get-tuple-element.22), channel_id=1, source_target_pairs={{0,24},{4,28},{8,0},{12,4},{16,8},{20,12},{24,16},{28,20},{1,25},{... | collective-permute-start | bytes 430088 | tf_op jit(solution)/shard_map/ppermute | solution.py:175
  98.6 8.3 %all-to-all-start.1 = ((f32[32,2,40]{2,1,0:T(2,128)}), f32[32,2,40]{2,1,0:T(2,128)S(1)}, u32[]{:S(2)}, u32[]{:S(2)}) async-start(f32[32,2,40]{2,1,0:T(2,128)} %shard_map.122.refs_0_.refs_4_), calls=%async_computation.2 | async-start | bytes 65536 | tf_op jit(solution)/shard_map/all_to_all | solution.py:164
  106.9 2.2 copy-done.4
  109.1 3.9 %collective-permute-start.14 = (bf16[40,896]{1,0:T(8,128)(2,1)S(1)}, bf16[40,896]{1,0:T(8,128)(2,1)S(1)}, u32[]{:S(2)}, u32[]{:S(2)}) collective-permute-start(bf16[40,896]{1,0:T(8,128)(2,1)S(1)} %get-tuple-element.24), channel_id=1, source_target_pairs={{0,4},{4,0},{8,12},{12,8},{16,20},{20,16},{24,28},{28,24},{1,5},{5... | collective-permute-start | bytes 215048 | tf_op jit(solution)/shard_map/ppermute | solution.py:180
  113.0 5.1 %shard_map.124.refs_0_ = bf16[4,1152,256]{2,1,0:T(8,128)(2,1)S(1)} custom-call(s32[2]{0:T(128)S(1)} %pad_add_fusion.1.first_ref, bf16[1152,896]{1,0:T(8,128)(2,1)S(1)} %bitcast.65, bf16[2048,896]{1,0:T(8,128)(2,1)} %bitcast.68, bf16[4,1152,256]{2,1,0:T(8,128)(2,1)} %shard_map.123.refs_0_), custom_call_target="tpu_custom_call" | custom-call | flops 2113929216 | bytes 6300000 | tf_op jit(solution)/shard_map/pallas_call | solution.py:94
  118.1 1.4 copy-done
  119.6 0.6 reshape.71.gate_ref
  120.6 1.7 copy-done.1
  122.3 0.7 broadcast_in_dim.72
  123.0 4.8 %all-to-all-start.2 = ((f32[8,32,128]{2,1,0:T(8,128)}), f32[8,32,128]{2,1,0:T(8,128)S(1)}, u32[]{:S(2)}, u32[]{:S(2)}) async-start(f32[8,32,128]{2,1,0:T(8,128)} %broadcast_in_dim.72), calls=%async_computation.3 | async-start | bytes 262144 | tf_op jit(solution)/shard_map/all_to_all | solution.py:164
  127.8 4.0 %collective-permute-start.18 = (bf16[80,896]{1,0:T(8,128)(2,1)S(1)}, bf16[80,896]{1,0:T(8,128)(2,1)S(1)}, u32[]{:S(2)}, u32[]{:S(2)}) collective-permute-start(bf16[80,896]{1,0:T(8,128)(2,1)S(1)} %pad_maximum_fusion.refs_0_), channel_id=1, source_target_pairs={{0,24},{4,28},{8,0},{12,4},{16,8},{20,12},{24,16},{28,20},{1,25},{... | collective-permute-start | bytes 430088 | tf_op jit(solution)/shard_map/ppermute | solution.py:175
  131.8 1.3 collective-permute-start.17
  133.1 2.8 %collective-permute-start.16 = (bf16[80,896]{1,0:T(8,128)(2,1)S(1)}, bf16[80,896]{1,0:T(8,128)(2,1)}, u32[]{:S(2)}, u32[]{:S(2)}) collective-permute-start(bf16[80,896]{1,0:T(8,128)(2,1)S(1)} %pad_maximum_fusion.refs_0_), channel_id=1, source_target_pairs={{0,8},{4,12},{8,16},{12,20},{16,24},{20,28},{24,0},{28,4},{1,9},{5... | collective-permute-start | bytes 430088 | tf_op jit(solution)/shard_map/ppermute | solution.py:175
  135.9 10.5 %shard_map.125.refs_0_ = bf16[1,2048,896]{2,1,0:T(8,128)(2,1)} custom-call(bf16[8,1152,256]{2,1,0:T(8,128)(2,1)} %all-gather.4.cloned.1.call-done.hidden_ref, bf16[1152,896]{1,0:T(8,128)(2,1)S(1)} %bitcast.66, f32[1152,1]{1,0:T(8,128)S(1)} %reshape.71.gate_ref), custom_call_target="tpu_custom_call" | custom-call | flops 4227858432 | bytes 12500000 | tf_op jit(solution)/shard_map/pallas_call | solution.py:145
  146.4 2.2 copy-done.6
  148.6 2.4 shard_map.129
  151.1 0.8 copy-done.13
  151.9 1.3 convolution_convert_fusion
  153.2 2.2 add_convert_fusion
  155.4 1.2 slice_bitcast_fusion.2
  156.7 0.4 collective-permute-start.8
  157.0 1.7 collective-permute-start.10
  158.7 1.5 collective-permute-start.9
  160.4 0.7 reshape.67
  161.1 9.9 %all-to-all-start.3 = ((f32[32,1,896]{2,1,0:T(1,128)}), f32[32,1,896]{2,1,0:T(1,128)S(1)}, u32[]{:S(2)}, u32[]{:S(2)}) async-start(f32[32,1,896]{2,1,0:T(1,128)} %reshape.67), calls=%async_computation.4 | async-start | bytes 229376 | tf_op jit(solution)/shard_map/all_to_all | solution.py:164
  171.1 22.9 %all-gather.6.cloned.1.call-done = bf16[2304,288]{1,0:T(8,128)(2,1)} async-done(((bf16[288,288]{1,0:T(8,128)(2,1)}), bf16[2304,288]{1,0:T(8,128)(2,1)}) %all-gather.6.cloned.1.call-update) | async-done | bytes 1327120 | tf_op jit(solution)/shard_map/all_gather | solution.py:431
  194.0 1.5 copy-done.9
  195.5 6.4 %shard_map.130.refs_0_ = bf16[288,896]{1,0:T(8,128)(2,1)S(1)} custom-call(bf16[8,288,288]{2,1,0:T(8,128)(2,1)S(1)} %bitcast.71, bf16[288,896]{1,0:T(8,128)(2,1)S(1)} %copy-done.14, f32[32,896]{1,0:T(8,128)S(1)} %fusion.10.after_ref), custom_call_target="tpu_custom_call" | custom-call | flops 3000000000 | bytes 3600000 | tf_op jit(solution)/shard_map/pallas_call | solution.py:315
  202.1 0.7 broadcast_in_dim.74
  202.8 12.1 %all-to-all-start.4 = ((f32[32,1,896]{2,1,0:T(1,128)}), f32[32,1,896]{2,1,0:T(1,128)S(1)}, u32[]{:S(2)}, u32[]{:S(2)}) async-start(f32[32,1,896]{2,1,0:T(1,128)} %broadcast_in_dim.74), calls=%async_computation.5 | async-start | bytes 229376 | tf_op jit(solution)/shard_map/all_to_all | solution.py:164
  215.2 12.9 %all-to-all-done.4 = f32[32,1,896]{2,1,0:T(1,128)S(1)} async-done(((f32[32,1,896]{2,1,0:T(1,128)}), f32[32,1,896]{2,1,0:T(1,128)S(1)}, u32[]{:S(2)}, u32[]{:S(2)}) %all-to-all-start.4) | async-done | bytes 114720 | tf_op jit(solution)/shard_map/all_to_all | solution.py:164
  228.1 0.7 copy.32
  228.8 2.7 %fusion.4 = bf16[1152,256]{1,0:T(8,128)(2,1)} fusion(bf16[1152,256]{1,0:T(8,128)(2,1)} %collective-permute-done.10, bf16[1152,256]{1,0:T(8,128)(2,1)} %collective-permute-done.9, bf16[1152,256]{1,0:T(8,128)(2,1)} %collective-permute-done.8, bf16[4,1152,256]{2,1,0:T(8,128)(2,1)} %copy-done.15, f32[1152]{0:T(1024)S(1)} %mul.61), kind=kLoop, calls=%fused_computation.9 | loop fusion | flops 2654208 | bytes 2953728 | tf_op jit(solution)/shard_map/convert_element_type | solution.py:437
  231.5 11.3 %collective-permute-done.19 = bf16[288,896]{1,0:T(8,128)(2,1)S(1)} collective-permute-done((bf16[288,896]{1,0:T(8,128)(2,1)S(1)}, bf16[288,896]{1,0:T(8,128)(2,1)S(1)}, u32[]{:S(2)}, u32[]{:S(2)}) %collective-permute-start.19) | collective-permute-done | bytes 516128 | tf_op jit(solution)/shard_map/ppermute | solution.py:175
  242.9 1.1 bitcast_dynamic-update-slice_fusion.1
  244.1 1.3 copy-done.16
  (88 shorter events, 2.5 us)
Async XLA Ops:
  8.0 1.4 copy-start.7
  8.0 1.4 copy-start.8
  8.0 1.4 copy-start.12
  8.0 1.4 copy-start.11
  8.0 53.3 %reduce-scatter.2.cloned.1.call-start = ((), (), s32[]{:S(2)}) async-start(), calls=%async_computation.7 | async-start | bytes 2580480 | tf_op jit(solution)/shard_map/reduce_scatter | solution.py:273
  8.8 56.2 %all-gather.4.cloned.1.call-start = ((), (), s32[]{:S(2)}) async-start(), calls=%async_computation.6 | async-start | bytes 5308416 | tf_op jit(solution)/shard_map/all_gather | solution.py:400
  11.7 65.3 %all-to-all-start = ((bf16[32,40,896]{2,1,0:T(8,128)(2,1)}), bf16[32,40,896]{2,1,0:T(8,128)(2,1)}, u32[]{:S(2)}, u32[]{:S(2)}) async-start(bf16[32,40,896]{2,1,0:T(8,128)(2,1)} %get-tuple-element.18), calls=%async_computation | async-start | bytes 4587520 | tf_op jit(solution)/shard_map/all_to_all | solution.py:164
  23.1 5.7 %collective-permute-start.6 = (f32[32,128]{1,0:T(8,128)S(1)}, f32[32,128]{1,0:T(8,128)S(1)}, u32[]{:S(2)}, u32[]{:S(2)}) collective-permute-start(f32[32,128]{1,0:T(8,128)S(1)} %get-tuple-element.17), channel_id=1, source_target_pairs={{0,224},{32,0},{64,32},{96,64},{128,96},{160,128},{192,160},{224,1... | collective-permute-start | bytes 49160 | tf_op jit(solution)/shard_map/ppermute | solution.py:175
  23.1 6.7 %collective-permute-start.5 = (f32[32,128]{1,0:T(8,128)S(1)}, f32[32,128]{1,0:T(8,128)S(1)}, u32[]{:S(2)}, u32[]{:S(2)}) collective-permute-start(f32[32,128]{1,0:T(8,128)S(1)} %get-tuple-element.17), channel_id=1, source_target_pairs={{0,192},{32,224},{64,0},{96,32},{128,64},{160,96},{192,128},{224,1... | collective-permute-start | bytes 49160 | tf_op jit(solution)/shard_map/ppermute | solution.py:175
  24.0 6.4 %collective-permute-start.4 = (f32[32,128]{1,0:T(8,128)S(1)}, f32[32,128]{1,0:T(8,128)S(1)}, u32[]{:S(2)}, u32[]{:S(2)}) collective-permute-start(f32[32,128]{1,0:T(8,128)S(1)} %get-tuple-element.17), channel_id=1, source_target_pairs={{0,160},{32,192},{64,224},{96,0},{128,32},{160,64},{192,96},{224,1... | collective-permute-start | bytes 49160 | tf_op jit(solution)/shard_map/ppermute | solution.py:175
  24.9 5.6 %collective-permute-start.3 = (f32[32,128]{1,0:T(8,128)S(1)}, f32[32,128]{1,0:T(8,128)S(1)}, u32[]{:S(2)}, u32[]{:S(2)}) collective-permute-start(f32[32,128]{1,0:T(8,128)S(1)} %get-tuple-element.17), channel_id=1, source_target_pairs={{0,128},{32,160},{64,192},{96,224},{128,0},{160,32},{192,64},{224,... | collective-permute-start | bytes 49160 | tf_op jit(solution)/shard_map/ppermute | solution.py:175
  27.3 5.0 %collective-permute-start.2 = (f32[32,128]{1,0:T(8,128)S(1)}, f32[32,128]{1,0:T(8,128)S(1)}, u32[]{:S(2)}, u32[]{:S(2)}) collective-permute-start(f32[32,128]{1,0:T(8,128)S(1)} %get-tuple-element.17), channel_id=1, source_target_pairs={{0,96},{32,128},{64,160},{96,192},{128,224},{160,0},{192,32},{224,... | collective-permute-start | bytes 49160 | tf_op jit(solution)/shard_map/ppermute | solution.py:175
  28.8 4.2 %collective-permute-start.1 = (f32[32,128]{1,0:T(8,128)S(1)}, f32[32,128]{1,0:T(8,128)S(1)}, u32[]{:S(2)}, u32[]{:S(2)}) collective-permute-start(f32[32,128]{1,0:T(8,128)S(1)} %get-tuple-element.17), channel_id=1, source_target_pairs={{0,64},{32,96},{64,128},{96,160},{128,192},{160,224},{192,0},{224,... | collective-permute-start | bytes 49160 | tf_op jit(solution)/shard_map/ppermute | solution.py:175
  29.8 3.5 %collective-permute-start = (f32[32,128]{1,0:T(8,128)S(1)}, f32[32,128]{1,0:T(8,128)S(1)}, u32[]{:S(2)}, u32[]{:S(2)}) collective-permute-start(f32[32,128]{1,0:T(8,128)S(1)} %get-tuple-element.17), channel_id=1, source_target_pairs={{0,32},{32,64},{64,96},{96,128},{128,160},{160,192},{192,224},{224... | collective-permute-start | bytes 49160 | tf_op jit(solution)/shard_map/ppermute | solution.py:175
  61.3 1.0 copy-start.10
  65.0 2.0 copy-start.5
  78.9 2.2 copy-start.3
  88.6 64.6 %collective-permute-start.7 = (bf16[4,1152,256]{2,1,0:T(8,128)(2,1)}, bf16[4,1152,256]{2,1,0:T(8,128)(2,1)}, u32[]{:S(2)}, u32[]{:S(2)}) collective-permute-start(bf16[4,1152,256]{2,1,0:T(8,128)(2,1)} %shard_map.123.refs_0_), channel_id=1, source_target_pairs={{0,32},{32,0},{1,33},{33,1},{2,34},{34,2},{3,35},{35,3},{4,36},{36... | collective-permute-start | bytes 7077896 | tf_op jit(solution)/shard_map/ppermute | solution.py:428
  88.7 18.2 %collective-permute-start.11 = (bf16[80,896]{1,0:T(8,128)(2,1)}, bf16[80,896]{1,0:T(8,128)(2,1)S(1)}, u32[]{:S(2)}, u32[]{:S(2)}) collective-permute-start(bf16[80,896]{1,0:T(8,128)(2,1)} %get-tuple-element.20), channel_id=1, source_target_pairs={{0,8},{4,12},{8,16},{12,20},{16,24},{20,28},{24,0},{28,4},{1,9},{5... | collective-permute-start | bytes 430088 | tf_op jit(solution)/shard_map/ppermute | solution.py:175
  91.0 15.8 %collective-permute-start.12 = (bf16[80,896]{1,0:T(8,128)(2,1)S(1)}, bf16[80,896]{1,0:T(8,128)(2,1)S(1)}, u32[]{:S(2)}, u32[]{:S(2)}) collective-permute-start(bf16[80,896]{1,0:T(8,128)(2,1)S(1)} %get-tuple-element.21), channel_id=1, source_target_pairs={{0,16},{4,20},{8,24},{12,28},{16,0},{20,4},{24,8},{28,12},{1,17},{... | collective-permute-start | bytes 430088 | tf_op jit(solution)/shard_map/ppermute | solution.py:175
  95.6 11.2 %collective-permute-start.13 = (bf16[80,896]{1,0:T(8,128)(2,1)S(1)}, bf16[80,896]{1,0:T(8,128)(2,1)S(1)}, u32[]{:S(2)}, u32[]{:S(2)}) collective-permute-start(bf16[80,896]{1,0:T(8,128)(2,1)S(1)} %get-tuple-element.22), channel_id=1, source_target_pairs={{0,24},{4,28},{8,0},{12,4},{16,8},{20,12},{24,16},{28,20},{1,25},{... | collective-permute-start | bytes 430088 | tf_op jit(solution)/shard_map/ppermute | solution.py:175
  98.6 20.9 %all-to-all-start.1 = ((f32[32,2,40]{2,1,0:T(2,128)}), f32[32,2,40]{2,1,0:T(2,128)S(1)}, u32[]{:S(2)}, u32[]{:S(2)}) async-start(f32[32,2,40]{2,1,0:T(2,128)} %shard_map.122.refs_0_.refs_4_), calls=%async_computation.2 | async-start | bytes 65536 | tf_op jit(solution)/shard_map/all_to_all | solution.py:164
  106.9 2.2 copy-start.4
  109.1 11.1 %collective-permute-start.14 = (bf16[40,896]{1,0:T(8,128)(2,1)S(1)}, bf16[40,896]{1,0:T(8,128)(2,1)S(1)}, u32[]{:S(2)}, u32[]{:S(2)}) collective-permute-start(bf16[40,896]{1,0:T(8,128)(2,1)S(1)} %get-tuple-element.24), channel_id=1, source_target_pairs={{0,4},{4,0},{8,12},{12,8},{16,20},{20,16},{24,28},{28,24},{1,5},{5... | collective-permute-start | bytes 215048 | tf_op jit(solution)/shard_map/ppermute | solution.py:180
  118.1 1.4 copy-start
  120.2 7.5 %collective-permute-start.15 = (bf16[40,896]{1,0:T(8,128)(2,1)S(1)}, bf16[40,896]{1,0:T(8,128)(2,1)S(1)}, u32[]{:S(2)}, u32[]{:S(2)}) collective-permute-start(bf16[40,896]{1,0:T(8,128)(2,1)S(1)} %add_convert_fusion.1), channel_id=1, source_target_pairs={{0,4},{4,0},{8,12},{12,8},{16,20},{20,16},{24,28},{28,24},{1,5},{5... | collective-permute-start | bytes 215048 | tf_op jit(solution)/shard_map/ppermute | solution.py:180
  120.6 1.7 copy-start.1
  123.0 23.4 %all-to-all-start.2 = ((f32[8,32,128]{2,1,0:T(8,128)}), f32[8,32,128]{2,1,0:T(8,128)S(1)}, u32[]{:S(2)}, u32[]{:S(2)}) async-start(f32[8,32,128]{2,1,0:T(8,128)} %broadcast_in_dim.72), calls=%async_computation.3 | async-start | bytes 262144 | tf_op jit(solution)/shard_map/all_to_all | solution.py:164
  127.7 66.3 %all-gather.6.cloned.1.call-start = ((), (), s32[]{:S(2)}) async-start(), calls=%async_computation.8 | async-start | bytes 1990656 | tf_op jit(solution)/shard_map/all_gather | solution.py:431
  127.8 20.9 %collective-permute-start.18 = (bf16[80,896]{1,0:T(8,128)(2,1)S(1)}, bf16[80,896]{1,0:T(8,128)(2,1)S(1)}, u32[]{:S(2)}, u32[]{:S(2)}) collective-permute-start(bf16[80,896]{1,0:T(8,128)(2,1)S(1)} %pad_maximum_fusion.refs_0_), channel_id=1, source_target_pairs={{0,24},{4,28},{8,0},{12,4},{16,8},{20,12},{24,16},{28,20},{1,25},{... | collective-permute-start | bytes 430088 | tf_op jit(solution)/shard_map/ppermute | solution.py:175
  131.8 16.9 %collective-permute-start.17 = (bf16[80,896]{1,0:T(8,128)(2,1)S(1)}, bf16[80,896]{1,0:T(8,128)(2,1)}, u32[]{:S(2)}, u32[]{:S(2)}) collective-permute-start(bf16[80,896]{1,0:T(8,128)(2,1)S(1)} %pad_maximum_fusion.refs_0_), channel_id=1, source_target_pairs={{0,16},{4,20},{8,24},{12,28},{16,0},{20,4},{24,8},{28,12},{1,17},{... | collective-permute-start | bytes 430088 | tf_op jit(solution)/shard_map/ppermute | solution.py:175
  133.1 15.6 %collective-permute-start.16 = (bf16[80,896]{1,0:T(8,128)(2,1)S(1)}, bf16[80,896]{1,0:T(8,128)(2,1)}, u32[]{:S(2)}, u32[]{:S(2)}) collective-permute-start(bf16[80,896]{1,0:T(8,128)(2,1)S(1)} %pad_maximum_fusion.refs_0_), channel_id=1, source_target_pairs={{0,8},{4,12},{8,16},{12,20},{16,24},{20,28},{24,0},{28,4},{1,9},{5... | collective-permute-start | bytes 430088 | tf_op jit(solution)/shard_map/ppermute | solution.py:175
  146.4 6.8 %copy-start.2 = (bf16[4,1152,256]{2,1,0:T(8,128)(2,1)S(1)}, bf16[4,1152,256]{2,1,0:T(8,128)(2,1)}, u32[]{:S(2)}) copy-start(bf16[4,1152,256]{2,1,0:T(8,128)(2,1)} %copy-done) | copy-start | bytes 7077892
  146.4 2.2 copy-start.6
  148.6 3.3 %copy-start.17 = (f32[128,32]{0,1:T(8,128)S(1)}, f32[128,32]{0,1:T(8,128)}, u32[]{:S(2)}) copy-start(f32[128,32]{0,1:T(8,128)} %param.12) | copy-start | bytes 49156
  151.1 0.8 copy-start.13
  155.4 5.0 %copy-start.15 = (bf16[4,1152,256]{2,1,0:T(8,128)(2,1)}, bf16[4,1152,256]{2,1,0:T(8,128)(2,1)S(1)}, u32[]{:S(2)}) copy-start(bf16[4,1152,256]{2,1,0:T(8,128)(2,1)S(1)} %add_convert_fusion) | copy-start | bytes 7077892
  155.4 38.5 %copy-start.14 = (bf16[288,896]{1,0:T(8,128)(2,1)S(1)}, bf16[288,896]{1,0:T(8,128)(2,1)}, u32[]{:S(2)}) copy-start(bf16[288,896]{1,0:T(8,128)(2,1)} %copy-done.13) | copy-start | bytes 1548292
  156.7 72.1 %collective-permute-start.8 = (bf16[1152,256]{1,0:T(8,128)(2,1)}, bf16[1152,256]{1,0:T(8,128)(2,1)}, u32[]{:S(2)}, u32[]{:S(2)}) collective-permute-start(bf16[1152,256]{1,0:T(8,128)(2,1)} %get-tuple-element.30), channel_id=1, source_target_pairs={{0,64},{64,128},{128,192},{192,0},{1,65},{65,129},{129,193},{193,1... | collective-permute-start | bytes 1769480 | tf_op jit(solution)/shard_map/ppermute | solution.py:175
  157.0 71.7 %collective-permute-start.10 = (bf16[1152,256]{1,0:T(8,128)(2,1)}, bf16[1152,256]{1,0:T(8,128)(2,1)}, u32[]{:S(2)}, u32[]{:S(2)}) collective-permute-start(bf16[1152,256]{1,0:T(8,128)(2,1)} %get-tuple-element.31), channel_id=1, source_target_pairs={{0,192},{64,0},{128,64},{192,128},{1,193},{65,1},{129,65},{193,129... | collective-permute-start | bytes 1769480 | tf_op jit(solution)/shard_map/ppermute | solution.py:175
  158.7 70.1 %collective-permute-start.9 = (bf16[1152,256]{1,0:T(8,128)(2,1)}, bf16[1152,256]{1,0:T(8,128)(2,1)}, u32[]{:S(2)}, u32[]{:S(2)}) collective-permute-start(bf16[1152,256]{1,0:T(8,128)(2,1)} %get-tuple-element.32), channel_id=1, source_target_pairs={{0,128},{64,192},{128,0},{192,64},{1,129},{65,193},{129,1},{193,65... | collective-permute-start | bytes 1769480 | tf_op jit(solution)/shard_map/ppermute | solution.py:175
  161.1 40.9 %all-to-all-start.3 = ((f32[32,1,896]{2,1,0:T(1,128)}), f32[32,1,896]{2,1,0:T(1,128)S(1)}, u32[]{:S(2)}, u32[]{:S(2)}) async-start(f32[32,1,896]{2,1,0:T(1,128)} %reshape.67), calls=%async_computation.4 | async-start | bytes 229376 | tf_op jit(solution)/shard_map/all_to_all | solution.py:164
  194.0 1.5 copy-start.9
  201.8 42.1 %collective-permute-start.21 = (bf16[288,896]{1,0:T(8,128)(2,1)S(1)}, bf16[288,896]{1,0:T(8,128)(2,1)S(1)}, u32[]{:S(2)}, u32[]{:S(2)}) collective-permute-start(bf16[288,896]{1,0:T(8,128)(2,1)S(1)} %shard_map.130.refs_0_), channel_id=1, source_target_pairs={{0,3},{1,0},{2,1},{3,2},{4,7},{5,4},{6,5},{7,6},{8,11},{9,8},{10,9... | collective-permute-start | bytes 1548296 | tf_op jit(solution)/shard_map/ppermute | solution.py:175
  201.9 40.9 %collective-permute-start.20 = (bf16[288,896]{1,0:T(8,128)(2,1)S(1)}, bf16[288,896]{1,0:T(8,128)(2,1)}, u32[]{:S(2)}, u32[]{:S(2)}) collective-permute-start(bf16[288,896]{1,0:T(8,128)(2,1)S(1)} %shard_map.130.refs_0_), channel_id=1, source_target_pairs={{0,2},{1,3},{2,0},{3,1},{4,6},{5,7},{6,4},{7,5},{8,10},{9,11},{10,... | collective-permute-start | bytes 1548296 | tf_op jit(solution)/shard_map/ppermute | solution.py:175
  202.8 25.3 %all-to-all-start.4 = ((f32[32,1,896]{2,1,0:T(1,128)}), f32[32,1,896]{2,1,0:T(1,128)S(1)}, u32[]{:S(2)}, u32[]{:S(2)}) async-start(f32[32,1,896]{2,1,0:T(1,128)} %broadcast_in_dim.74), calls=%async_computation.5 | async-start | bytes 229376 | tf_op jit(solution)/shard_map/all_to_all | solution.py:164
  228.8 14.0 %collective-permute-start.19 = (bf16[288,896]{1,0:T(8,128)(2,1)S(1)}, bf16[288,896]{1,0:T(8,128)(2,1)S(1)}, u32[]{:S(2)}, u32[]{:S(2)}) collective-permute-start(bf16[288,896]{1,0:T(8,128)(2,1)S(1)} %shard_map.130.refs_0_), channel_id=1, source_target_pairs={{0,1},{1,2},{2,3},{3,0},{4,5},{5,6},{6,7},{7,4},{8,9},{9,10},{10,1... | collective-permute-start | bytes 1548296 | tf_op jit(solution)/shard_map/ppermute | solution.py:175
  244.1 1.3 copy-start.16
Sparse Core Ops, SparseCore 0:
  11.5 49.8 reduce-scatter.1
Sparse Core Ops, SparseCore 1:
  11.2 38.8 all-gather.3
  152.0 42.0 all-gather.5

commit v5 on v4

--- a/solution.py
+++ b/solution.py
@@ -322,14 +322,6 @@
             flops=3_000_000_000, bytes_accessed=3_600_000, transcendentals=0
         ),
     )(grams, whole, after)
-
-
-def muon_spread(update):
-    y_at = lax.axis_index("y")
-    out = jnp.zeros((4,) + update.shape, bf16)
-    for k, got in enumerate(swap([update] * 4, "y", 4)):
-        out = lax.dynamic_update_index_in_dim(out, got, lax.rem(y_at + 4 - k, 4), 0)
-    return out
 
 
 def join_kernel(first_ref, second_ref, after_ref, out_ref):
@@ -443,7 +435,7 @@
     router_part = jnp.dot(logit_grad, input_f, precision=lax.Precision.HIGHEST)
     router_got = exchange(router_part.reshape(EXPERTS, 1, width), EP)
     update = muon_update_of(whole, grams, router_part)
-    muon_update = muon_spread(update)
+    muon_update = lax.all_gather(update, "y", axis=0, tiled=False)
     router_row = add_up(router_got, update)
     router_grad = spread(router_row, EP, EXPERTS).reshape(EXPERTS, width).T
     token_grad = lax.dot_general(

time: 254 us -> 230 us (0.906)
  the two profiles are of different devices: /device:TPU:38 before, /device:TPU:2 now
where the time goes in v5:
time: 230 us; the launch traced here: 228 us
  starting transfers between devices  68.1 us (30%)
  waiting for transfers between devices  67.4 us (29%)
  Pallas kernels  42.4 us (18%)
  local copies, waits for them, and re-layouts  23.9 us (10%)
  between operations  17.1 us (7%)
  other arithmetic  7.92 us (3%)
    all_to_all x5, starting transfers between devices, exchange(): return lax.all_to_all(value, axes, split_axis=0, concat_axis=0, tiled=True)  37.1 us
    ppermute x16, starting transfers between devices, swap(): got.append(lax.ppermute(pieces[k], axes, pairs))  30.6 us
    reduce_scatter x1, waiting for transfers between devices, muon_blocks(): part = lax.psum_scatter(attention, 'y', scatter_dimension=0, tiled=True)[0]  28.5 us
    all_to_all x5, waiting for transfers between devices, exchange(): return lax.all_to_all(value, axes, split_axis=0, concat_axis=0, tiled=True)  19.5 us
    unnamed x36, local copies, waits for them, and re-layouts  19.4 us
    ppermute x16, waiting for transfers between devices, swap(): got.append(lax.ppermute(pieces[k], axes, pairs))  14.1 us
    pallas_call x2, Pallas kernels, upstream_partial(): pl.pallas_call(upstream_kernel, grid_spec=grid_spec, out_shape=jax.ShapeD...  11.2 us
    pallas_call x1, Pallas kernels, grad_down_of(): pl.pallas_call(grad_down_kernel, grid=(parts,), in_specs=[pl.BlockSpec((1...  10.5 us
  transfers between devices with their start and end apart: 28, of which 13 were waited for; matrix products, arithmetic and copies ran while one was open for 6% of the time, Pallas kernels for 18%

profile of v5, /device:TPU:2, one launch (start us, length us, event | category | flops | bytes accessed | tf_op | source)
XLA Modules:
  0.0 228.3 jit_solution(15210386167220604870)
XLA Ops:
  8.1 0.7 reduce-scatter.2.cloned.1.call-update
  8.8 0.5 all-gather.6.cloned.1.call-update
  9.4 2.3 %shard_map.119 = (bf16[32,40,896]{2,1,0:T(8,128)(2,1)}, f32[32,128]{1,0:T(8,128)S(1)}, f32[32,128]{1,0:T(8,128)S(1)}) custom-call(s32[8,128]{1,0:T(8,128)S(1)} %bitcast.66, bf16[128,896]{1,0:T(8,128)(2,1)S(1)} %copy-done.11, bf16[128,896]{1,0:T(8,128)(2,1)S(1)} %copy-done.7, f32[32,896]{1,0:T(8,128)S(1)} %bitcast.63), custom_call_target="tpu_custom_call" | custom-call | flops 300000000 | bytes 2800000 | tf_op jit(solution)/shard_map/pallas_call | solution.py:63
  11.7 11.6 %all-to-all-start = ((bf16[32,40,896]{2,1,0:T(8,128)(2,1)}), bf16[32,40,896]{2,1,0:T(8,128)(2,1)}, u32[]{:S(2)}, u32[]{:S(2)}) async-start(bf16[32,40,896]{2,1,0:T(8,128)(2,1)} %get-tuple-element.18), calls=%async_computation | async-start | bytes 4587520 | tf_op jit(solution)/shard_map/all_to_all | solution.py:164
  23.4 2.4 %collective-permute-start.5 = (f32[32,128]{1,0:T(8,128)S(1)}, f32[32,128]{1,0:T(8,128)S(1)}, u32[]{:S(2)}, u32[]{:S(2)}) collective-permute-start(f32[32,128]{1,0:T(8,128)S(1)} %get-tuple-element.17), channel_id=1, source_target_pairs={{0,192},{32,224},{64,0},{96,32},{128,64},{160,96},{192,128},{224,1... | collective-permute-start | bytes 49160 | tf_op jit(solution)/shard_map/ppermute | solution.py:175
  26.2 1.1 collective-permute-start.3
  27.3 1.2 collective-permute-start.2
  28.5 1.8 collective-permute-start.1
  30.3 1.1 collective-permute-start
  31.5 0.7 collective-permute-done.2
  32.2 1.4 collective-permute-done.1
  34.2 28.5 %reduce-scatter.2.cloned.1.call-done = bf16[1,288,896]{2,1,0:T(8,128)(2,1)} async-done(((bf16[4,288,896]{2,1,0:T(8,128)(2,1)}), bf16[1,288,896]{2,1,0:T(8,128)(2,1)}) %reduce-scatter.2.cloned.1.call-update) | async-done | bytes 516112 | tf_op jit(solution)/shard_map/reduce_scatter | solution.py:273
  62.7 1.0 copy-done.10
  63.8 0.7 shard_map.121
  64.5 2.4 %collective-permute-start.11 = (bf16[80,896]{1,0:T(8,128)(2,1)S(1)}, bf16[80,896]{1,0:T(8,128)(2,1)S(1)}, u32[]{:S(2)}, u32[]{:S(2)}) collective-permute-start(bf16[80,896]{1,0:T(8,128)(2,1)S(1)} %get-tuple-element.20), channel_id=1, source_target_pairs={{0,8},{4,12},{8,16},{12,20},{16,24},{20,28},{24,0},{28,4},{1,9},{5... | collective-permute-start | bytes 430088 | tf_op jit(solution)/shard_map/ppermute | solution.py:175
  66.9 5.1 %collective-permute-start.12 = (bf16[80,896]{1,0:T(8,128)(2,1)S(1)}, bf16[80,896]{1,0:T(8,128)(2,1)S(1)}, u32[]{:S(2)}, u32[]{:S(2)}) collective-permute-start(bf16[80,896]{1,0:T(8,128)(2,1)S(1)} %get-tuple-element.21), channel_id=1, source_target_pairs={{0,16},{4,20},{8,24},{12,28},{16,0},{20,4},{24,8},{28,12},{1,17},{... | collective-permute-start | bytes 430088 | tf_op jit(solution)/shard_map/ppermute | solution.py:175
  72.0 4.0 %collective-permute-start.13 = (bf16[80,896]{1,0:T(8,128)(2,1)S(1)}, bf16[80,896]{1,0:T(8,128)(2,1)S(1)}, u32[]{:S(2)}, u32[]{:S(2)}) collective-permute-start(bf16[80,896]{1,0:T(8,128)(2,1)S(1)} %get-tuple-element.22), channel_id=1, source_target_pairs={{0,24},{4,28},{8,0},{12,4},{16,8},{20,12},{24,16},{28,20},{1,25},{... | collective-permute-start | bytes 430088 | tf_op jit(solution)/shard_map/ppermute | solution.py:175
  76.1 2.0 copy-done.5
  78.1 8.2 %shard_map.120.refs_4_ = f32[1152,896]{1,0:T(8,128)} custom-call(bf16[8,1152,256]{2,1,0:T(8,128)(2,1)} %all-gather.6.cloned.1.call-done.hidden_ref, bf16[2048,896]{1,0:T(8,128)(2,1)S(1)} %bitcast.62), custom_call_target="tpu_custom_call" | custom-call | flops 4227858432 | bytes 12500000 | tf_op jit(solution)/shard_map/pallas_call | solution.py:116
  86.3 2.0 collective-permute-done.12.refs_2_
  88.4 2.2 copy-done.3
  90.7 0.5 slice.28
  91.9 0.5 slice.37
  93.1 2.0 collective-permute-done.14
  95.2 1.9 fusion
  97.3 2.1 collective-permute-done.15
  99.5 3.1 %collective-permute-start.18 = (bf16[80,896]{1,0:T(8,128)(2,1)S(1)}, bf16[80,896]{1,0:T(8,128)(2,1)S(1)}, u32[]{:S(2)}, u32[]{:S(2)}) collective-permute-start(bf16[80,896]{1,0:T(8,128)(2,1)S(1)} %pad_maximum_fusion.refs_0_), channel_id=1, source_target_pairs={{0,24},{4,28},{8,0},{12,4},{16,8},{20,12},{24,16},{28,20},{1,25},{... | collective-permute-start | bytes 430088 | tf_op jit(solution)/shard_map/ppermute | solution.py:175
  102.6 3.8 %collective-permute-start.17 = (bf16[80,896]{1,0:T(8,128)(2,1)S(1)}, bf16[80,896]{1,0:T(8,128)(2,1)S(1)}, u32[]{:S(2)}, u32[]{:S(2)}) collective-permute-start(bf16[80,896]{1,0:T(8,128)(2,1)S(1)} %pad_maximum_fusion.refs_0_), channel_id=1, source_target_pairs={{0,16},{4,20},{8,24},{12,28},{16,0},{20,4},{24,8},{28,12},{1,17},{... | collective-permute-start | bytes 430088 | tf_op jit(solution)/shard_map/ppermute | solution.py:175
  106.4 0.6 multiply_reduce_fusion
  107.1 0.6 shard_map.122.refs_0_.refs_4_
  107.8 0.8 collective-permute-done.18.refs_3_
  108.6 6.8 %collective-permute-done.17.refs_2_ = bf16[80,896]{1,0:T(8,128)(2,1)S(1)} collective-permute-done((bf16[80,896]{1,0:T(8,128)(2,1)S(1)}, bf16[80,896]{1,0:T(8,128)(2,1)S(1)}, u32[]{:S(2)}, u32[]{:S(2)}) %collective-permute-start.17) | collective-permute-done | bytes 143392 | tf_op jit(solution)/shard_map/ppermute | solution.py:175
  115.4 1.9 collective-permute-done.16.refs_1_
  117.3 1.4 shard_map.129
  118.7 0.8 copy-done.13
  119.7 6.9 %all-to-all-start.1 = ((f32[32,2,40]{2,1,0:T(2,128)}), f32[32,2,40]{2,1,0:T(2,128)S(1)}, u32[]{:S(2)}, u32[]{:S(2)}) async-start(f32[32,2,40]{2,1,0:T(2,128)} %shard_map.122.refs_0_.refs_4_), calls=%async_computation.2 | async-start | bytes 65536 | tf_op jit(solution)/shard_map/all_to_all | solution.py:164
  126.7 6.1 %shard_map.123.refs_0_ = bf16[4,1152,256]{2,1,0:T(8,128)(2,1)} custom-call(s32[2]{0:T(128)S(1)} %pad_add_fusion.first_ref, bf16[1152,896]{1,0:T(8,128)(2,1)S(1)} %bitcast.57, bf16[2048,896]{1,0:T(8,128)(2,1)} %bitcast.60, f32[32,2,40]{2,1,0:T(2,128)} %shard_map.122.refs_0_.refs_4_), custom_call_target="tpu_custom_call" | custom-call | flops 2113929216 | bytes 6300000 | tf_op jit(solution)/shard_map/pallas_call | solution.py:94
  132.8 5.1 %shard_map.124.refs_0_ = bf16[4,1152,256]{2,1,0:T(8,128)(2,1)S(1)} custom-call(s32[2]{0:T(128)S(1)} %pad_add_fusion.1.first_ref, bf16[1152,896]{1,0:T(8,128)(2,1)S(1)} %bitcast.58, bf16[2048,896]{1,0:T(8,128)(2,1)} %bitcast.61, bf16[4,1152,256]{2,1,0:T(8,128)(2,1)} %shard_map.123.refs_0_), custom_call_target="tpu_custom_call" | custom-call | flops 2113929216 | bytes 6300000 | tf_op jit(solution)/shard_map/pallas_call | solution.py:94
  137.9 1.4 copy-done
  139.4 0.6 reshape.72.gate_ref
  140.3 1.7 copy-done.1
  142.0 0.7 broadcast_in_dim.56
  142.6 5.0 %all-to-all-start.2 = ((f32[8,32,128]{2,1,0:T(8,128)}), f32[8,32,128]{2,1,0:T(8,128)S(1)}, u32[]{:S(2)}, u32[]{:S(2)}) async-start(f32[8,32,128]{2,1,0:T(8,128)} %broadcast_in_dim.56), calls=%async_computation.3 | async-start | bytes 262144 | tf_op jit(solution)/shard_map/all_to_all | solution.py:164
  147.6 10.5 %shard_map.125.refs_0_ = bf16[1,2048,896]{2,1,0:T(8,128)(2,1)} custom-call(bf16[8,1152,256]{2,1,0:T(8,128)(2,1)} %all-gather.6.cloned.1.call-done.hidden_ref, bf16[1152,896]{1,0:T(8,128)(2,1)S(1)} %bitcast.59, f32[1152,1]{1,0:T(8,128)S(1)} %reshape.72.gate_ref), custom_call_target="tpu_custom_call" | custom-call | flops 4227858432 | bytes 12500000 | tf_op jit(solution)/shard_map/pallas_call | solution.py:145
  158.1 2.0 copy-done.6
  160.2 0.7 copy-done.16
  161.1 1.5 copy-done.9
  162.6 1.0 copy-done.14
  163.6 7.2 %shard_map.130.refs_0_ = bf16[288,896]{1,0:T(8,128)(2,1)} custom-call(bf16[8,288,288]{2,1,0:T(8,128)(2,1)S(1)} %bitcast.64, bf16[288,896]{1,0:T(8,128)(2,1)S(1)} %copy-done.14, f32[32,896]{1,0:T(8,128)S(1)} %fusion.10.after_ref), custom_call_target="tpu_custom_call" | custom-call | flops 3000000000 | bytes 3600000 | tf_op jit(solution)/shard_map/pallas_call | solution.py:315
  170.8 2.2 add_convert_fusion
  173.1 1.4 copy-done.15
  174.6 1.5 collective-permute-start.8
  176.1 0.6 collective-permute-start.10
  176.7 2.1 collective-permute-start.9
  178.8 0.7 reshape.67
  179.5 9.8 %all-to-all-start.3 = ((f32[32,1,896]{2,1,0:T(1,128)}), f32[32,1,896]{2,1,0:T(1,128)S(1)}, u32[]{:S(2)}, u32[]{:S(2)}) async-start(f32[32,1,896]{2,1,0:T(1,128)} %reshape.67), calls=%async_computation.4 | async-start | bytes 229376 | tf_op jit(solution)/shard_map/all_to_all | solution.py:164
  189.4 10.3 %all-to-all-done.3.values_ref = f32[32,1,896]{2,1,0:T(1,128)S(1)} async-done(((f32[32,1,896]{2,1,0:T(1,128)}), f32[32,1,896]{2,1,0:T(1,128)S(1)}, u32[]{:S(2)}, u32[]{:S(2)}) %all-to-all-start.3) | async-done | bytes 114720 | tf_op jit(solution)/shard_map/all_to_all | solution.py:164
  199.8 0.7 broadcast_in_dim.58
  200.5 3.9 %all-to-all-start.4 = ((f32[32,1,896]{2,1,0:T(1,128)}), f32[32,1,896]{2,1,0:T(1,128)S(1)}, u32[]{:S(2)}, u32[]{:S(2)}) async-start(f32[32,1,896]{2,1,0:T(1,128)} %broadcast_in_dim.58), calls=%async_computation.5 | async-start | bytes 229376 | tf_op jit(solution)/shard_map/all_to_all | solution.py:164
  204.3 1.3 convolution_convert_fusion
  205.6 9.1 %all-to-all-done.4 = f32[32,1,896]{2,1,0:T(1,128)S(1)} async-done(((f32[32,1,896]{2,1,0:T(1,128)}), f32[32,1,896]{2,1,0:T(1,128)S(1)}, u32[]{:S(2)}, u32[]{:S(2)}) %all-to-all-start.4) | async-done | bytes 114720 | tf_op jit(solution)/shard_map/all_to_all | solution.py:164
  214.7 0.7 copy.32
  215.4 2.4 %fusion.4 = bf16[1152,256]{1,0:T(8,128)(2,1)} fusion(bf16[1152,256]{1,0:T(8,128)(2,1)S(1)} %collective-permute-done.10, bf16[1152,256]{1,0:T(8,128)(2,1)} %collective-permute-done.9, bf16[1152,256]{1,0:T(8,128)(2,1)S(1)} %collective-permute-done.8, bf16[4,1152,256]{2,1,0:T(8,128)(2,1)} %copy-done.15, f32[1152]{0:T(1024)S(1)} %mul.61), kind=kLoop, calls=%fused_computation.9 | loop fusion | flops 2654208 | bytes 2953728 | tf_op jit(solution)/shard_map/convert_element_type | solution.py:429
  217.8 3.0 %copy.34 = bf16[4,288,896]{2,1,0:T(8,128)(2,1)} copy(bf16[4,288,896]{2,1,0:T(8,128)(2,1)} %bitcast.68) | data formatting | bytes 4128768
  (79 shorter events, 3.2 us)
Async XLA Ops:
  8.0 1.4 copy-start.7
  8.0 1.4 copy-start.8
  8.0 1.4 copy-start.12
  8.0 1.4 copy-start.11
  8.0 54.7 %reduce-scatter.2.cloned.1.call-start = ((), (), s32[]{:S(2)}) async-start(), calls=%async_computation.7 | async-start | bytes 2580480 | tf_op jit(solution)/shard_map/reduce_scatter | solution.py:273
  8.8 67.3 %all-gather.6.cloned.1.call-start = ((), (), s32[]{:S(2)}) async-start(), calls=%async_computation.6 | async-start | bytes 5308416 | tf_op jit(solution)/shard_map/all_gather | solution.py:392
  11.7 83.5 %all-to-all-start = ((bf16[32,40,896]{2,1,0:T(8,128)(2,1)}), bf16[32,40,896]{2,1,0:T(8,128)(2,1)}, u32[]{:S(2)}, u32[]{:S(2)}) async-start(bf16[32,40,896]{2,1,0:T(8,128)(2,1)} %get-tuple-element.18), calls=%async_computation | async-start | bytes 4587520 | tf_op jit(solution)/shard_map/all_to_all | solution.py:164
  23.3 137.8 %all-gather.8.cloned.1.call-start = ((), (), s32[]{:S(2)}) async-start(), calls=%async_computation.8 | async-start | bytes 1990656 | tf_op jit(solution)/shard_map/all_gather | solution.py:423
  23.4 5.1 %collective-permute-start.6 = (f32[32,128]{1,0:T(8,128)S(1)}, f32[32,128]{1,0:T(8,128)S(1)}, u32[]{:S(2)}, u32[]{:S(2)}) collective-permute-start(f32[32,128]{1,0:T(8,128)S(1)} %get-tuple-element.17), channel_id=1, source_target_pairs={{0,224},{32,0},{64,32},{96,64},{128,96},{160,128},{192,160},{224,1... | collective-permute-start | bytes 49160 | tf_op jit(solution)/shard_map/ppermute | solution.py:175
  23.4 6.9 %collective-permute-start.5 = (f32[32,128]{1,0:T(8,128)S(1)}, f32[32,128]{1,0:T(8,128)S(1)}, u32[]{:S(2)}, u32[]{:S(2)}) collective-permute-start(f32[32,128]{1,0:T(8,128)S(1)} %get-tuple-element.17), channel_id=1, source_target_pairs={{0,192},{32,224},{64,0},{96,32},{128,64},{160,96},{192,128},{224,1... | collective-permute-start | bytes 49160 | tf_op jit(solution)/shard_map/ppermute | solution.py:175
  25.8 5.5 %collective-permute-start.4 = (f32[32,128]{1,0:T(8,128)S(1)}, f32[32,128]{1,0:T(8,128)S(1)}, u32[]{:S(2)}, u32[]{:S(2)}) collective-permute-start(f32[32,128]{1,0:T(8,128)S(1)} %get-tuple-element.17), channel_id=1, source_target_pairs={{0,160},{32,192},{64,224},{96,0},{128,32},{160,64},{192,96},{224,1... | collective-permute-start | bytes 49160 | tf_op jit(solution)/shard_map/ppermute | solution.py:175
  26.2 5.3 %collective-permute-start.3 = (f32[32,128]{1,0:T(8,128)S(1)}, f32[32,128]{1,0:T(8,128)S(1)}, u32[]{:S(2)}, u32[]{:S(2)}) collective-permute-start(f32[32,128]{1,0:T(8,128)S(1)} %get-tuple-element.17), channel_id=1, source_target_pairs={{0,128},{32,160},{64,192},{96,224},{128,0},{160,32},{192,64},{224,... | collective-permute-start | bytes 49160 | tf_op jit(solution)/shard_map/ppermute | solution.py:175
  27.3 4.9 %collective-permute-start.2 = (f32[32,128]{1,0:T(8,128)S(1)}, f32[32,128]{1,0:T(8,128)S(1)}, u32[]{:S(2)}, u32[]{:S(2)}) collective-permute-start(f32[32,128]{1,0:T(8,128)S(1)} %get-tuple-element.17), channel_id=1, source_target_pairs={{0,96},{32,128},{64,160},{96,192},{128,224},{160,0},{192,32},{224,... | collective-permute-start | bytes 49160 | tf_op jit(solution)/shard_map/ppermute | solution.py:175
  28.5 5.1 %collective-permute-start.1 = (f32[32,128]{1,0:T(8,128)S(1)}, f32[32,128]{1,0:T(8,128)S(1)}, u32[]{:S(2)}, u32[]{:S(2)}) collective-permute-start(f32[32,128]{1,0:T(8,128)S(1)} %get-tuple-element.17), channel_id=1, source_target_pairs={{0,64},{32,96},{64,128},{96,160},{128,192},{160,224},{192,0},{224,... | collective-permute-start | bytes 49160 | tf_op jit(solution)/shard_map/ppermute | solution.py:175
  30.3 3.6 %collective-permute-start = (f32[32,128]{1,0:T(8,128)S(1)}, f32[32,128]{1,0:T(8,128)S(1)}, u32[]{:S(2)}, u32[]{:S(2)}) collective-permute-start(f32[32,128]{1,0:T(8,128)S(1)} %get-tuple-element.17), channel_id=1, source_target_pairs={{0,32},{32,64},{64,96},{96,128},{128,160},{160,192},{192,224},{224... | collective-permute-start | bytes 49160 | tf_op jit(solution)/shard_map/ppermute | solution.py:175
  62.7 1.0 copy-start.10
  64.5 21.8 %collective-permute-start.11 = (bf16[80,896]{1,0:T(8,128)(2,1)S(1)}, bf16[80,896]{1,0:T(8,128)(2,1)S(1)}, u32[]{:S(2)}, u32[]{:S(2)}) collective-permute-start(bf16[80,896]{1,0:T(8,128)(2,1)S(1)} %get-tuple-element.20), channel_id=1, source_target_pairs={{0,8},{4,12},{8,16},{12,20},{16,24},{20,28},{24,0},{28,4},{1,9},{5... | collective-permute-start | bytes 430088 | tf_op jit(solution)/shard_map/ppermute | solution.py:175
  66.9 21.5 %collective-permute-start.12 = (bf16[80,896]{1,0:T(8,128)(2,1)S(1)}, bf16[80,896]{1,0:T(8,128)(2,1)S(1)}, u32[]{:S(2)}, u32[]{:S(2)}) collective-permute-start(bf16[80,896]{1,0:T(8,128)(2,1)S(1)} %get-tuple-element.21), channel_id=1, source_target_pairs={{0,16},{4,20},{8,24},{12,28},{16,0},{20,4},{24,8},{28,12},{1,17},{... | collective-permute-start | bytes 430088 | tf_op jit(solution)/shard_map/ppermute | solution.py:175
  72.0 16.3 %collective-permute-start.13 = (bf16[80,896]{1,0:T(8,128)(2,1)S(1)}, bf16[80,896]{1,0:T(8,128)(2,1)S(1)}, u32[]{:S(2)}, u32[]{:S(2)}) collective-permute-start(bf16[80,896]{1,0:T(8,128)(2,1)S(1)} %get-tuple-element.22), channel_id=1, source_target_pairs={{0,24},{4,28},{8,0},{12,4},{16,8},{20,12},{24,16},{28,20},{1,25},{... | collective-permute-start | bytes 430088 | tf_op jit(solution)/shard_map/ppermute | solution.py:175
  76.1 2.0 copy-start.5
  88.4 2.2 copy-start.3
  90.6 4.4 %collective-permute-start.14 = (bf16[40,896]{1,0:T(8,128)(2,1)S(1)}, bf16[40,896]{1,0:T(8,128)(2,1)S(1)}, u32[]{:S(2)}, u32[]{:S(2)}) collective-permute-start(bf16[40,896]{1,0:T(8,128)(2,1)S(1)} %get-tuple-element.24), channel_id=1, source_target_pairs={{0,4},{4,0},{8,12},{12,8},{16,20},{20,16},{24,28},{28,24},{1,5},{5... | collective-permute-start | bytes 215048 | tf_op jit(solution)/shard_map/ppermute | solution.py:180
  95.1 4.4 %collective-permute-start.15 = (bf16[40,896]{1,0:T(8,128)(2,1)S(1)}, bf16[40,896]{1,0:T(8,128)(2,1)S(1)}, u32[]{:S(2)}, u32[]{:S(2)}) collective-permute-start(bf16[40,896]{1,0:T(8,128)(2,1)S(1)} %add_convert_fusion.1), channel_id=1, source_target_pairs={{0,4},{4,0},{8,12},{12,8},{16,20},{20,16},{24,28},{28,24},{1,5},{5... | collective-permute-start | bytes 215048 | tf_op jit(solution)/shard_map/ppermute | solution.py:180
  97.1 9.3 %copy-start.4 = (f32[1152,896]{1,0:T(8,128)S(1)}, f32[1152,896]{1,0:T(8,128)}, u32[]{:S(2)}) copy-start(f32[1152,896]{1,0:T(8,128)} %shard_map.120.refs_4_) | copy-start | bytes 12386308
  99.5 9.1 %collective-permute-start.18 = (bf16[80,896]{1,0:T(8,128)(2,1)S(1)}, bf16[80,896]{1,0:T(8,128)(2,1)S(1)}, u32[]{:S(2)}, u32[]{:S(2)}) collective-permute-start(bf16[80,896]{1,0:T(8,128)(2,1)S(1)} %pad_maximum_fusion.refs_0_), channel_id=1, source_target_pairs={{0,24},{4,28},{8,0},{12,4},{16,8},{20,12},{24,16},{28,20},{1,25},{... | collective-permute-start | bytes 430088 | tf_op jit(solution)/shard_map/ppermute | solution.py:175
  102.6 12.8 %collective-permute-start.17 = (bf16[80,896]{1,0:T(8,128)(2,1)S(1)}, bf16[80,896]{1,0:T(8,128)(2,1)S(1)}, u32[]{:S(2)}, u32[]{:S(2)}) collective-permute-start(bf16[80,896]{1,0:T(8,128)(2,1)S(1)} %pad_maximum_fusion.refs_0_), channel_id=1, source_target_pairs={{0,16},{4,20},{8,24},{12,28},{16,0},{20,4},{24,8},{28,12},{1,17},{... | collective-permute-start | bytes 430088 | tf_op jit(solution)/shard_map/ppermute | solution.py:175
  106.4 10.9 %collective-permute-start.16 = (bf16[80,896]{1,0:T(8,128)(2,1)S(1)}, bf16[80,896]{1,0:T(8,128)(2,1)S(1)}, u32[]{:S(2)}, u32[]{:S(2)}) collective-permute-start(bf16[80,896]{1,0:T(8,128)(2,1)S(1)} %pad_maximum_fusion.refs_0_), channel_id=1, source_target_pairs={{0,8},{4,12},{8,16},{12,20},{16,24},{20,28},{24,0},{28,4},{1,9},{5... | collective-permute-start | bytes 430088 | tf_op jit(solution)/shard_map/ppermute | solution.py:175
  118.7 0.8 copy-start.13
  119.7 19.6 %all-to-all-start.1 = ((f32[32,2,40]{2,1,0:T(2,128)}), f32[32,2,40]{2,1,0:T(2,128)S(1)}, u32[]{:S(2)}, u32[]{:S(2)}) async-start(f32[32,2,40]{2,1,0:T(2,128)} %shard_map.122.refs_0_.refs_4_), calls=%async_computation.2 | async-start | bytes 65536 | tf_op jit(solution)/shard_map/all_to_all | solution.py:164
  132.8 38.0 %collective-permute-start.7 = (bf16[4,1152,256]{2,1,0:T(8,128)(2,1)}, bf16[4,1152,256]{2,1,0:T(8,128)(2,1)}, u32[]{:S(2)}, u32[]{:S(2)}) collective-permute-start(bf16[4,1152,256]{2,1,0:T(8,128)(2,1)} %shard_map.123.refs_0_), channel_id=1, source_target_pairs={{0,32},{32,0},{1,33},{33,1},{2,34},{34,2},{3,35},{35,3},{4,36},{36... | collective-permute-start | bytes 7077896 | tf_op jit(solution)/shard_map/ppermute | solution.py:420
  137.9 1.4 copy-start
  140.3 1.7 copy-start.1
  142.6 15.4 %all-to-all-start.2 = ((f32[8,32,128]{2,1,0:T(8,128)}), f32[8,32,128]{2,1,0:T(8,128)S(1)}, u32[]{:S(2)}, u32[]{:S(2)}) async-start(f32[8,32,128]{2,1,0:T(8,128)} %broadcast_in_dim.56), calls=%async_computation.3 | async-start | bytes 262144 | tf_op jit(solution)/shard_map/all_to_all | solution.py:164
  147.6 70.2 %all-gather.10.cloned.1.call-start = ((), (), s32[]{:S(2)}) async-start(), calls=%async_computation.9 | async-start | bytes 2580480 | tf_op jit(solution)/shard_map/all_gather | solution.py:438
  158.1 2.0 copy-start.6
  160.1 0.7 copy-start.16
  161.1 1.5 copy-start.9
  162.6 1.0 copy-start.14
  163.6 7.2 %copy-start.2 = (bf16[4,1152,256]{2,1,0:T(8,128)(2,1)S(1)}, bf16[4,1152,256]{2,1,0:T(8,128)(2,1)}, u32[]{:S(2)}) copy-start(bf16[4,1152,256]{2,1,0:T(8,128)(2,1)} %copy-done) | copy-start | bytes 7077892
  173.1 1.4 copy-start.15
  174.6 40.8 %collective-permute-start.8 = (bf16[1152,256]{1,0:T(8,128)(2,1)S(1)}, bf16[1152,256]{1,0:T(8,128)(2,1)S(1)}, u32[]{:S(2)}, u32[]{:S(2)}) collective-permute-start(bf16[1152,256]{1,0:T(8,128)(2,1)S(1)} %get-tuple-element.30), channel_id=1, source_target_pairs={{0,64},{64,128},{128,192},{192,0},{1,65},{65,129},{129,193},{193,1... | collective-permute-start | bytes 1769480 | tf_op jit(solution)/shard_map/ppermute | solution.py:175
  176.1 39.3 %collective-permute-start.10 = (bf16[1152,256]{1,0:T(8,128)(2,1)S(1)}, bf16[1152,256]{1,0:T(8,128)(2,1)S(1)}, u32[]{:S(2)}, u32[]{:S(2)}) collective-permute-start(bf16[1152,256]{1,0:T(8,128)(2,1)S(1)} %get-tuple-element.31), channel_id=1, source_target_pairs={{0,192},{64,0},{128,64},{192,128},{1,193},{65,1},{129,65},{193,129... | collective-permute-start | bytes 1769480 | tf_op jit(solution)/shard_map/ppermute | solution.py:175
  176.7 38.7 %collective-permute-start.9 = (bf16[1152,256]{1,0:T(8,128)(2,1)S(1)}, bf16[1152,256]{1,0:T(8,128)(2,1)}, u32[]{:S(2)}, u32[]{:S(2)}) collective-permute-start(bf16[1152,256]{1,0:T(8,128)(2,1)S(1)} %get-tuple-element.32), channel_id=1, source_target_pairs={{0,128},{64,192},{128,0},{192,64},{1,129},{65,193},{129,1},{193,65... | collective-permute-start | bytes 1769480 | tf_op jit(solution)/shard_map/ppermute | solution.py:175
  179.5 20.2 %all-to-all-start.3 = ((f32[32,1,896]{2,1,0:T(1,128)}), f32[32,1,896]{2,1,0:T(1,128)S(1)}, u32[]{:S(2)}, u32[]{:S(2)}) async-start(f32[32,1,896]{2,1,0:T(1,128)} %reshape.67), calls=%async_computation.4 | async-start | bytes 229376 | tf_op jit(solution)/shard_map/all_to_all | solution.py:164
  200.5 14.3 %all-to-all-start.4 = ((f32[32,1,896]{2,1,0:T(1,128)}), f32[32,1,896]{2,1,0:T(1,128)S(1)}, u32[]{:S(2)}, u32[]{:S(2)}) async-start(f32[32,1,896]{2,1,0:T(1,128)} %broadcast_in_dim.58), calls=%async_computation.5 | async-start | bytes 229376 | tf_op jit(solution)/shard_map/all_to_all | solution.py:164
Sparse Core Ops, SparseCore 0:
  11.5 51.2 reduce-scatter.1
  170.9 35.6 all-gather.9
Sparse Core Ops, SparseCore 1:
  11.2 39.2 all-gather.5
  119.6 24.1 all-gather.7

commit v6 on v5

--- a/solution.py
+++ b/solution.py
@@ -434,7 +434,7 @@
     logit_grad = score_grad * scores * (1.0 - scores)
     router_part = jnp.dot(logit_grad, input_f, precision=lax.Precision.HIGHEST)
     router_got = exchange(router_part.reshape(EXPERTS, 1, width), EP)
-    update = muon_update_of(whole, grams, router_part)
+    update = muon_update_of(whole, grams, for_own)
     muon_update = lax.all_gather(update, "y", axis=0, tiled=False)
     router_row = add_up(router_got, update)
     router_grad = spread(router_row, EP, EXPERTS).reshape(EXPERTS, width).T

time: 230 us -> 228 us (level)
  starting transfers between devices: 68.1 us -> 64.6 us
  waiting for transfers between devices: 67.4 us -> 70.7 us
    all_to_all x5, starting transfers between devices: 37.1 us -> 33.7 us  [exchange(): return lax.all_to_all(value, axes, split_axis=0, concat_axis=0, tiled=True)]
    all_to_all x5, waiting for transfers between devices: 19.5 us -> 22.8 us  [exchange(): return lax.all_to_all(value, axes, split_axis=0, concat_axis=0, tiled=True)]
  transfers between devices with their start and end apart: 28 -> 28, of which waited for: 13 -> 14; matrix products, arithmetic and copies ran while one was open for 6% -> 6% of each run, Pallas kernels for 18% -> 18%
where the time goes in v6:
time: 228 us; the launch traced here: 227 us
  waiting for transfers between devices  70.7 us (31%)
  starting transfers between devices  64.6 us (28%)
  Pallas kernels  42.3 us (19%)
  local copies, waits for them, and re-layouts  22.5 us (10%)
  between operations  17.1 us (8%)
  other arithmetic  7.92 us (3%)
    all_to_all x5, starting transfers between devices, exchange(): return lax.all_to_all(value, axes, split_axis=0, concat_axis=0, tiled=True)  33.7 us
    ppermute x16, starting transfers between devices, swap(): got.append(lax.ppermute(pieces[k], axes, pairs))  30.6 us
    reduce_scatter x1, waiting for transfers between devices, muon_blocks(): part = lax.psum_scatter(attention, 'y', scatter_dimension=0, tiled=True)[0]  28.5 us
    all_to_all x5, waiting for transfers between devices, exchange(): return lax.all_to_all(value, axes, split_axis=0, concat_axis=0, tiled=True)  22.8 us
    unnamed x36, local copies, waits for them, and re-layouts  18 us
    ppermute x16, waiting for transfers between devices, swap(): got.append(lax.ppermute(pieces[k], axes, pairs))  14.1 us
    pallas_call x2, Pallas kernels, upstream_partial(): pl.pallas_call(upstream_kernel, grid_spec=grid_spec, out_shape=jax.ShapeD...  11.2 us
    pallas_call x1, Pallas kernels, grad_down_of(): pl.pallas_call(grad_down_kernel, grid=(parts,), in_specs=[pl.BlockSpec((1...  10.5 us
  transfers between devices with their start and end apart: 28, of which 14 were waited for; matrix products, arithmetic and copies ran while one was open for 6% of the time, Pallas kernels for 18%

profile of v6, /device:TPU:2, one launch (start us, length us, event | category | flops | bytes accessed | tf_op | source)
XLA Modules:
  0.0 226.7 jit_solution(697795134535410183)
XLA Ops:
  8.1 0.7 reduce-scatter.2.cloned.1.call-update
  8.8 0.5 all-gather.6.cloned.1.call-update
  9.4 2.3 %shard_map.119 = (bf16[32,40,896]{2,1,0:T(8,128)(2,1)}, f32[32,128]{1,0:T(8,128)S(1)}, f32[32,128]{1,0:T(8,128)S(1)}) custom-call(s32[8,128]{1,0:T(8,128)S(1)} %bitcast.66, bf16[128,896]{1,0:T(8,128)(2,1)S(1)} %copy-done.11, bf16[128,896]{1,0:T(8,128)(2,1)S(1)} %copy-done.7, f32[32,896]{1,0:T(8,128)S(1)} %bitcast.63), custom_call_target="tpu_custom_call" | custom-call | flops 300000000 | bytes 2800000 | tf_op jit(solution)/shard_map/pallas_call | solution.py:63
  11.7 11.6 %all-to-all-start = ((bf16[32,40,896]{2,1,0:T(8,128)(2,1)}), bf16[32,40,896]{2,1,0:T(8,128)(2,1)}, u32[]{:S(2)}, u32[]{:S(2)}) async-start(bf16[32,40,896]{2,1,0:T(8,128)(2,1)} %get-tuple-element.18), calls=%async_computation | async-start | bytes 4587520 | tf_op jit(solution)/shard_map/all_to_all | solution.py:164
  23.4 2.4 %collective-permute-start.5 = (f32[32,128]{1,0:T(8,128)S(1)}, f32[32,128]{1,0:T(8,128)S(1)}, u32[]{:S(2)}, u32[]{:S(2)}) collective-permute-start(f32[32,128]{1,0:T(8,128)S(1)} %get-tuple-element.17), channel_id=1, source_target_pairs={{0,192},{32,224},{64,0},{96,32},{128,64},{160,96},{192,128},{224,1... | collective-permute-start | bytes 49160 | tf_op jit(solution)/shard_map/ppermute | solution.py:175
  26.2 1.1 collective-permute-start.3
  27.3 1.2 collective-permute-start.2
  28.5 1.8 collective-permute-start.1
  30.3 1.1 collective-permute-start
  31.5 0.7 collective-permute-done.2
  32.2 1.4 collective-permute-done.1
  34.2 28.5 %reduce-scatter.2.cloned.1.call-done = bf16[1,288,896]{2,1,0:T(8,128)(2,1)} async-done(((bf16[4,288,896]{2,1,0:T(8,128)(2,1)}), bf16[1,288,896]{2,1,0:T(8,128)(2,1)}) %reduce-scatter.2.cloned.1.call-update) | async-done | bytes 516112 | tf_op jit(solution)/shard_map/reduce_scatter | solution.py:273
  62.7 1.0 copy-done.10
  63.8 0.7 shard_map.121
  64.5 2.4 %collective-permute-start.11 = (bf16[80,896]{1,0:T(8,128)(2,1)S(1)}, bf16[80,896]{1,0:T(8,128)(2,1)S(1)}, u32[]{:S(2)}, u32[]{:S(2)}) collective-permute-start(bf16[80,896]{1,0:T(8,128)(2,1)S(1)} %get-tuple-element.20), channel_id=1, source_target_pairs={{0,8},{4,12},{8,16},{12,20},{16,24},{20,28},{24,0},{28,4},{1,9},{5... | collective-permute-start | bytes 430088 | tf_op jit(solution)/shard_map/ppermute | solution.py:175
  66.9 5.1 %collective-permute-start.12 = (bf16[80,896]{1,0:T(8,128)(2,1)S(1)}, bf16[80,896]{1,0:T(8,128)(2,1)S(1)}, u32[]{:S(2)}, u32[]{:S(2)}) collective-permute-start(bf16[80,896]{1,0:T(8,128)(2,1)S(1)} %get-tuple-element.21), channel_id=1, source_target_pairs={{0,16},{4,20},{8,24},{12,28},{16,0},{20,4},{24,8},{28,12},{1,17},{... | collective-permute-start | bytes 430088 | tf_op jit(solution)/shard_map/ppermute | solution.py:175
  72.0 4.0 %collective-permute-start.13 = (bf16[80,896]{1,0:T(8,128)(2,1)S(1)}, bf16[80,896]{1,0:T(8,128)(2,1)S(1)}, u32[]{:S(2)}, u32[]{:S(2)}) collective-permute-start(bf16[80,896]{1,0:T(8,128)(2,1)S(1)} %get-tuple-element.22), channel_id=1, source_target_pairs={{0,24},{4,28},{8,0},{12,4},{16,8},{20,12},{24,16},{28,20},{1,25},{... | collective-permute-start | bytes 430088 | tf_op jit(solution)/shard_map/ppermute | solution.py:175
  76.1 2.0 copy-done.5
  78.1 8.2 %shard_map.120.refs_4_ = f32[1152,896]{1,0:T(8,128)} custom-call(bf16[8,1152,256]{2,1,0:T(8,128)(2,1)} %all-gather.6.cloned.1.call-done.hidden_ref, bf16[2048,896]{1,0:T(8,128)(2,1)S(1)} %bitcast.62), custom_call_target="tpu_custom_call" | custom-call | flops 4227858432 | bytes 12500000 | tf_op jit(solution)/shard_map/pallas_call | solution.py:116
  86.3 2.0 collective-permute-done.12.refs_2_
  88.4 2.2 copy-done.3
  90.7 0.5 slice.28
  91.9 0.5 slice.37
  93.1 2.0 collective-permute-done.14
  95.2 1.9 fusion
  97.3 2.1 collective-permute-done.15
  99.5 3.1 %collective-permute-start.18 = (bf16[80,896]{1,0:T(8,128)(2,1)S(1)}, bf16[80,896]{1,0:T(8,128)(2,1)S(1)}, u32[]{:S(2)}, u32[]{:S(2)}) collective-permute-start(bf16[80,896]{1,0:T(8,128)(2,1)S(1)} %pad_maximum_fusion.refs_0_), channel_id=1, source_target_pairs={{0,24},{4,28},{8,0},{12,4},{16,8},{20,12},{24,16},{28,20},{1,25},{... | collective-permute-start | bytes 430088 | tf_op jit(solution)/shard_map/ppermute | solution.py:175
  102.6 3.8 %collective-permute-start.17 = (bf16[80,896]{1,0:T(8,128)(2,1)S(1)}, bf16[80,896]{1,0:T(8,128)(2,1)S(1)}, u32[]{:S(2)}, u32[]{:S(2)}) collective-permute-start(bf16[80,896]{1,0:T(8,128)(2,1)S(1)} %pad_maximum_fusion.refs_0_), channel_id=1, source_target_pairs={{0,16},{4,20},{8,24},{12,28},{16,0},{20,4},{24,8},{28,12},{1,17},{... | collective-permute-start | bytes 430088 | tf_op jit(solution)/shard_map/ppermute | solution.py:175
  106.4 0.6 multiply_reduce_fusion
  107.1 0.6 shard_map.122.refs_0_.refs_4_
  107.8 0.8 collective-permute-done.18.refs_3_
  108.6 6.8 %collective-permute-done.17.refs_2_ = bf16[80,896]{1,0:T(8,128)(2,1)S(1)} collective-permute-done((bf16[80,896]{1,0:T(8,128)(2,1)S(1)}, bf16[80,896]{1,0:T(8,128)(2,1)S(1)}, u32[]{:S(2)}, u32[]{:S(2)}) %collective-permute-start.17) | collective-permute-done | bytes 143392 | tf_op jit(solution)/shard_map/ppermute | solution.py:175
  115.4 1.9 collective-permute-done.16.refs_1_
  117.3 1.4 shard_map.129
  118.7 0.8 copy-done.13
  119.6 6.1 %shard_map.123.refs_0_ = bf16[4,1152,256]{2,1,0:T(8,128)(2,1)} custom-call(s32[2]{0:T(128)S(1)} %pad_add_fusion.first_ref, bf16[1152,896]{1,0:T(8,128)(2,1)S(1)} %bitcast.57, bf16[2048,896]{1,0:T(8,128)(2,1)} %bitcast.60, f32[32,2,40]{2,1,0:T(2,128)} %shard_map.122.refs_0_.refs_4_), custom_call_target="tpu_custom_call" | custom-call | flops 2113929216 | bytes 6300000 | tf_op jit(solution)/shard_map/pallas_call | solution.py:94
  125.8 6.9 %all-to-all-start.1 = ((f32[32,2,40]{2,1,0:T(2,128)}), f32[32,2,40]{2,1,0:T(2,128)S(1)}, u32[]{:S(2)}, u32[]{:S(2)}) async-start(f32[32,2,40]{2,1,0:T(2,128)} %shard_map.122.refs_0_.refs_4_), calls=%async_computation.2 | async-start | bytes 65536 | tf_op jit(solution)/shard_map/all_to_all | solution.py:164
  132.8 5.1 %shard_map.124.refs_0_.after_ref = bf16[4,1152,256]{2,1,0:T(8,128)(2,1)S(1)} custom-call(s32[2]{0:T(128)S(1)} %pad_add_fusion.1.first_ref, bf16[1152,896]{1,0:T(8,128)(2,1)S(1)} %bitcast.58, bf16[2048,896]{1,0:T(8,128)(2,1)} %bitcast.61, bf16[4,1152,256]{2,1,0:T(8,128)(2,1)} %shard_map.123.refs_0_), custom_call_target="tpu_custom_call" | custom-call | flops 2113929216 | bytes 6300000 | tf_op jit(solution)/shard_map/pallas_call | solution.py:94
  137.9 1.4 copy-done
  139.3 3.3 %all-to-all-done.1 = f32[32,2,40]{2,1,0:T(2,128)S(1)} async-done(((f32[32,2,40]{2,1,0:T(2,128)}), f32[32,2,40]{2,1,0:T(2,128)S(1)}, u32[]{:S(2)}, u32[]{:S(2)}) %all-to-all-start.1) | async-done | bytes 10272 | tf_op jit(solution)/shard_map/all_to_all | solution.py:164
  142.7 0.6 reshape.72.gate_ref
  143.6 1.7 copy-done.1
  145.3 0.7 broadcast_in_dim.56
  145.9 4.8 %all-to-all-start.2 = ((f32[8,32,128]{2,1,0:T(8,128)}), f32[8,32,128]{2,1,0:T(8,128)S(1)}, u32[]{:S(2)}, u32[]{:S(2)}) async-start(f32[8,32,128]{2,1,0:T(8,128)} %broadcast_in_dim.56), calls=%async_computation.3 | async-start | bytes 262144 | tf_op jit(solution)/shard_map/all_to_all | solution.py:164
  150.8 10.5 %shard_map.125.refs_0_ = bf16[1,2048,896]{2,1,0:T(8,128)(2,1)} custom-call(bf16[8,1152,256]{2,1,0:T(8,128)(2,1)} %all-gather.6.cloned.1.call-done.hidden_ref, bf16[1152,896]{1,0:T(8,128)(2,1)S(1)} %bitcast.59, f32[1152,1]{1,0:T(8,128)S(1)} %reshape.72.gate_ref), custom_call_target="tpu_custom_call" | custom-call | flops 4227858432 | bytes 12500000 | tf_op jit(solution)/shard_map/pallas_call | solution.py:145
  161.2 2.2 copy-done.6
  163.5 0.5 copy-done.2
  164.0 1.5 copy-done.9
  165.5 1.0 copy-done.14
  166.5 7.2 %shard_map.130.refs_0_ = bf16[288,896]{1,0:T(8,128)(2,1)} custom-call(bf16[8,288,288]{2,1,0:T(8,128)(2,1)S(1)} %bitcast.64, bf16[288,896]{1,0:T(8,128)(2,1)S(1)} %copy-done.14, bf16[4,1152,256]{2,1,0:T(8,128)(2,1)S(1)} %copy-done.2), custom_call_target="tpu_custom_call" | custom-call | flops 3000000000 | bytes 3600000 | tf_op jit(solution)/shard_map/pallas_call | solution.py:315
  173.8 2.2 add_convert_fusion
  176.1 1.5 collective-permute-start.8
  177.7 0.6 collective-permute-start.10
  178.2 2.1 collective-permute-start.9
  180.5 0.7 reshape.67
  181.3 6.5 %all-to-all-start.3 = ((f32[32,1,896]{2,1,0:T(1,128)}), f32[32,1,896]{2,1,0:T(1,128)S(1)}, u32[]{:S(2)}, u32[]{:S(2)}) async-start(f32[32,1,896]{2,1,0:T(1,128)} %reshape.67), calls=%async_computation.4 | async-start | bytes 229376 | tf_op jit(solution)/shard_map/all_to_all | solution.py:164
  187.8 10.3 %all-to-all-done.3.values_ref = f32[32,1,896]{2,1,0:T(1,128)S(1)} async-done(((f32[32,1,896]{2,1,0:T(1,128)}), f32[32,1,896]{2,1,0:T(1,128)S(1)}, u32[]{:S(2)}, u32[]{:S(2)}) %all-to-all-start.3) | async-done | bytes 114720 | tf_op jit(solution)/shard_map/all_to_all | solution.py:164
  198.2 0.7 broadcast_in_dim.58
  198.9 3.9 %all-to-all-start.4 = ((f32[32,1,896]{2,1,0:T(1,128)}), f32[32,1,896]{2,1,0:T(1,128)S(1)}, u32[]{:S(2)}, u32[]{:S(2)}) async-start(f32[32,1,896]{2,1,0:T(1,128)} %broadcast_in_dim.58), calls=%async_computation.5 | async-start | bytes 229376 | tf_op jit(solution)/shard_map/all_to_all | solution.py:164
  202.8 1.3 convolution_convert_fusion
  204.0 9.1 %all-to-all-done.4 = f32[32,1,896]{2,1,0:T(1,128)S(1)} async-done(((f32[32,1,896]{2,1,0:T(1,128)}), f32[32,1,896]{2,1,0:T(1,128)S(1)}, u32[]{:S(2)}, u32[]{:S(2)}) %all-to-all-start.4) | async-done | bytes 114720 | tf_op jit(solution)/shard_map/all_to_all | solution.py:164
  213.2 0.7 copy.32
  213.9 2.4 %fusion.4 = bf16[1152,256]{1,0:T(8,128)(2,1)} fusion(bf16[1152,256]{1,0:T(8,128)(2,1)S(1)} %collective-permute-done.10, bf16[1152,256]{1,0:T(8,128)(2,1)} %collective-permute-done.9, bf16[1152,256]{1,0:T(8,128)(2,1)S(1)} %collective-permute-done.8, bf16[4,1152,256]{2,1,0:T(8,128)(2,1)} %copy-done.15, f32[1152]{0:T(1024)S(1)} %mul.61), kind=kLoop, calls=%fused_computation.9 | loop fusion | flops 2654208 | bytes 2953728 | tf_op jit(solution)/shard_map/convert_element_type | solution.py:429
  216.2 3.0 %copy.34 = bf16[4,288,896]{2,1,0:T(8,128)(2,1)} copy(bf16[4,288,896]{2,1,0:T(8,128)(2,1)} %bitcast.68) | data formatting | bytes 4128768
  (79 shorter events, 3.2 us)
Async XLA Ops:
  8.0 1.4 copy-start.7
  8.0 1.4 copy-start.8
  8.0 1.4 copy-start.12
  8.0 1.4 copy-start.11
  8.0 54.7 %reduce-scatter.2.cloned.1.call-start = ((), (), s32[]{:S(2)}) async-start(), calls=%async_computation.7 | async-start | bytes 2580480 | tf_op jit(solution)/shard_map/reduce_scatter | solution.py:273
  8.8 67.3 %all-gather.6.cloned.1.call-start = ((), (), s32[]{:S(2)}) async-start(), calls=%async_computation.6 | async-start | bytes 5308416 | tf_op jit(solution)/shard_map/all_gather | solution.py:392
  11.7 83.5 %all-to-all-start = ((bf16[32,40,896]{2,1,0:T(8,128)(2,1)}), bf16[32,40,896]{2,1,0:T(8,128)(2,1)}, u32[]{:S(2)}, u32[]{:S(2)}) async-start(bf16[32,40,896]{2,1,0:T(8,128)(2,1)} %get-tuple-element.18), calls=%async_computation | async-start | bytes 4587520 | tf_op jit(solution)/shard_map/all_to_all | solution.py:164
  23.3 140.2 %all-gather.8.cloned.1.call-start = ((), (), s32[]{:S(2)}) async-start(), calls=%async_computation.8 | async-start | bytes 1990656 | tf_op jit(solution)/shard_map/all_gather | solution.py:423
  23.4 5.1 %collective-permute-start.6 = (f32[32,128]{1,0:T(8,128)S(1)}, f32[32,128]{1,0:T(8,128)S(1)}, u32[]{:S(2)}, u32[]{:S(2)}) collective-permute-start(f32[32,128]{1,0:T(8,128)S(1)} %get-tuple-element.17), channel_id=1, source_target_pairs={{0,224},{32,0},{64,32},{96,64},{128,96},{160,128},{192,160},{224,1... | collective-permute-start | bytes 49160 | tf_op jit(solution)/shard_map/ppermute | solution.py:175
  23.4 6.9 %collective-permute-start.5 = (f32[32,128]{1,0:T(8,128)S(1)}, f32[32,128]{1,0:T(8,128)S(1)}, u32[]{:S(2)}, u32[]{:S(2)}) collective-permute-start(f32[32,128]{1,0:T(8,128)S(1)} %get-tuple-element.17), channel_id=1, source_target_pairs={{0,192},{32,224},{64,0},{96,32},{128,64},{160,96},{192,128},{224,1... | collective-permute-start | bytes 49160 | tf_op jit(solution)/shard_map/ppermute | solution.py:175
  25.8 5.5 %collective-permute-start.4 = (f32[32,128]{1,0:T(8,128)S(1)}, f32[32,128]{1,0:T(8,128)S(1)}, u32[]{:S(2)}, u32[]{:S(2)}) collective-permute-start(f32[32,128]{1,0:T(8,128)S(1)} %get-tuple-element.17), channel_id=1, source_target_pairs={{0,160},{32,192},{64,224},{96,0},{128,32},{160,64},{192,96},{224,1... | collective-permute-start | bytes 49160 | tf_op jit(solution)/shard_map/ppermute | solution.py:175
  26.2 5.3 %collective-permute-start.3 = (f32[32,128]{1,0:T(8,128)S(1)}, f32[32,128]{1,0:T(8,128)S(1)}, u32[]{:S(2)}, u32[]{:S(2)}) collective-permute-start(f32[32,128]{1,0:T(8,128)S(1)} %get-tuple-element.17), channel_id=1, source_target_pairs={{0,128},{32,160},{64,192},{96,224},{128,0},{160,32},{192,64},{224,... | collective-permute-start | bytes 49160 | tf_op jit(solution)/shard_map/ppermute | solution.py:175
  27.3 4.9 %collective-permute-start.2 = (f32[32,128]{1,0:T(8,128)S(1)}, f32[32,128]{1,0:T(8,128)S(1)}, u32[]{:S(2)}, u32[]{:S(2)}) collective-permute-start(f32[32,128]{1,0:T(8,128)S(1)} %get-tuple-element.17), channel_id=1, source_target_pairs={{0,96},{32,128},{64,160},{96,192},{128,224},{160,0},{192,32},{224,... | collective-permute-start | bytes 49160 | tf_op jit(solution)/shard_map/ppermute | solution.py:175
  28.5 5.1 %collective-permute-start.1 = (f32[32,128]{1,0:T(8,128)S(1)}, f32[32,128]{1,0:T(8,128)S(1)}, u32[]{:S(2)}, u32[]{:S(2)}) collective-permute-start(f32[32,128]{1,0:T(8,128)S(1)} %get-tuple-element.17), channel_id=1, source_target_pairs={{0,64},{32,96},{64,128},{96,160},{128,192},{160,224},{192,0},{224,... | collective-permute-start | bytes 49160 | tf_op jit(solution)/shard_map/ppermute | solution.py:175
  30.3 3.6 %collective-permute-start = (f32[32,128]{1,0:T(8,128)S(1)}, f32[32,128]{1,0:T(8,128)S(1)}, u32[]{:S(2)}, u32[]{:S(2)}) collective-permute-start(f32[32,128]{1,0:T(8,128)S(1)} %get-tuple-element.17), channel_id=1, source_target_pairs={{0,32},{32,64},{64,96},{96,128},{128,160},{160,192},{192,224},{224... | collective-permute-start | bytes 49160 | tf_op jit(solution)/shard_map/ppermute | solution.py:175
  62.7 1.0 copy-start.10
  64.5 21.8 %collective-permute-start.11 = (bf16[80,896]{1,0:T(8,128)(2,1)S(1)}, bf16[80,896]{1,0:T(8,128)(2,1)S(1)}, u32[]{:S(2)}, u32[]{:S(2)}) collective-permute-start(bf16[80,896]{1,0:T(8,128)(2,1)S(1)} %get-tuple-element.20), channel_id=1, source_target_pairs={{0,8},{4,12},{8,16},{12,20},{16,24},{20,28},{24,0},{28,4},{1,9},{5... | collective-permute-start | bytes 430088 | tf_op jit(solution)/shard_map/ppermute | solution.py:175
  66.9 21.5 %collective-permute-start.12 = (bf16[80,896]{1,0:T(8,128)(2,1)S(1)}, bf16[80,896]{1,0:T(8,128)(2,1)S(1)}, u32[]{:S(2)}, u32[]{:S(2)}) collective-permute-start(bf16[80,896]{1,0:T(8,128)(2,1)S(1)} %get-tuple-element.21), channel_id=1, source_target_pairs={{0,16},{4,20},{8,24},{12,28},{16,0},{20,4},{24,8},{28,12},{1,17},{... | collective-permute-start | bytes 430088 | tf_op jit(solution)/shard_map/ppermute | solution.py:175
  72.0 16.3 %collective-permute-start.13 = (bf16[80,896]{1,0:T(8,128)(2,1)S(1)}, bf16[80,896]{1,0:T(8,128)(2,1)S(1)}, u32[]{:S(2)}, u32[]{:S(2)}) collective-permute-start(bf16[80,896]{1,0:T(8,128)(2,1)S(1)} %get-tuple-element.22), channel_id=1, source_target_pairs={{0,24},{4,28},{8,0},{12,4},{16,8},{20,12},{24,16},{28,20},{1,25},{... | collective-permute-start | bytes 430088 | tf_op jit(solution)/shard_map/ppermute | solution.py:175
  76.1 2.0 copy-start.5
  88.4 2.2 copy-start.3
  90.6 4.4 %collective-permute-start.14 = (bf16[40,896]{1,0:T(8,128)(2,1)S(1)}, bf16[40,896]{1,0:T(8,128)(2,1)S(1)}, u32[]{:S(2)}, u32[]{:S(2)}) collective-permute-start(bf16[40,896]{1,0:T(8,128)(2,1)S(1)} %get-tuple-element.24), channel_id=1, source_target_pairs={{0,4},{4,0},{8,12},{12,8},{16,20},{20,16},{24,28},{28,24},{1,5},{5... | collective-permute-start | bytes 215048 | tf_op jit(solution)/shard_map/ppermute | solution.py:180
  95.1 4.4 %collective-permute-start.15 = (bf16[40,896]{1,0:T(8,128)(2,1)S(1)}, bf16[40,896]{1,0:T(8,128)(2,1)S(1)}, u32[]{:S(2)}, u32[]{:S(2)}) collective-permute-start(bf16[40,896]{1,0:T(8,128)(2,1)S(1)} %add_convert_fusion.1), channel_id=1, source_target_pairs={{0,4},{4,0},{8,12},{12,8},{16,20},{20,16},{24,28},{28,24},{1,5},{5... | collective-permute-start | bytes 215048 | tf_op jit(solution)/shard_map/ppermute | solution.py:180
  97.1 9.3 %copy-start.4 = (f32[1152,896]{1,0:T(8,128)S(1)}, f32[1152,896]{1,0:T(8,128)}, u32[]{:S(2)}) copy-start(f32[1152,896]{1,0:T(8,128)} %shard_map.120.refs_4_) | copy-start | bytes 12386308
  99.5 9.1 %collective-permute-start.18 = (bf16[80,896]{1,0:T(8,128)(2,1)S(1)}, bf16[80,896]{1,0:T(8,128)(2,1)S(1)}, u32[]{:S(2)}, u32[]{:S(2)}) collective-permute-start(bf16[80,896]{1,0:T(8,128)(2,1)S(1)} %pad_maximum_fusion.refs_0_), channel_id=1, source_target_pairs={{0,24},{4,28},{8,0},{12,4},{16,8},{20,12},{24,16},{28,20},{1,25},{... | collective-permute-start | bytes 430088 | tf_op jit(solution)/shard_map/ppermute | solution.py:175
  102.6 12.8 %collective-permute-start.17 = (bf16[80,896]{1,0:T(8,128)(2,1)S(1)}, bf16[80,896]{1,0:T(8,128)(2,1)S(1)}, u32[]{:S(2)}, u32[]{:S(2)}) collective-permute-start(bf16[80,896]{1,0:T(8,128)(2,1)S(1)} %pad_maximum_fusion.refs_0_), channel_id=1, source_target_pairs={{0,16},{4,20},{8,24},{12,28},{16,0},{20,4},{24,8},{28,12},{1,17},{... | collective-permute-start | bytes 430088 | tf_op jit(solution)/shard_map/ppermute | solution.py:175
  106.4 10.9 %collective-permute-start.16 = (bf16[80,896]{1,0:T(8,128)(2,1)S(1)}, bf16[80,896]{1,0:T(8,128)(2,1)S(1)}, u32[]{:S(2)}, u32[]{:S(2)}) collective-permute-start(bf16[80,896]{1,0:T(8,128)(2,1)S(1)} %pad_maximum_fusion.refs_0_), channel_id=1, source_target_pairs={{0,8},{4,12},{8,16},{12,20},{16,24},{20,28},{24,0},{28,4},{1,9},{5... | collective-permute-start | bytes 430088 | tf_op jit(solution)/shard_map/ppermute | solution.py:175
  118.7 0.8 copy-start.13
  125.8 48.0 %collective-permute-start.7 = (bf16[4,1152,256]{2,1,0:T(8,128)(2,1)}, bf16[4,1152,256]{2,1,0:T(8,128)(2,1)}, u32[]{:S(2)}, u32[]{:S(2)}) collective-permute-start(bf16[4,1152,256]{2,1,0:T(8,128)(2,1)} %shard_map.123.refs_0_), channel_id=1, source_target_pairs={{0,32},{32,0},{1,33},{33,1},{2,34},{34,2},{3,35},{35,3},{4,36},{36... | collective-permute-start | bytes 7077896 | tf_op jit(solution)/shard_map/ppermute | solution.py:420
  125.8 16.7 %all-to-all-start.1 = ((f32[32,2,40]{2,1,0:T(2,128)}), f32[32,2,40]{2,1,0:T(2,128)S(1)}, u32[]{:S(2)}, u32[]{:S(2)}) async-start(f32[32,2,40]{2,1,0:T(2,128)} %shard_map.122.refs_0_.refs_4_), calls=%async_computation.2 | async-start | bytes 65536 | tf_op jit(solution)/shard_map/all_to_all | solution.py:164
  137.9 1.4 copy-start
  143.6 1.7 copy-start.1
  145.9 15.3 %all-to-all-start.2 = ((f32[8,32,128]{2,1,0:T(8,128)}), f32[8,32,128]{2,1,0:T(8,128)S(1)}, u32[]{:S(2)}, u32[]{:S(2)}) async-start(f32[8,32,128]{2,1,0:T(8,128)} %broadcast_in_dim.56), calls=%async_computation.3 | async-start | bytes 262144 | tf_op jit(solution)/shard_map/all_to_all | solution.py:164
  150.7 65.5 %all-gather.10.cloned.1.call-start = ((), (), s32[]{:S(2)}) async-start(), calls=%async_computation.9 | async-start | bytes 2580480 | tf_op jit(solution)/shard_map/all_gather | solution.py:438
  161.2 2.8 %copy-start.2 = (bf16[4,1152,256]{2,1,0:T(8,128)(2,1)S(1)}, bf16[4,1152,256]{2,1,0:T(8,128)(2,1)}, u32[]{:S(2)}) copy-start(bf16[4,1152,256]{2,1,0:T(8,128)(2,1)} %copy-done) | copy-start | bytes 7077892
  161.2 2.2 copy-start.6
  164.0 1.5 copy-start.9
  165.5 1.0 copy-start.14
  166.5 7.2 %copy-start.16 = (f32[128,32]{0,1:T(8,128)S(1)}, f32[128,32]{0,1:T(8,128)}, u32[]{:S(2)}) copy-start(f32[128,32]{0,1:T(8,128)} %param.12) | copy-start | bytes 49156
  176.0 4.5 %copy-start.15 = (bf16[4,1152,256]{2,1,0:T(8,128)(2,1)}, bf16[4,1152,256]{2,1,0:T(8,128)(2,1)S(1)}, u32[]{:S(2)}) copy-start(bf16[4,1152,256]{2,1,0:T(8,128)(2,1)S(1)} %add_convert_fusion) | copy-start | bytes 7077892
  176.1 37.7 %collective-permute-start.8 = (bf16[1152,256]{1,0:T(8,128)(2,1)S(1)}, bf16[1152,256]{1,0:T(8,128)(2,1)S(1)}, u32[]{:S(2)}, u32[]{:S(2)}) collective-permute-start(bf16[1152,256]{1,0:T(8,128)(2,1)S(1)} %get-tuple-element.30), channel_id=1, source_target_pairs={{0,64},{64,128},{128,192},{192,0},{1,65},{65,129},{129,193},{193,1... | collective-permute-start | bytes 1769480 | tf_op jit(solution)/shard_map/ppermute | solution.py:175
  177.7 36.2 %collective-permute-start.10 = (bf16[1152,256]{1,0:T(8,128)(2,1)S(1)}, bf16[1152,256]{1,0:T(8,128)(2,1)S(1)}, u32[]{:S(2)}, u32[]{:S(2)}) collective-permute-start(bf16[1152,256]{1,0:T(8,128)(2,1)S(1)} %get-tuple-element.31), channel_id=1, source_target_pairs={{0,192},{64,0},{128,64},{192,128},{1,193},{65,1},{129,65},{193,129... | collective-permute-start | bytes 1769480 | tf_op jit(solution)/shard_map/ppermute | solution.py:175
  178.2 35.6 %collective-permute-start.9 = (bf16[1152,256]{1,0:T(8,128)(2,1)S(1)}, bf16[1152,256]{1,0:T(8,128)(2,1)}, u32[]{:S(2)}, u32[]{:S(2)}) collective-permute-start(bf16[1152,256]{1,0:T(8,128)(2,1)S(1)} %get-tuple-element.32), channel_id=1, source_target_pairs={{0,128},{64,192},{128,0},{192,64},{1,129},{65,193},{129,1},{193,65... | collective-permute-start | bytes 1769480 | tf_op jit(solution)/shard_map/ppermute | solution.py:175
  181.3 16.9 %all-to-all-start.3 = ((f32[32,1,896]{2,1,0:T(1,128)}), f32[32,1,896]{2,1,0:T(1,128)S(1)}, u32[]{:S(2)}, u32[]{:S(2)}) async-start(f32[32,1,896]{2,1,0:T(1,128)} %reshape.67), calls=%async_computation.4 | async-start | bytes 229376 | tf_op jit(solution)/shard_map/all_to_all | solution.py:164
  198.9 14.3 %all-to-all-start.4 = ((f32[32,1,896]{2,1,0:T(1,128)}), f32[32,1,896]{2,1,0:T(1,128)S(1)}, u32[]{:S(2)}, u32[]{:S(2)}) async-start(f32[32,1,896]{2,1,0:T(1,128)} %broadcast_in_dim.58), calls=%async_computation.5 | async-start | bytes 229376 | tf_op jit(solution)/shard_map/all_to_all | solution.py:164
Sparse Core Ops, SparseCore 0:
  11.5 51.2 reduce-scatter.1
  173.8 32.3 all-gather.9
Sparse Core Ops, SparseCore 1:
  11.2 39.2 all-gather.5
  119.6 24.1 all-gather.7
